TPU v7x, 512 devices: a whole 4x4x16 slice. The times are simulated.
512 devices in a mesh: dp: 64 (over x, z), mp: 8 (over y, core).
Axes of the slice: x: 4, y: 4, z: 16, core: 2. Of those that a mesh axis runs over, the one named last changes fastest.
Arguments:
- query: bfloat16 [1024, 32, 8192], P('dp', None, 'mp'), may hold values from -30 to 30
- comp_key: bfloat16 [1024, 32, 1024], P('dp', None, 'mp'), may hold values from -6 to 6
- comp_value: bfloat16 [1024, 32, 1024], P('dp', None, 'mp'), may hold values from -6 to 6
- prefix_key: bfloat16 [64, 1024, 1024], P('dp', 'mp'), may hold values from -6 to 6
- prefix_value: bfloat16 [64, 1024, 1024], P('dp', 'mp'), may hold values from -6 to 6
- grad_out: bfloat16 [1024, 32, 8192], P('dp', None, 'mp'), may hold values from -6 to 6
- owner: int32 [64], replicated, may hold values from 0 to 63, as said below
- group: int32 [1024], P('dp'), may hold values from 0 to 63, as said below
- lengths: int32 [1024], P('dp'), may hold values from 1 to 32, as said below
Outputs:
- grad_query: bfloat16 [1024, 32, 8192], P('dp', None, 'mp')
- grad_comp_key: bfloat16 [1024, 32, 1024], P('dp', None, 'mp')
- grad_comp_value: bfloat16 [1024, 32, 1024], P('dp', None, 'mp')
- grad_prefix_key: bfloat16 [64, 1024, 1024], P('dp', 'mp')
- grad_prefix_value: bfloat16 [64, 1024, 1024], P('dp', 'mp')
Inputs may be any that keep to these rules, and one draw needn't show every extreme that they name: `owner`: a permutation: every dp index owns exactly one prompt. `group`: every prompt has exactly 16 completions; the owner of the prompt of a completion held by dp index d is one of d - 2, d - 1, d, d + 1, d + 2 taken cyclically, and every dp index holds at least one completion of a prompt owned by each of d - 2, d - 1, d + 1, d + 2. `lengths`: every dp index holds at least one completion of 32 tokens.
All inputs are finite; a program needn't handle non-finite values.
Results may differ from a plain program's by a relative error of at most 0.012.
The roundings to bfloat16 on the way count: a program that leaves them out, or rounds other values in their place, can miss the bound.
Values may be sent and summed in bfloat16 or wider, within the bound.
No kernel may reach another device: no remote copies, remote signals or barrier semaphores. Data moves between devices by JAX's collectives and lax.ppermute only.
A program may use at most 64 MiB of HBM per device.

v0:
```python
import jax
import jax.numpy as jnp
from jax import lax
from jax.sharding import PartitionSpec as P

HD = 128


def shifted(value, axis, steps):
    count = lax.axis_size(axis)
    pairs = [(source, (source + steps) % count) for source in range(count)]
    return lax.ppermute(value, axis, pairs)


def slot_grads(query, comp_key, comp_value, pre_key, pre_value, grad_out, length):
    row_count = query.shape[0]
    prefix_rows = pre_key.shape[0]
    kv_heads = comp_key.shape[1] // HD
    repeat = query.shape[1] // comp_key.shape[1]
    scaling = HD ** (-0.5)
    queries = query.reshape(row_count, kv_heads, repeat, HD)
    all_keys = jnp.concatenate([pre_key, comp_key], 0).reshape(
        prefix_rows + row_count, kv_heads, HD
    )
    all_values = jnp.concatenate([pre_value, comp_value], 0).reshape(
        prefix_rows + row_count, kv_heads, HD
    )
    scores = (
        jnp.einsum("igrd,jgd->grij", queries, all_keys, preferred_element_type=jnp.float32)
        * scaling
    )
    query_pos = jnp.arange(row_count)[:, None]
    key_pos = jnp.arange(prefix_rows + row_count)[None, :]
    offset = key_pos - prefix_rows
    visible = (key_pos < prefix_rows) | (offset <= query_pos) & (offset < length)
    scores = jnp.where(visible, scores, -jnp.inf)
    row_max = jnp.max(scores, axis=-1, keepdims=True)
    exponent = jnp.exp(scores - row_max)
    probability = exponent / jnp.sum(exponent, axis=-1, keepdims=True)
    weights = probability.astype(jnp.bfloat16)
    attended = jnp.einsum("grij,jgd->igrd", weights, all_values, preferred_element_type=jnp.float32)
    live_rows = jnp.arange(row_count) < length
    upstream = jnp.where(live_rows[:, None], grad_out, jnp.zeros_like(grad_out))
    upstream = upstream.reshape(row_count, kv_heads, repeat, HD)
    grad_prob = jnp.einsum(
        "igrd,jgd->grij", upstream, all_values, preferred_element_type=jnp.float32
    )
    row_delta = jnp.transpose(jnp.sum(upstream.astype(jnp.float32) * attended, axis=-1), (1, 2, 0))
    grad_score = (probability * (grad_prob - row_delta[..., None])).astype(jnp.bfloat16)
    grad_query = (
        jnp.einsum("grij,jgd->igrd", grad_score, all_keys, preferred_element_type=jnp.float32)
        * scaling
    )
    grad_key = (
        jnp.einsum("grij,igrd->jgd", grad_score, queries, preferred_element_type=jnp.float32)
        * scaling
    )
    grad_value = jnp.einsum("grij,igrd->jgd", weights, upstream, preferred_element_type=jnp.float32)
    kv_width = kv_heads * HD
    grad_key = grad_key.reshape(prefix_rows + row_count, kv_width)
    grad_value = grad_value.reshape(prefix_rows + row_count, kv_width)
    return (
        grad_query.reshape(row_count, -1),
        grad_key[:prefix_rows],
        grad_value[:prefix_rows],
        grad_key[prefix_rows:],
        grad_value[prefix_rows:],
    )


def fetch_nearby(prefix_pair):
    lower_two = shifted(prefix_pair, "dp", 2)
    lower_one = shifted(prefix_pair, "dp", 1)
    upper_one = shifted(prefix_pair, "dp", -1)
    upper_two = shifted(prefix_pair, "dp", -2)
    return jnp.stack([lower_two, lower_one, prefix_pair, upper_one, upper_two])


def return_terms(totals):
    gathered = totals[2]
    gathered = gathered + shifted(totals[0], "dp", -2)
    gathered = gathered + shifted(totals[1], "dp", -1)
    gathered = gathered + shifted(totals[3], "dp", 1)
    gathered = gathered + shifted(totals[4], "dp", 2)
    return gathered


def per_device(
    query, comp_key, comp_value, prefix_key, prefix_value, grad_out, owner, group, lengths
):
    axis_count = lax.axis_size("dp")
    position = lax.axis_index("dp")
    slot_count = query.shape[0]
    prompt_ids = jnp.arange(owner.shape[0], dtype=jnp.int32)
    holder_of = jnp.sum(jnp.where(group[:, None] == prompt_ids[None, :], owner[None, :], 0), axis=1)
    which_near = (holder_of - position + 2 + axis_count) % axis_count
    prefix_pair = jnp.stack([prefix_key[0], prefix_value[0]])
    nearby = lax.all_to_all(
        fetch_nearby(prefix_pair), "mp", split_axis=3, concat_axis=2, tiled=True
    )
    block_count = slot_count // 2

    def blocked(array):
        return array.reshape((block_count, 2) + array.shape[1:])

    def advance(totals, inputs):
        block_query, block_key, block_value, block_grad, block_near, block_length = inputs
        chosen = jnp.take(nearby, block_near, axis=0)
        grad_q, key_pre, value_pre, key_comp, value_comp = jax.vmap(slot_grads)(
            block_query,
            block_key,
            block_value,
            chosen[:, 0],
            chosen[:, 1],
            block_grad,
            block_length,
        )
        terms = jnp.stack([key_pre, value_pre], axis=1)
        for member in range(2):
            target = block_near[member]
            current = lax.dynamic_index_in_dim(totals, target, 0, keepdims=False)
            totals = lax.dynamic_update_index_in_dim(totals, current + terms[member], target, 0)
        return (
            totals,
            (
                grad_q.astype(jnp.bfloat16),
                key_comp.astype(jnp.bfloat16),
                value_comp.astype(jnp.bfloat16),
            ),
        )

    start_totals = jnp.zeros(nearby.shape, jnp.float32)
    totals, (grad_q, key_comp, value_comp) = lax.scan(
        advance,
        start_totals,
        (
            blocked(query),
            blocked(comp_key),
            blocked(comp_value),
            blocked(grad_out),
            blocked(which_near),
            blocked(lengths),
        ),
    )
    gathered = return_terms(totals)
    token_split = lax.all_to_all(
        gathered.astype(jnp.bfloat16), "mp", split_axis=1, concat_axis=2, tiled=True
    )
    return (
        grad_q.reshape(query.shape),
        key_comp.reshape(comp_key.shape),
        value_comp.reshape(comp_value.shape),
        token_split[0][None],
        token_split[1][None],
    )


def solution(mesh):
    return jax.shard_map(
        per_device,
        mesh=mesh,
        in_specs=(
            P("dp", None, "mp"),
            P("dp", None, "mp"),
            P("dp", None, "mp"),
            P("dp", "mp", None),
            P("dp", "mp", None),
            P("dp", None, "mp"),
            P(),
            P("dp"),
            P("dp"),
        ),
        out_specs=(
            P("dp", None, "mp"),
            P("dp", None, "mp"),
            P("dp", None, "mp"),
            P("dp", "mp", None),
            P("dp", "mp", None),
        ),
        check_vma=False,
    )
```

profile of v0, /device:TPU:1, one launch (start us, length us, event | category | flops | bytes accessed | tf_op | source)
XLA Modules:
  0.0 380.2 jit_solution(14107992214301561335)
XLA Ops:
  0.6 1.3 copy.61
  1.9 1.3 copy.62
  3.2 1.2 pad_maximum_fusion.1
  4.4 5.7 %collective-permute-start = (bf16[2,128,1024]{1,0,2:T(2,128)(2,1)S(1)}, bf16[2,128,1024]{1,0,2:T(2,128)(2,1)S(1)}, u32[]{:S(2)}, u32[]{:S(2)}) collective-permute-start(bf16[2,128,1024]{1,0,2:T(2,128)(2,1)S(1)} %pad_maximum_fusion.1), channel_id=1, source_target_pairs={{0,16},{8,24},{16,32},{24,40},{32,48},{40,56},{48,64},{56,72},{64,... | collective-permute-start | bytes 1572872 | tf_op jit(solution)/shard_map/ppermute | solution.py:12
  10.1 3.5 collective-permute-start.1
  13.7 8.7 %collective-permute-start.2 = (bf16[2,128,1024]{1,0,2:T(2,128)(2,1)S(1)}, bf16[2,128,1024]{1,0,2:T(2,128)(2,1)S(1)}, u32[]{:S(2)}, u32[]{:S(2)}) collective-permute-start(bf16[2,128,1024]{1,0,2:T(2,128)(2,1)S(1)} %pad_maximum_fusion.1), channel_id=1, source_target_pairs={{0,504},{8,0},{16,8},{24,16},{32,24},{40,32},{48,40},{56,48},{64,5... | collective-permute-start | bytes 1572872 | tf_op jit(solution)/shard_map/ppermute | solution.py:12
  22.4 4.3 %collective-permute-start.3 = (bf16[2,128,1024]{1,0,2:T(2,128)(2,1)S(1)}, bf16[2,128,1024]{1,0,2:T(2,128)(2,1)S(1)}, u32[]{:S(2)}, u32[]{:S(2)}) collective-permute-start(bf16[2,128,1024]{1,0,2:T(2,128)(2,1)S(1)} %pad_maximum_fusion.1), channel_id=1, source_target_pairs={{0,496},{8,504},{16,0},{24,8},{32,16},{40,24},{48,32},{56,40},{64,... | collective-permute-start | bytes 1572872 | tf_op jit(solution)/shard_map/ppermute | solution.py:12
  26.7 7.1 %collective-permute-done = bf16[2,128,1024]{1,0,2:T(2,128)(2,1)S(1)} collective-permute-done((bf16[2,128,1024]{1,0,2:T(2,128)(2,1)S(1)}, bf16[2,128,1024]{1,0,2:T(2,128)(2,1)S(1)}, u32[]{:S(2)}, u32[]{:S(2)}) %collective-permute-start) | collective-permute-done | bytes 524320 | tf_op jit(solution)/shard_map/ppermute | solution.py:12
  33.8 1.2 bitcast_dynamic-update-slice_fusion.3
  35.0 18.0 %collective-permute-done.1 = bf16[2,128,1024]{1,0,2:T(2,128)(2,1)S(1)} collective-permute-done((bf16[2,128,1024]{1,0,2:T(2,128)(2,1)S(1)}, bf16[2,128,1024]{1,0,2:T(2,128)(2,1)S(1)}, u32[]{:S(2)}, u32[]{:S(2)}) %collective-permute-start.1) | collective-permute-done | bytes 524320 | tf_op jit(solution)/shard_map/ppermute | solution.py:12
  52.9 1.2 bitcast_dynamic-update-slice_fusion.2
  54.1 2.0 bitcast_dynamic-update-slice_fusion.1
  56.2 1.2 bitcast_dynamic-update-slice_fusion
  57.4 1.2 bitcast_dynamic-update-slice_fusion.4
  58.6 5.5 %all-to-all-start = ((bf16[5,2,128,1024]{2,1,0,3:T(2,128)(2,1)}), bf16[5,2,128,1024]{2,1,0,3:T(2,128)(2,1)S(1)}, u32[]{:S(2)}, u32[]{:S(2)}) async-start(bf16[5,2,128,1024]{2,1,0,3:T(2,128)(2,1)} %bitcast_dynamic-update-slice_fusion.4), calls=%async_computation | async-start | bytes 5242880 | tf_op jit(solution)/shard_map/all_to_all | solution.py:98
  64.5 31.6 %all-to-all-done = bf16[5,2,128,1024]{2,1,0,3:T(2,128)(2,1)S(1)} async-done(((bf16[5,2,128,1024]{2,1,0,3:T(2,128)(2,1)}), bf16[5,2,128,1024]{2,1,0,3:T(2,128)(2,1)S(1)}, u32[]{:S(2)}, u32[]{:S(2)}) %all-to-all-start) | async-done | bytes 2621472 | tf_op jit(solution)/shard_map/all_to_all | solution.py:98
  96.1 5.7 %copy.67 = bf16[5,2,8,128,128]{4,3,2,1,0:T(8,128)(2,1)} copy(bf16[5,2,8,128,128]{3,1,0,4,2:T(2,128)(2,1)S(1)} %bitcast.262) | data formatting | bytes 5242880 | tf_op jit(solution)/shard_map/all_to_all | solution.py:98
  101.8 2.8 broadcast_in_dim.98
  104.5 173.7 %while.18 = (s32[]{:T(128)}, f32[5,2,1024,128]{3,2,0,1:T(8,128)}, bf16[8,2,32,1024]{3,2,1,0:T(8,128)(2,1)}, bf16[8,2,32,128]{3,2,1,0:T(8,128)(2,1)}, bf16[8,2,32...) while((s32[]{:T(128)}, f32[5,2,1024,128]{3,2,0,1:T(8,128)}, ...), condition=%wide.region_5.6_spmd, body=%wide.region_1.5_spmd.sunk | while | flops 844300992 | bytes 41598052 | solution.py:133
  110.7 0.9 constant_dynamic-slice_fusion.7
  111.8 0.9 constant_dynamic-slice_fusion.8
  112.7 2.5 gather_fusion
  121.5 2.4 fusion.78
  123.9 2.4 fusion.79
  132.4 0.9 constant_dynamic-slice_fusion.7
  133.5 0.9 constant_dynamic-slice_fusion.8
  134.5 2.5 gather_fusion
  143.3 2.4 fusion.78
  145.6 2.3 fusion.79
  154.1 0.9 constant_dynamic-slice_fusion.7
  155.2 0.9 constant_dynamic-slice_fusion.8
  156.2 2.5 gather_fusion
  164.9 2.4 fusion.78
  167.3 2.3 fusion.79
  175.8 0.9 constant_dynamic-slice_fusion.7
  177.9 2.5 gather_fusion
  186.6 2.3 fusion.78
  189.0 2.4 fusion.79
  199.5 2.5 gather_fusion
  208.3 2.4 fusion.78
  210.7 2.4 fusion.79
  220.3 0.9 constant_dynamic-slice_fusion.8
  221.3 2.5 gather_fusion
  230.0 2.4 fusion.78
  232.4 2.4 fusion.79
  242.0 0.9 constant_dynamic-slice_fusion.8
  243.0 2.5 gather_fusion
  251.8 2.4 fusion.78
  254.1 2.4 fusion.79
  262.7 0.9 constant_dynamic-slice_fusion.7
  263.8 0.9 constant_dynamic-slice_fusion.8
  264.7 2.5 gather_fusion
  273.5 2.4 fusion.78
  275.9 2.4 fusion.79
  278.2 6.5 %copy.68 = f32[5,2,1024,128]{3,1,2,0:T(2,128)S(1)} copy(f32[5,2,1024,128]{3,2,0,1:T(8,128)} %get-tuple-element.160) | data formatting | bytes 10485760 | tf_op jit(solution)/shard_map/while | solution.py:133
  285.0 6.9 %collective-permute-start.4 = (f32[2,1024,128]{2,0,1:T(2,128)S(1)}, f32[2,1024,128]{2,0,1:T(2,128)S(1)}, u32[]{:S(2)}, u32[]{:S(2)}) collective-permute-start(f32[2,1024,128]{2,0,1:T(2,128)S(1)} %get-tuple-element.197), channel_id=1, source_target_pairs={{0,496},{8,504},{16,0},{24,8},{32,16},{40,24},{48,32},{56,40},{64,... | collective-permute-start | bytes 3145736 | tf_op jit(solution)/shard_map/ppermute | solution.py:12
  292.0 1.9 collective-permute-start.7
  293.9 1.9 collective-permute-start.6
  295.8 6.9 %collective-permute-start.5 = (f32[2,1024,128]{2,0,1:T(2,128)S(1)}, f32[2,1024,128]{2,0,1:T(2,128)S(1)}, u32[]{:S(2)}, u32[]{:S(2)}) collective-permute-start(f32[2,1024,128]{2,0,1:T(2,128)S(1)} %get-tuple-element.200), channel_id=1, source_target_pairs={{0,504},{8,0},{16,8},{24,16},{32,24},{40,32},{48,40},{56,48},{64,5... | collective-permute-start | bytes 3145736 | tf_op jit(solution)/shard_map/ppermute | solution.py:12
  302.7 27.2 %collective-permute-done.4 = f32[2,1024,128]{2,0,1:T(2,128)S(1)} collective-permute-done((f32[2,1024,128]{2,0,1:T(2,128)S(1)}, f32[2,1024,128]{2,0,1:T(2,128)S(1)}, u32[]{:S(2)}, u32[]{:S(2)}) %collective-permute-start.4) | collective-permute-done | bytes 1048608 | tf_op jit(solution)/shard_map/ppermute | solution.py:12
  329.9 12.8 %collective-permute-done.7 = f32[2,1024,128]{2,0,1:T(2,128)S(1)} collective-permute-done((f32[2,1024,128]{2,0,1:T(2,128)S(1)}, f32[2,1024,128]{2,0,1:T(2,128)S(1)}, u32[]{:S(2)}, u32[]{:S(2)}) %collective-permute-start.7) | collective-permute-done | bytes 1048608 | tf_op jit(solution)/shard_map/ppermute | solution.py:12
  342.7 19.6 %collective-permute-done.6 = f32[2,1024,128]{2,0,1:T(2,128)S(1)} collective-permute-done((f32[2,1024,128]{2,0,1:T(2,128)S(1)}, f32[2,1024,128]{2,0,1:T(2,128)S(1)}, u32[]{:S(2)}, u32[]{:S(2)}) %collective-permute-start.6) | collective-permute-done | bytes 1048608 | tf_op jit(solution)/shard_map/ppermute | solution.py:12
  362.3 1.1 fusion.38
  363.4 13.8 %all_to_all.33 = bf16[2,1024,128]{2,0,1:T(2,128)(2,1)S(1)} all-to-all(bf16[2,1024,128]{2,0,1:T(2,128)(2,1)S(1)} %fusion.38), channel_id=1, replica_groups=mesh['dp'=64,'mp'=8] {'mp'}, dimensions={1} | all-to-all | bytes 1048576 | tf_op jit(solution)/shard_map/all_to_all | solution.py:146
  (276 shorter events, 77.6 us)
Async XLA Ops:
  4.4 29.4 %collective-permute-start = (bf16[2,128,1024]{1,0,2:T(2,128)(2,1)S(1)}, bf16[2,128,1024]{1,0,2:T(2,128)(2,1)S(1)}, u32[]{:S(2)}, u32[]{:S(2)}) collective-permute-start(bf16[2,128,1024]{1,0,2:T(2,128)(2,1)S(1)} %pad_maximum_fusion.1), channel_id=1, source_target_pairs={{0,16},{8,24},{16,32},{24,40},{32,48},{40,56},{48,64},{56,72},{64,... | collective-permute-start | bytes 1572872 | tf_op jit(solution)/shard_map/ppermute | solution.py:12
  10.1 42.8 %collective-permute-start.1 = (bf16[2,128,1024]{1,0,2:T(2,128)(2,1)S(1)}, bf16[2,128,1024]{1,0,2:T(2,128)(2,1)S(1)}, u32[]{:S(2)}, u32[]{:S(2)}) collective-permute-start(bf16[2,128,1024]{1,0,2:T(2,128)(2,1)S(1)} %pad_maximum_fusion.1), channel_id=1, source_target_pairs={{0,8},{8,16},{16,24},{24,32},{32,40},{40,48},{48,56},{56,64},{64,7... | collective-permute-start | bytes 1572872 | tf_op jit(solution)/shard_map/ppermute | solution.py:12
  13.7 42.5 %collective-permute-start.2 = (bf16[2,128,1024]{1,0,2:T(2,128)(2,1)S(1)}, bf16[2,128,1024]{1,0,2:T(2,128)(2,1)S(1)}, u32[]{:S(2)}, u32[]{:S(2)}) collective-permute-start(bf16[2,128,1024]{1,0,2:T(2,128)(2,1)S(1)} %pad_maximum_fusion.1), channel_id=1, source_target_pairs={{0,504},{8,0},{16,8},{24,16},{32,24},{40,32},{48,40},{56,48},{64,5... | collective-permute-start | bytes 1572872 | tf_op jit(solution)/shard_map/ppermute | solution.py:12
  22.4 35.0 %collective-permute-start.3 = (bf16[2,128,1024]{1,0,2:T(2,128)(2,1)S(1)}, bf16[2,128,1024]{1,0,2:T(2,128)(2,1)S(1)}, u32[]{:S(2)}, u32[]{:S(2)}) collective-permute-start(bf16[2,128,1024]{1,0,2:T(2,128)(2,1)S(1)} %pad_maximum_fusion.1), channel_id=1, source_target_pairs={{0,496},{8,504},{16,0},{24,8},{32,16},{40,24},{48,32},{56,40},{64,... | collective-permute-start | bytes 1572872 | tf_op jit(solution)/shard_map/ppermute | solution.py:12
  58.6 5.5 %copy-start.1 = (s32[64]{0:T(128)S(1)}, s32[64]{0:T(128)}, u32[]{:S(2)}) copy-start(s32[64]{0:T(128)} %param.17) | copy-start | bytes 772
  58.6 5.5 %copy-start.2 = (s32[16]{0:T(128)S(1)}, s32[16]{0:T(128)}, u32[]{:S(2)}) copy-start(s32[16]{0:T(128)} %param.18) | copy-start | bytes 196
  58.6 5.8 %copy-start = (s32[16]{0:T(128)S(1)}, s32[16]{0:T(128)}, u32[]{:S(2)}) copy-start(s32[16]{0:T(128)} %param.19) | copy-start | bytes 196
  58.6 37.5 %all-to-all-start = ((bf16[5,2,128,1024]{2,1,0,3:T(2,128)(2,1)}), bf16[5,2,128,1024]{2,1,0,3:T(2,128)(2,1)S(1)}, u32[]{:S(2)}, u32[]{:S(2)}) async-start(bf16[5,2,128,1024]{2,1,0,3:T(2,128)(2,1)} %bitcast_dynamic-update-slice_fusion.4), calls=%async_computation | async-start | bytes 5242880 | tf_op jit(solution)/shard_map/all_to_all | solution.py:98
  285.0 44.9 %collective-permute-start.4 = (f32[2,1024,128]{2,0,1:T(2,128)S(1)}, f32[2,1024,128]{2,0,1:T(2,128)S(1)}, u32[]{:S(2)}, u32[]{:S(2)}) collective-permute-start(f32[2,1024,128]{2,0,1:T(2,128)S(1)} %get-tuple-element.197), channel_id=1, source_target_pairs={{0,496},{8,504},{16,0},{24,8},{32,16},{40,24},{48,32},{56,40},{64,... | collective-permute-start | bytes 3145736 | tf_op jit(solution)/shard_map/ppermute | solution.py:12
  292.0 50.8 %collective-permute-start.7 = (f32[2,1024,128]{2,0,1:T(2,128)S(1)}, f32[2,1024,128]{2,0,1:T(2,128)S(1)}, u32[]{:S(2)}, u32[]{:S(2)}) collective-permute-start(f32[2,1024,128]{2,0,1:T(2,128)S(1)} %get-tuple-element.198), channel_id=1, source_target_pairs={{0,16},{8,24},{16,32},{24,40},{32,48},{40,56},{48,64},{56,72},{64,... | collective-permute-start | bytes 3145736 | tf_op jit(solution)/shard_map/ppermute | solution.py:12
  293.9 68.4 %collective-permute-start.6 = (f32[2,1024,128]{2,0,1:T(2,128)S(1)}, f32[2,1024,128]{2,0,1:T(2,128)S(1)}, u32[]{:S(2)}, u32[]{:S(2)}) collective-permute-start(f32[2,1024,128]{2,0,1:T(2,128)S(1)} %get-tuple-element.199), channel_id=1, source_target_pairs={{0,8},{8,16},{16,24},{24,32},{32,40},{40,48},{48,56},{56,64},{64,7... | collective-permute-start | bytes 3145736 | tf_op jit(solution)/shard_map/ppermute | solution.py:12
  295.8 66.5 %collective-permute-start.5 = (f32[2,1024,128]{2,0,1:T(2,128)S(1)}, f32[2,1024,128]{2,0,1:T(2,128)S(1)}, u32[]{:S(2)}, u32[]{:S(2)}) collective-permute-start(f32[2,1024,128]{2,0,1:T(2,128)S(1)} %get-tuple-element.200), channel_id=1, source_target_pairs={{0,504},{8,0},{16,8},{24,16},{32,24},{40,32},{48,40},{56,48},{64,5... | collective-permute-start | bytes 3145736 | tf_op jit(solution)/shard_map/ppermute | solution.py:12
where the time goes:
time: 383 us; the launch traced here: 380 us
  waiting for transfers between devices  116 us (30%)
  local copies, waits for them, and re-layouts  89.8 us (23%)
  other arithmetic  54.6 us (14%)
  starting transfers between devices  45.4 us (12%)
  loops' own time  31.8 us (8%)
  matrix products  27.8 us (7%)
  blocking collectives  13.8 us (4%)
    ppermute x8, waiting for transfers between devices, shifted(): return lax.ppermute(value, axis, pairs)  84.7 us
    ppermute x8, starting transfers between devices, shifted(): return lax.ppermute(value, axis, pairs)  39.9 us
    dynamic_update_slice x16, other arithmetic, advance(): lax.dynamic_update_index_in_dim(totals, current + terms[member], target, 0)  37.9 us
    another operation x1, loops' own time, per_device(): lax.scan(advance, start_totals, (blocked(query), blocked(comp_key), block...  31.8 us
    all_to_all x1, waiting for transfers between devices, per_device(): lax.all_to_all(fetch_nearby(prefix_pair), 'mp', split_axis=3, concat_axis...  31.6 us
    gather x8, local copies, waits for them, and re-layouts, advance(): chosen = jnp.take(nearby, block_near, axis=0)  19.9 us
    dynamic_slice x16, local copies, waits for them, and re-layouts, per_device(): lax.scan(advance, start_totals, (blocked(query), blocked(comp_key), block...  14.7 us
    all_to_all x1, blocking collectives, per_device(): lax.all_to_all(gathered.astype(jnp.bfloat16), 'mp', split_axis=1, concat_...  13.8 us
  transfers between devices with their start and end apart: 9, of which 6 were waited for; matrix products, arithmetic and copies ran while one was open for 2% of the time, Pallas kernels for 0%

commit v1 on v0

v1 whole, which is shorter than its diff:
```python
import functools

import jax
import jax.numpy as jnp
from jax import lax
from jax.experimental import pallas as pl
from jax.experimental.pallas import tpu as pltpu
from jax.sharding import PartitionSpec as P

HD = 128
SCALE = HD**-0.5
LOG2E = 1.4426950408889634
CHUNK = 128
HALF = 16
HIDDEN = -1e30
NT = (((1,), (1,)), ((), ()))


def dot(left, right):
    return jnp.dot(left, right, preferred_element_type=jnp.float32)


def dot_nt(left, right):
    return lax.dot_general(left, right, NT, preferred_element_type=jnp.float32)


def fold(value, reduce):
    return reduce(value.reshape(-1, 8, value.shape[-1]), axis=0)


def block_rows(ref, slot, half):
    heads = ref.shape[2] // HD
    rows = pl.ds(pl.multiple_of(half * HALF, HALF), HALF)
    return jnp.concatenate(
        [ref[slot, rows, head * HD : (head + 1) * HD] for head in range(heads)], axis=0
    )


def live_rows(block, half, length):
    row = lax.broadcasted_iota(jnp.int32, block.shape, 0) % HALF + half * HALF
    return jnp.where(row < length, block.astype(jnp.float32), 0.0).astype(jnp.bfloat16)


def two_blocks(
    first, second, lengths, query, comp_key, comp_value, grad_out, dq_buf, dk_sum, dv_sum,
    keys, values, key_flip, weight_buf, slope_buf, exp_buf, prob_buf, key_sum, value_sum
):
    slots = query.shape[1]
    prefix = key_sum.shape[0]
    extent = keys.shape[0]
    blocks = (first, second)
    spots = [(slot, half, jnp.where(valid, lengths[slot], 0)) for slot, half, valid in blocks]
    queries = jnp.concatenate([block_rows(query, slot, half) for slot, half, _ in spots], axis=0)
    upstream = jnp.concatenate(
        [live_rows(block_rows(grad_out, slot, half), half, size) for slot, half, size in spots],
        axis=0,
    )
    lanes = queries.shape[0]
    for at, (slot, _, _) in enumerate(spots):
        keys[prefix + at * slots : prefix + (at + 1) * slots] = comp_key[slot]
        values[prefix + at * slots : prefix + (at + 1) * slots] = comp_value[slot]

    row = lax.broadcasted_iota(jnp.int32, (2 * slots, lanes), 0)
    lane = lax.broadcasted_iota(jnp.int32, (2 * slots, lanes), 1)
    side = lane // (lanes // 2)
    key_at = row % slots
    query_at = lane % HALF + HALF * jnp.where(side == 0, spots[0][1], spots[1][1])
    size = jnp.where(side == 0, spots[0][2], spots[1][2])
    visible = (row // slots == side) & (key_at <= query_at) & (key_at < size)

    spans = [(start, min(start + CHUNK, extent)) for start in range(0, extent, CHUNK)]
    scores = dot_nt(keys[...], queries)
    slope_buf[...] = dot_nt(values[...], upstream)
    tops, sums = [], []
    for start, end in spans:
        part = scores[start:end]
        if start >= prefix:
            part = jnp.where(visible, part, HIDDEN)
        top = jnp.max(fold(part, jnp.max), axis=0, keepdims=True)
        part = jnp.exp2((part - top) * (SCALE * LOG2E))
        exp_buf[start:end] = part
        tops.append(top)
        sums.append(fold(part, jnp.sum))
    top = functools.reduce(jnp.maximum, tops)
    shares = [jnp.exp2((each - top) * (SCALE * LOG2E)) for each in tops]
    total = sum(part * share for part, share in zip(sums, shares))
    inverse = 1.0 / jnp.sum(total, axis=0, keepdims=True)
    shares = [share * inverse for share in shares]

    delta = 0.0
    for (start, end), share in zip(spans, shares):
        weight = (exp_buf[start:end] * share).astype(jnp.bfloat16)
        weight_buf[start:end] = weight
        delta = delta + fold(weight.astype(jnp.float32) * slope_buf[start:end], jnp.sum)
    delta = jnp.sum(delta, axis=0, keepdims=True)
    terms = dot(weight_buf[...], upstream)
    value_sum[...] += terms[:prefix]
    for at, (slot, _, _) in enumerate(spots):
        dv_sum[slot] += terms[prefix + at * slots : prefix + (at + 1) * slots]

    for (start, end), share in zip(spans, shares):
        part = exp_buf[start:end] * share * (slope_buf[start:end] - delta)
        prob_buf[start:end] = part.astype(jnp.bfloat16)
    terms = dot(prob_buf[...], queries)
    key_sum[...] += terms[:prefix]
    for at, (slot, _, _) in enumerate(spots):
        dk_sum[slot] += terms[prefix + at * slots : prefix + (at + 1) * slots]
    own_flip = keys[prefix:].astype(jnp.float32).T.astype(jnp.bfloat16)
    flipped = dot(key_flip[...], prob_buf[:prefix]) + dot(own_flip, prob_buf[prefix:])
    query_grad = (flipped.T * SCALE).astype(jnp.bfloat16)
    for at, (slot, half, valid) in enumerate(blocks):

        @pl.when(valid)
        def _():
            rows = pl.ds(pl.multiple_of(half * HALF, HALF), HALF)
            for head in range(query.shape[2] // HD):
                start = at * (lanes // 2) + head * HALF
                dq_buf[slot, rows, head * HD : (head + 1) * HD] = query_grad[start : start + HALF]


def near_kernel(
    code, chained, near, lengths, query, comp_key, comp_value, grad_out, pair, *refs
):
    if chained:
        refs = refs[3:]
    (term, dq, dk, dv, dq_buf, dk_buf, dv_buf, dk_sum, dv_sum, keys, values, key_flip,
     weight_buf, slope_buf, exp_buf, prob_buf, key_sum, value_sum, listed, out_sem) = refs
    count = near.shape[0]
    prefix = key_sum.shape[0]
    rows = pair.shape[2]

    def stores(slot):
        return [
            pltpu.make_async_copy(source.at[slot], target.at[slot], out_sem.at[at, slot])
            for at, (source, target) in enumerate(((dq_buf, dq), (dk_buf, dk), (dv_buf, dv)))
        ]

    def gather(slot, found):
        @pl.when(near[slot] == code)
        def _():
            listed[found] = 2 * slot
            listed[found + 1] = 2 * slot + 1
            dk_sum[slot] = jnp.zeros_like(dk_sum[slot])
            dv_sum[slot] = jnp.zeros_like(dv_sum[slot])

        blocks = jnp.where(lengths[slot] > HALF, 2, 1)
        return found + jnp.where(near[slot] == code, blocks, 0)

    found = lax.fori_loop(0, count, gather, 0)
    key_sum[...] = jnp.zeros_like(key_sum)
    value_sum[...] = jnp.zeros_like(value_sum)

    @pl.when(found > 0)
    def _():
        for at in range(pair.shape[0]):
            span = slice(at * rows, (at + 1) * rows)
            keys[span] = pair[at, 0]
            values[span] = pair[at, 1]
            key_flip[:, span] = pair[at, 0].astype(jnp.float32).T.astype(jnp.bfloat16)

    def step(at, carry):
        def spot(index):
            return listed[index] // 2, listed[index] % 2

        one_slot, one_half = spot(2 * at)
        valid = 2 * at + 1 < found
        two_slot, two_half = spot(jnp.where(valid, 2 * at + 1, 2 * at))
        two_blocks(
            (one_slot, one_half, 2 * at < found), (two_slot, two_half, valid), lengths,
            query, comp_key, comp_value, grad_out, dq_buf, dk_sum, dv_sum, keys, values,
            key_flip, weight_buf, slope_buf, exp_buf, prob_buf, key_sum, value_sum
        )
        return carry

    lax.fori_loop(0, (found + 1) // 2, step, 0)

    def send(slot, carry):
        @pl.when(near[slot] == code)
        def _():
            @pl.when(lengths[slot] <= HALF)
            def _():
                dq_buf[slot, HALF:] = jnp.zeros_like(dq_buf[slot, HALF:])

            dk_buf[slot] = (dk_sum[slot] * SCALE).astype(jnp.bfloat16)
            dv_buf[slot] = dv_sum[slot].astype(jnp.bfloat16)
            for copy in stores(slot):
                copy.start()

        return carry

    def finish(slot, carry):
        @pl.when(near[slot] == code)
        def _():
            for copy in stores(slot):
                copy.wait()

        return carry

    lax.fori_loop(0, count, send, 0)
    for at in range(pair.shape[0]):
        span = slice(at * rows, (at + 1) * rows)
        term[at, 0] = (key_sum[span] * SCALE).astype(term.dtype)
        term[at, 1] = value_sum[span].astype(term.dtype)
    lax.fori_loop(0, count, finish, 0)


def near_grads(code, pair, near, lengths, query, comp_key, comp_value, grad_out, chain, kind):
    count, slots, width = query.shape
    lanes = 2 * HALF * (width // HD)
    prefix = pair.shape[0] * pair.shape[2]
    extent = prefix + 2 * slots
    anywhere = pl.BlockSpec(memory_space=pl.ANY)
    scalar = pl.BlockSpec(memory_space=pltpu.SMEM)
    vmem = pl.BlockSpec(memory_space=pltpu.VMEM)
    narrow = jax.ShapeDtypeStruct(comp_key.shape, jnp.bfloat16)
    operands = [near, lengths, query, comp_key, comp_value, grad_out, pair]
    aliases = {}
    if chain is not None:
        aliases = {len(operands) + at: 1 + at for at in range(3)}
        operands += list(chain)
    work = 4
    out = pl.pallas_call(
        functools.partial(near_kernel, code, chain is not None),
        out_shape=[
            jax.ShapeDtypeStruct(pair.shape, kind),
            jax.ShapeDtypeStruct(query.shape, jnp.bfloat16),
            narrow,
            narrow,
        ],
        in_specs=[scalar] * 2 + [vmem] * 5 + [anywhere] * len(aliases),
        out_specs=[vmem] + [anywhere] * 3,
        scratch_shapes=[
            pltpu.VMEM(query.shape, jnp.bfloat16),
            pltpu.VMEM(comp_key.shape, jnp.bfloat16),
            pltpu.VMEM(comp_key.shape, jnp.bfloat16),
            pltpu.VMEM(comp_key.shape, jnp.float32),
            pltpu.VMEM(comp_key.shape, jnp.float32),
            pltpu.VMEM((extent, HD), jnp.bfloat16),
            pltpu.VMEM((extent, HD), jnp.bfloat16),
            pltpu.VMEM((HD, prefix), jnp.bfloat16),
            pltpu.VMEM((extent, lanes), jnp.bfloat16),
            pltpu.VMEM((extent, lanes), jnp.float32),
            pltpu.VMEM((extent, lanes), jnp.float32),
            pltpu.VMEM((extent, lanes), jnp.bfloat16),
            pltpu.VMEM((prefix, HD), jnp.float32),
            pltpu.VMEM((prefix, HD), jnp.float32),
            pltpu.SMEM((2 * count + 2,), jnp.int32),
            pltpu.SemaphoreType.DMA((3, count)),
        ],
        input_output_aliases=aliases,
        compiler_params=pltpu.CompilerParams(vmem_limit_bytes=28 * 2**20),
        cost_estimate=pl.CostEstimate(
            flops=work * 12 * extent * lanes * HD,
            bytes_accessed=work * 10 * slots * width,
            transcendentals=work * extent * lanes,
        ),
    )(*operands)
    return out[0], out[1:]


def split_kernel(key, value, pair):
    for head in range(pair.shape[0]):
        columns = slice(head * HD, (head + 1) * HD)
        pair[head, 0] = key[:, columns]
        pair[head, 1] = value[:, columns]


def split_heads(key, value, shards):
    return pl.pallas_call(
        split_kernel,
        out_shape=jax.ShapeDtypeStruct((shards, 2, key.shape[0], HD), key.dtype),
    )(key, value)


def join_kernel(pair, key, value):
    for head in range(pair.shape[0]):
        columns = slice(head * HD, (head + 1) * HD)
        key[:, columns] = pair[head, 0]
        value[:, columns] = pair[head, 1]


def join_heads(pair):
    shards, _, rows, _ = pair.shape
    whole = jax.ShapeDtypeStruct((rows, shards * HD), pair.dtype)
    return pl.pallas_call(join_kernel, out_shape=[whole, whole])(pair)


def shifted(value, steps):
    size, shards = lax.axis_size("dp"), lax.axis_size("mp")
    pairs = []
    for at in range(size):
        for shard in range(shards):
            target = (at + (steps if shard % 2 == 0 else -steps)) % size
            pairs.append((at * shards + shard, target * shards + shard))
    return lax.ppermute(value, ("dp", "mp"), pairs)


def per_device(
    query, comp_key, comp_value, prefix_key, prefix_value, grad_out, owner, group, lengths
):
    axis_count = lax.axis_size("dp")
    shards = lax.axis_size("mp")
    position = lax.axis_index("dp")
    prompt_ids = jnp.arange(owner.shape[0], dtype=jnp.int32)
    holder_of = jnp.sum(jnp.where(group[:, None] == prompt_ids[None, :], owner[None, :], 0), axis=1)
    near = ((holder_of - position + 2 + axis_count) % axis_count).astype(jnp.int32)
    near = jnp.where(lax.axis_index("mp") % 2 == 0, near, 4 - near)

    pair = split_heads(prefix_key[0], prefix_value[0], shards)
    own = lax.all_to_all(pair, "mp", split_axis=0, concat_axis=0, tiled=True)
    low_one = shifted(own, 1)
    up_one = shifted(own, -1)
    low_two = shifted(low_one, 1)
    up_two = shifted(up_one, -1)

    arrays = (near, lengths, query, comp_key, comp_value, grad_out)
    own_term, chain = near_grads(2, own, *arrays, None, jnp.float32)
    low_two_term, chain = near_grads(0, low_two, *arrays, chain, jnp.bfloat16)
    up_two_term, chain = near_grads(4, up_two, *arrays, chain, jnp.bfloat16)
    low_term, chain = near_grads(1, low_one, *arrays, chain, jnp.float32)
    up_term, chain = near_grads(3, up_one, *arrays, chain, jnp.float32)
    low_back = shifted(low_two_term, -1).astype(jnp.float32)
    up_back = shifted(up_two_term, 1).astype(jnp.float32)
    low_back = shifted((low_term + low_back).astype(jnp.bfloat16), -1).astype(jnp.float32)
    up_back = shifted((up_term + up_back).astype(jnp.bfloat16), 1).astype(jnp.float32)
    gathered = (own_term + low_back + up_back).astype(jnp.bfloat16)
    back = lax.all_to_all(gathered, "mp", split_axis=0, concat_axis=0, tiled=True)
    key_back, value_back = join_heads(back)
    return chain[0], chain[1], chain[2], key_back[None], value_back[None]


def solution(mesh):
    return jax.shard_map(
        per_device,
        mesh=mesh,
        in_specs=(
            P("dp", None, "mp"),
            P("dp", None, "mp"),
            P("dp", None, "mp"),
            P("dp", "mp", None),
            P("dp", "mp", None),
            P("dp", None, "mp"),
            P(),
            P("dp"),
            P("dp"),
        ),
        out_specs=(
            P("dp", None, "mp"),
            P("dp", None, "mp"),
            P("dp", None, "mp"),
            P("dp", "mp", None),
            P("dp", "mp", None),
        ),
        check_vma=False,
    )
```

time: 383 us -> 131 us (0.34)
  waiting for transfers between devices: 116 us -> 18.9 us
  local copies, waits for them, and re-layouts: 89.8 us -> 2.49 us
  other arithmetic: 54.6 us -> 0.65 us
  Pallas kernels: 0 us -> 32.2 us
  loops' own time: 31.8 us -> 0 us
  matrix products: 27.8 us -> 0 us
  blocking collectives: 13.8 us -> 35.7 us
  starting transfers between devices: 45.4 us -> 39.8 us
    ppermute x8, waiting for transfers between devices: 84.7 us -> 18.9 us  [shifted(): return lax.ppermute(value, ('dp', 'mp'), pairs)]
    dynamic_update_slice x16 -> x0, other arithmetic: 37.9 us -> none  [advance(): lax.dynamic_update_index_in_dim(totals, current + terms[member], target, 0)]
    pallas_call x0 -> x7, Pallas kernels: none -> 32.2 us  [the longest x5 28.2 us: near_grads(): pl.pallas_call(functools.partial(near_kernel, code, chain is not None), o...]
    another operation x1 -> x0, loops' own time: 31.8 us -> none  [per_device(): lax.scan(advance, start_totals, (blocked(query), blocked(comp_key), block...]
    all_to_all x1 -> x0, waiting for transfers between devices: 31.6 us -> none  [per_device(): lax.all_to_all(fetch_nearby(prefix_pair), 'mp', split_axis=3, concat_axis...]
    dot_general x48 -> x0, matrix products: 27.8 us -> none  [the longest x8 5.96 us: slot_grads(): jnp.einsum('igrd,jgd->grij', upstream, all_values, preferred_element_type...]
    all_to_all x1 -> x2, blocking collectives: 13.8 us -> 35.7 us  [the longest x1 19.6 us: per_device(): own = lax.all_to_all(pair, 'mp', split_axis=0, concat_axis=0, tiled=True)]
    gather x8 -> x0, local copies, waits for them, and re-layouts: 19.9 us -> none  [advance(): chosen = jnp.take(nearby, block_near, axis=0)]
  transfers between devices with their start and end apart: 9 -> 8, of which waited for: 6 -> 4; matrix products, arithmetic and copies ran while one was open for 2% -> 0% of each run, Pallas kernels for 0% -> 22%
where the time goes in v1:
time: 131 us
  starting transfers between devices  39.8 us (30%)
  blocking collectives  35.7 us (27%)
  Pallas kernels  32.2 us (25%)
  waiting for transfers between devices  18.9 us (14%)
  local copies, waits for them, and re-layouts  2.49 us (2%)
    ppermute x8, starting transfers between devices, shifted(): return lax.ppermute(value, ('dp', 'mp'), pairs)  39.8 us
    pallas_call x5, Pallas kernels, near_grads(): pl.pallas_call(functools.partial(near_kernel, code, chain is not None), o...  28.2 us
    all_to_all x1, blocking collectives, per_device(): own = lax.all_to_all(pair, 'mp', split_axis=0, concat_axis=0, tiled=True)  19.6 us
    ppermute x8, waiting for transfers between devices, shifted(): return lax.ppermute(value, ('dp', 'mp'), pairs)  18.9 us
    all_to_all x1, blocking collectives, per_device(): lax.all_to_all(gathered, 'mp', split_axis=0, concat_axis=0, tiled=True)  16 us
  transfers between devices with their start and end apart: 8, of which 4 were waited for; matrix products, arithmetic and copies ran while one was open for 0% of the time, Pallas kernels for 22%

profile of v1, /device:TPU:1, one launch (start us, length us, event | category | flops | bytes accessed | tf_op | source)
XLA Modules:
  0.0 130.6 jit_solution(14405304318600261217)
XLA Ops:
  0.6 0.0 copy-start
  0.6 0.0 copy-start.1
  0.7 2.1 %shard_map.128 = bf16[8,2,128,128]{3,2,1,0:T(8,128)(2,1)} custom-call(bf16[128,1024]{1,0:T(8,128)(2,1)} %bitcast.4, bf16[128,1024]{1,0:T(8,128)(2,1)} %bitcast.5), custom_call_target="tpu_custom_call" | custom-call | tf_op jit(solution)/shard_map/pallas_call | solution.py:269
  2.7 19.6 %all_to_all.10.pair = bf16[8,2,128,128]{3,2,1,0:T(8,128)(2,1)S(1)} all-to-all(bf16[8,2,128,128]{3,2,1,0:T(8,128)(2,1)} %shard_map.128), channel_id=1, replica_groups=mesh['dp'=64,'mp'=8] {'mp'}, dimensions={0} | all-to-all | bytes 1048576 | tf_op jit(solution)/shard_map/all_to_all | solution.py:310
  22.3 9.0 %collective-permute-start.1 = (bf16[8,2,128,128]{3,2,1,0:T(8,128)(2,1)S(1)}, bf16[8,2,128,128]{3,2,1,0:T(8,128)(2,1)}, u32[]{:S(2)}, u32[]{:S(2)}) collective-permute-start(bf16[8,2,128,128]{3,2,1,0:T(8,128)(2,1)S(1)} %all_to_all.10.pair), channel_id=1, source_target_pairs={{0,8},{1,505},{2,10},{3,507},{4,12},{5,509},{6,14},{7,511},{8,16},... | collective-permute-start | bytes 1572872 | tf_op jit(solution)/shard_map/ppermute | solution.py:295
  31.4 1.9 %collective-permute-start = (bf16[8,2,128,128]{3,2,1,0:T(8,128)(2,1)S(1)}, bf16[8,2,128,128]{3,2,1,0:T(8,128)(2,1)S(1)}, u32[]{:S(2)}, u32[]{:S(2)}) collective-permute-start(bf16[8,2,128,128]{3,2,1,0:T(8,128)(2,1)S(1)} %all_to_all.10.pair), channel_id=1, source_target_pairs={{0,504},{1,9},{2,506},{3,11},{4,508},{5,13},{6,510},{7,15},{8,0},{... | collective-permute-start | bytes 1572872 | tf_op jit(solution)/shard_map/ppermute | solution.py:295
  33.3 6.3 %collective-permute-done.1.pair = bf16[8,2,128,128]{3,2,1,0:T(8,128)(2,1)} collective-permute-done((bf16[8,2,128,128]{3,2,1,0:T(8,128)(2,1)S(1)}, bf16[8,2,128,128]{3,2,1,0:T(8,128)(2,1)}, u32[]{:S(2)}, u32[]{:S(2)}) %collective-permute-start.1) | collective-permute-done | bytes 524320 | tf_op jit(solution)/shard_map/ppermute | solution.py:295
  39.6 7.4 %collective-permute-start.3 = (bf16[8,2,128,128]{3,2,1,0:T(8,128)(2,1)}, bf16[8,2,128,128]{3,2,1,0:T(8,128)(2,1)}, u32[]{:S(2)}, u32[]{:S(2)}) collective-permute-start(bf16[8,2,128,128]{3,2,1,0:T(8,128)(2,1)} %collective-permute-done.1.pair), channel_id=1, source_target_pairs={{0,8},{1,505},{2,10},{3,507},{4,12},{5,509},{6,14},{7,511},{8,16},... | collective-permute-start | bytes 1572872 | tf_op jit(solution)/shard_map/ppermute | solution.py:295
  47.0 0.0 copy-start.7
  47.0 0.0 copy-start.8
  47.0 0.6 copy-done.7
  47.7 0.0 copy-done.8
  47.7 0.2 select_reduce_fusion
  47.9 0.0 copy-start.6
  47.9 0.0 collective-permute-done.pair
  47.9 1.9 %collective-permute-start.2 = (bf16[8,2,128,128]{3,2,1,0:T(8,128)(2,1)S(1)}, bf16[8,2,128,128]{3,2,1,0:T(8,128)(2,1)S(1)}, u32[]{:S(2)}, u32[]{:S(2)}) collective-permute-start(bf16[8,2,128,128]{3,2,1,0:T(8,128)(2,1)S(1)} %collective-permute-done.pair), channel_id=1, source_target_pairs={{0,504},{1,9},{2,506},{3,11},{4,508},{5,13},{6,510},{7,15},{8,0},{... | collective-permute-start | bytes 1572872 | tf_op jit(solution)/shard_map/ppermute | solution.py:295
  49.8 0.0 copy-done
  49.8 0.0 copy-done.1
  49.9 0.0 copy-done.6
  49.9 0.0 copy-start.2
  49.9 0.9 copy-done.2
  50.8 0.0 copy-start.4
  50.8 0.9 copy-done.4
  51.7 1.8 %shard_map.129 = (f32[8,2,128,128]{3,2,1,0:T(8,128)S(1)}, bf16[16,32,1024]{2,1,0:T(8,128)(2,1)}, bf16[16,32,128]{2,1,0:T(8,128)(2,1)}, bf16[16,32,128]{2,1,0:T(8,128)(2,1)}) custom-call(s32[16]{0:T(128)S(1)} %broadcast_select_fusion.near, s32[16]{0:T(128)S(1)} %copy-done.6, bf16[16,32,1024]{2,1,0:T(8,128)(2,1)S(1)} %copy-done, ...), custom_call_target="tpu_custom_call" | custom-call | flops 1711276032 | bytes 1310720 | tf_op jit(solution)/shard_map/pallas_call | solution.py:222
  53.5 1.4 %collective-permute-done.3.pair = bf16[8,2,128,128]{3,2,1,0:T(8,128)(2,1)} collective-permute-done((bf16[8,2,128,128]{3,2,1,0:T(8,128)(2,1)}, bf16[8,2,128,128]{3,2,1,0:T(8,128)(2,1)}, u32[]{:S(2)}, u32[]{:S(2)}) %collective-permute-start.3) | collective-permute-done | bytes 524320 | tf_op jit(solution)/shard_map/ppermute | solution.py:295
  54.8 4.0 %shard_map.130 = (bf16[8,2,128,128]{3,2,1,0:T(8,128)(2,1)S(1)}, bf16[16,32,1024]{2,1,0:T(8,128)(2,1)}, bf16[16,32,128]{2,1,0:T(8,128)(2,1)}, bf16[16,32,128]{2,1,0:T(8,128)(2,1)}) custom-call(s32[16]{0:T(128)S(1)} %broadcast_select_fusion.near, s32[16]{0:T(128)S(1)} %copy-done.6, ...), custom_call_target="tpu_custom_call", output_to_operand_aliasing={{1}: (7, {}), {2}: (8, {}), {3}: (9, {})} | custom-call | flops 1711276032 | bytes 1310720 | tf_op jit(solution)/shard_map/pallas_call | solution.py:222
  58.8 4.5 %collective-permute-start.4 = (bf16[8,2,128,128]{3,2,1,0:T(8,128)(2,1)S(1)}, bf16[8,2,128,128]{3,2,1,0:T(8,128)(2,1)S(1)}, u32[]{:S(2)}, u32[]{:S(2)}) collective-permute-start(bf16[8,2,128,128]{3,2,1,0:T(8,128)(2,1)S(1)} %get-tuple-element.44), channel_id=1, source_target_pairs={{0,504},{1,9},{2,506},{3,11},{4,508},{5,13},{6,510},{7,15},{8,0},{... | collective-permute-start | bytes 1572872 | tf_op jit(solution)/shard_map/ppermute | solution.py:295
  63.3 0.0 collective-permute-done.2.pair
  63.4 0.0 copy-start.3
  63.4 0.0 copy-start.5
  63.4 11.1 %shard_map.131 = (bf16[8,2,128,128]{3,2,1,0:T(8,128)(2,1)S(1)}, bf16[16,32,1024]{2,1,0:T(8,128)(2,1)}, bf16[16,32,128]{2,1,0:T(8,128)(2,1)}, bf16[16,32,128]{2,1,0:T(8,128)(2,1)}) custom-call(s32[16]{0:T(128)S(1)} %broadcast_select_fusion.near, s32[16]{0:T(128)S(1)} %copy-done.6, ...), custom_call_target="tpu_custom_call", output_to_operand_aliasing={{1}: (7, {}), {2}: (8, {}), {3}: (9, {})} | custom-call | flops 1711276032 | bytes 1310720 | tf_op jit(solution)/shard_map/pallas_call | solution.py:222
  74.5 5.8 %collective-permute-start.6 = (bf16[8,2,128,128]{3,2,1,0:T(8,128)(2,1)S(1)}, bf16[8,2,128,128]{3,2,1,0:T(8,128)(2,1)S(1)}, u32[]{:S(2)}, u32[]{:S(2)}) collective-permute-start(bf16[8,2,128,128]{3,2,1,0:T(8,128)(2,1)S(1)} %get-tuple-element.46), channel_id=1, source_target_pairs={{0,8},{1,505},{2,10},{3,507},{4,12},{5,509},{6,14},{7,511},{8,16},... | collective-permute-start | bytes 1572872 | tf_op jit(solution)/shard_map/ppermute | solution.py:295
  80.3 0.0 copy-done.3
  80.3 0.0 copy-done.5
  80.3 4.0 %shard_map.132 = (f32[8,2,128,128]{3,2,1,0:T(8,128)S(1)}, bf16[16,32,1024]{2,1,0:T(8,128)(2,1)}, bf16[16,32,128]{2,1,0:T(8,128)(2,1)}, bf16[16,32,128]{2,1,0:T(8,128)(2,1)}) custom-call(s32[16]{0:T(128)S(1)} %broadcast_select_fusion.near, s32[16]{0:T(128)S(1)} %copy-done.6, ...), custom_call_target="tpu_custom_call", output_to_operand_aliasing={{1}: (7, {}), {2}: (8, {}), {3}: (9, {})} | custom-call | flops 1711276032 | bytes 1310720 | tf_op jit(solution)/shard_map/pallas_call | solution.py:222
  84.3 7.3 %shard_map.133 = (f32[8,2,128,128]{3,2,1,0:T(8,128)S(1)}, bf16[16,32,1024]{2,1,0:T(8,128)(2,1)}, bf16[16,32,128]{2,1,0:T(8,128)(2,1)}, bf16[16,32,128]{2,1,0:T(8,128)(2,1)}) custom-call(s32[16]{0:T(128)S(1)} %broadcast_select_fusion.near, s32[16]{0:T(128)S(1)} %copy-done.6, ...), custom_call_target="tpu_custom_call", output_to_operand_aliasing={{1}: (7, {}), {2}: (8, {}), {3}: (9, {})} | custom-call | flops 1711276032 | bytes 1310720 | tf_op jit(solution)/shard_map/pallas_call | solution.py:222
  91.7 0.0 collective-permute-done.4
  91.7 0.1 add_convert_fusion.2
  91.8 1.9 %collective-permute-start.5 = (bf16[8,2,128,128]{3,2,1,0:T(8,128)(2,1)S(1)}, bf16[8,2,128,128]{3,2,1,0:T(8,128)(2,1)S(1)}, u32[]{:S(2)}, u32[]{:S(2)}) collective-permute-start(bf16[8,2,128,128]{3,2,1,0:T(8,128)(2,1)S(1)} %add_convert_fusion.2), channel_id=1, source_target_pairs={{0,504},{1,9},{2,506},{3,11},{4,508},{5,13},{6,510},{7,15},{8,0},{... | collective-permute-start | bytes 1572872 | tf_op jit(solution)/shard_map/ppermute | solution.py:295
  93.7 0.0 collective-permute-done.6
  93.7 0.1 add_convert_fusion.1
  93.9 7.3 %collective-permute-start.7 = (bf16[8,2,128,128]{3,2,1,0:T(8,128)(2,1)S(1)}, bf16[8,2,128,128]{3,2,1,0:T(8,128)(2,1)S(1)}, u32[]{:S(2)}, u32[]{:S(2)}) collective-permute-start(bf16[8,2,128,128]{3,2,1,0:T(8,128)(2,1)S(1)} %add_convert_fusion.1), channel_id=1, source_target_pairs={{0,8},{1,505},{2,10},{3,507},{4,12},{5,509},{6,14},{7,511},{8,16},... | collective-permute-start | bytes 1572872 | tf_op jit(solution)/shard_map/ppermute | solution.py:295
  101.2 4.5 %collective-permute-done.5 = bf16[8,2,128,128]{3,2,1,0:T(8,128)(2,1)S(1)} collective-permute-done((bf16[8,2,128,128]{3,2,1,0:T(8,128)(2,1)S(1)}, bf16[8,2,128,128]{3,2,1,0:T(8,128)(2,1)S(1)}, u32[]{:S(2)}, u32[]{:S(2)}) %collective-permute-start.5) | collective-permute-done | bytes 524320 | tf_op jit(solution)/shard_map/ppermute | solution.py:295
  105.6 6.8 %collective-permute-done.7 = bf16[8,2,128,128]{3,2,1,0:T(8,128)(2,1)S(1)} collective-permute-done((bf16[8,2,128,128]{3,2,1,0:T(8,128)(2,1)S(1)}, bf16[8,2,128,128]{3,2,1,0:T(8,128)(2,1)S(1)}, u32[]{:S(2)}, u32[]{:S(2)}) %collective-permute-start.7) | collective-permute-done | bytes 524320 | tf_op jit(solution)/shard_map/ppermute | solution.py:295
  112.4 0.2 add_convert_fusion
  112.6 16.0 %all_to_all.11.pair = bf16[8,2,128,128]{3,2,1,0:T(8,128)(2,1)} all-to-all(bf16[8,2,128,128]{3,2,1,0:T(8,128)(2,1)S(1)} %add_convert_fusion), channel_id=1, replica_groups=mesh['dp'=64,'mp'=8] {'mp'}, dimensions={0} | all-to-all | bytes 1048576 | tf_op jit(solution)/shard_map/all_to_all | solution.py:327
  128.7 2.0 %shard_map.134 = (bf16[128,1024]{1,0:T(8,128)(2,1)}, bf16[128,1024]{1,0:T(8,128)(2,1)}) custom-call(bf16[8,2,128,128]{3,2,1,0:T(8,128)(2,1)} %all_to_all.11.pair), custom_call_target="tpu_custom_call" | custom-call | tf_op jit(solution)/shard_map/pallas_call | solution.py:285
  (1 shorter events, 0.0 us)
Async XLA Ops:
  0.6 49.2 %copy-start = (bf16[16,32,1024]{2,1,0:T(8,128)(2,1)S(1)}, bf16[16,32,1024]{2,1,0:T(8,128)(2,1)}, u32[]{:S(2)}) copy-start(bf16[16,32,1024]{2,1,0:T(8,128)(2,1)} %query.9) | copy-start | bytes 3145732
  0.6 49.2 %copy-start.1 = (bf16[16,32,1024]{2,1,0:T(8,128)(2,1)S(1)}, bf16[16,32,1024]{2,1,0:T(8,128)(2,1)}, u32[]{:S(2)}) copy-start(bf16[16,32,1024]{2,1,0:T(8,128)(2,1)} %grad_out.9) | copy-start | bytes 3145732
  22.3 17.2 %collective-permute-start.1 = (bf16[8,2,128,128]{3,2,1,0:T(8,128)(2,1)S(1)}, bf16[8,2,128,128]{3,2,1,0:T(8,128)(2,1)}, u32[]{:S(2)}, u32[]{:S(2)}) collective-permute-start(bf16[8,2,128,128]{3,2,1,0:T(8,128)(2,1)S(1)} %all_to_all.10.pair), channel_id=1, source_target_pairs={{0,8},{1,505},{2,10},{3,507},{4,12},{5,509},{6,14},{7,511},{8,16},... | collective-permute-start | bytes 1572872 | tf_op jit(solution)/shard_map/ppermute | solution.py:295
  31.4 16.5 %collective-permute-start = (bf16[8,2,128,128]{3,2,1,0:T(8,128)(2,1)S(1)}, bf16[8,2,128,128]{3,2,1,0:T(8,128)(2,1)S(1)}, u32[]{:S(2)}, u32[]{:S(2)}) collective-permute-start(bf16[8,2,128,128]{3,2,1,0:T(8,128)(2,1)S(1)} %all_to_all.10.pair), channel_id=1, source_target_pairs={{0,504},{1,9},{2,506},{3,11},{4,508},{5,13},{6,510},{7,15},{8,0},{... | collective-permute-start | bytes 1572872 | tf_op jit(solution)/shard_map/ppermute | solution.py:295
  39.6 15.2 %collective-permute-start.3 = (bf16[8,2,128,128]{3,2,1,0:T(8,128)(2,1)}, bf16[8,2,128,128]{3,2,1,0:T(8,128)(2,1)}, u32[]{:S(2)}, u32[]{:S(2)}) collective-permute-start(bf16[8,2,128,128]{3,2,1,0:T(8,128)(2,1)} %collective-permute-done.1.pair), channel_id=1, source_target_pairs={{0,8},{1,505},{2,10},{3,507},{4,12},{5,509},{6,14},{7,511},{8,16},... | collective-permute-start | bytes 1572872 | tf_op jit(solution)/shard_map/ppermute | solution.py:295
  47.0 0.7 copy-start.7
  47.0 0.7 copy-start.8
  47.9 2.0 %copy-start.6 = (s32[16]{0:T(128)S(1)}, s32[16]{0:T(128)}, u32[]{:S(2)}) copy-start(s32[16]{0:T(128)} %lengths.9) | copy-start | bytes 196
  47.9 15.5 %collective-permute-start.2 = (bf16[8,2,128,128]{3,2,1,0:T(8,128)(2,1)S(1)}, bf16[8,2,128,128]{3,2,1,0:T(8,128)(2,1)S(1)}, u32[]{:S(2)}, u32[]{:S(2)}) collective-permute-start(bf16[8,2,128,128]{3,2,1,0:T(8,128)(2,1)S(1)} %collective-permute-done.pair), channel_id=1, source_target_pairs={{0,504},{1,9},{2,506},{3,11},{4,508},{5,13},{6,510},{7,15},{8,0},{... | collective-permute-start | bytes 1572872 | tf_op jit(solution)/shard_map/ppermute | solution.py:295
  49.9 0.9 copy-start.2
  50.8 0.9 copy-start.4
  58.8 32.9 %collective-permute-start.4 = (bf16[8,2,128,128]{3,2,1,0:T(8,128)(2,1)S(1)}, bf16[8,2,128,128]{3,2,1,0:T(8,128)(2,1)S(1)}, u32[]{:S(2)}, u32[]{:S(2)}) collective-permute-start(bf16[8,2,128,128]{3,2,1,0:T(8,128)(2,1)S(1)} %get-tuple-element.44), channel_id=1, source_target_pairs={{0,504},{1,9},{2,506},{3,11},{4,508},{5,13},{6,510},{7,15},{8,0},{... | collective-permute-start | bytes 1572872 | tf_op jit(solution)/shard_map/ppermute | solution.py:295
  63.4 17.0 %copy-start.3 = (bf16[16,32,128]{2,1,0:T(8,128)(2,1)S(1)}, bf16[16,32,128]{2,1,0:T(8,128)(2,1)}, u32[]{:S(2)}) copy-start(bf16[16,32,128]{2,1,0:T(8,128)(2,1)} %comp_key.9) | copy-start | bytes 393220
  63.4 17.0 %copy-start.5 = (bf16[16,32,128]{2,1,0:T(8,128)(2,1)S(1)}, bf16[16,32,128]{2,1,0:T(8,128)(2,1)}, u32[]{:S(2)}) copy-start(bf16[16,32,128]{2,1,0:T(8,128)(2,1)} %comp_value.9) | copy-start | bytes 393220
  74.5 19.3 %collective-permute-start.6 = (bf16[8,2,128,128]{3,2,1,0:T(8,128)(2,1)S(1)}, bf16[8,2,128,128]{3,2,1,0:T(8,128)(2,1)S(1)}, u32[]{:S(2)}, u32[]{:S(2)}) collective-permute-start(bf16[8,2,128,128]{3,2,1,0:T(8,128)(2,1)S(1)} %get-tuple-element.46), channel_id=1, source_target_pairs={{0,8},{1,505},{2,10},{3,507},{4,12},{5,509},{6,14},{7,511},{8,16},... | collective-permute-start | bytes 1572872 | tf_op jit(solution)/shard_map/ppermute | solution.py:295
  91.8 13.8 %collective-permute-start.5 = (bf16[8,2,128,128]{3,2,1,0:T(8,128)(2,1)S(1)}, bf16[8,2,128,128]{3,2,1,0:T(8,128)(2,1)S(1)}, u32[]{:S(2)}, u32[]{:S(2)}) collective-permute-start(bf16[8,2,128,128]{3,2,1,0:T(8,128)(2,1)S(1)} %add_convert_fusion.2), channel_id=1, source_target_pairs={{0,504},{1,9},{2,506},{3,11},{4,508},{5,13},{6,510},{7,15},{8,0},{... | collective-permute-start | bytes 1572872 | tf_op jit(solution)/shard_map/ppermute | solution.py:295
  93.9 18.6 %collective-permute-start.7 = (bf16[8,2,128,128]{3,2,1,0:T(8,128)(2,1)S(1)}, bf16[8,2,128,128]{3,2,1,0:T(8,128)(2,1)S(1)}, u32[]{:S(2)}, u32[]{:S(2)}) collective-permute-start(bf16[8,2,128,128]{3,2,1,0:T(8,128)(2,1)S(1)} %add_convert_fusion.1), channel_id=1, source_target_pairs={{0,8},{1,505},{2,10},{3,507},{4,12},{5,509},{6,14},{7,511},{8,16},... | collective-permute-start | bytes 1572872 | tf_op jit(solution)/shard_map/ppermute | solution.py:295

commit v2 on v1

v2 whole, which is shorter than its diff:
```python
import functools

import jax
import jax.numpy as jnp
from jax import lax
from jax.experimental import pallas as pl
from jax.experimental.pallas import tpu as pltpu
from jax.sharding import PartitionSpec as P

HD = 128
SCALE = HD**-0.5
LOG2E = 1.4426950408889634
CHUNK = 128
HALF = 16
HIDDEN = -1e30


def dot(left, right):
    return jnp.dot(left, right, preferred_element_type=jnp.float32)


def fold(value, reduce):
    return reduce(value.reshape(-1, 8, value.shape[-1]), axis=0)


def prepare_kernel(lengths, query, grad_out, query_rows, query_flip, live, live_flip):
    slots = query.shape[1]
    heads = query.shape[2] // HD
    for ref in (query_rows, query_flip, live, live_flip):
        ref[ref.shape[0] - 1] = jnp.zeros_like(ref[0])

    def step(slot, carry):
        for half in range(slots // HALF):
            rows = slice(half * HALF, (half + 1) * HALF)
            cells = [(rows, slice(head * HD, (head + 1) * HD)) for head in range(heads)]
            at = slot * (slots // HALF) + half
            block = jnp.concatenate([query[slot, row, col] for row, col in cells], axis=0)
            query_rows[at] = block
            query_flip[at] = block.T
            row_at = lax.broadcasted_iota(jnp.int32, (HALF, HD), 0) + half * HALF
            block = jnp.concatenate(
                [
                    jnp.where(
                        row_at < lengths[slot], grad_out[slot, row, col].astype(jnp.float32), 0.0
                    ).astype(jnp.bfloat16)
                    for row, col in cells
                ],
                axis=0,
            )
            live[at] = block
            live_flip[at] = block.T
        return carry

    lax.fori_loop(0, query.shape[0], step, 0)


def prepare(lengths, query, grad_out):
    count, slots, width = query.shape
    blocks = count * (slots // HALF) + 1
    rows = HALF * (width // HD)
    vmem = pl.BlockSpec(memory_space=pltpu.VMEM)
    tall = jax.ShapeDtypeStruct((blocks, rows, HD), jnp.bfloat16)
    wide = jax.ShapeDtypeStruct((blocks, HD, rows), jnp.bfloat16)
    return pl.pallas_call(
        prepare_kernel,
        out_shape=[tall, wide, tall, wide],
        in_specs=[pl.BlockSpec(memory_space=pltpu.SMEM), vmem, vmem],
        out_specs=[vmem] * 4,
        compiler_params=pltpu.CompilerParams(vmem_limit_bytes=8 * 2**20),
        cost_estimate=pl.CostEstimate(
            flops=0, bytes_accessed=12 * count * slots * width, transcendentals=0
        ),
    )(lengths, query, grad_out)


def stack(ref, spots, axis):
    return jnp.concatenate([ref[block] for block, _, _, _ in spots], axis=axis)


def first_half(spots, prepared, comp_key, comp_value, prefix, bufs):
    _, query_flip, _, live_flip = prepared
    keys, values, _, slope_buf, exp_buf, _ = bufs
    slots = comp_key.shape[1]
    extent = keys.shape[0]
    for at, (_, slot, _, _) in enumerate(spots):
        keys[prefix + at * slots : prefix + (at + 1) * slots] = comp_key[slot]
        values[prefix + at * slots : prefix + (at + 1) * slots] = comp_value[slot]
    queries = stack(query_flip, spots, 1)
    lanes = queries.shape[1]
    row = lax.broadcasted_iota(jnp.int32, (2 * slots, lanes), 0)
    lane = lax.broadcasted_iota(jnp.int32, (2 * slots, lanes), 1)
    side = lane // (lanes // 2)
    key_at = row % slots
    query_at = lane % HALF + HALF * jnp.where(side == 0, spots[0][2], spots[1][2])
    size = jnp.where(side == 0, spots[0][3], spots[1][3])
    visible = (row // slots == side) & (key_at <= query_at) & (key_at < size)

    spans = [(start, min(start + CHUNK, extent)) for start in range(0, extent, CHUNK)]
    scores = dot(keys[...], queries)
    slope_buf[...] = dot(values[...], stack(live_flip, spots, 1))
    tops, sums = [], []
    for start, end in spans:
        part = scores[start:end]
        if start >= prefix:
            part = jnp.where(visible, part, HIDDEN)
        top = jnp.max(fold(part, jnp.max), axis=0, keepdims=True)
        part = jnp.exp2((part - top) * (SCALE * LOG2E))
        exp_buf[start:end] = part
        tops.append(top)
        sums.append(fold(part, jnp.sum))
    top = functools.reduce(jnp.maximum, tops)
    shares = [jnp.exp2((each - top) * (SCALE * LOG2E)) for each in tops]
    total = sum(part * share for part, share in zip(sums, shares))
    inverse = 1.0 / jnp.sum(total, axis=0, keepdims=True)
    return spans, [share * inverse for share in shares]


def second_half(state, spots, prepared, key_flip, bufs, prefix, dk_sum, dv_sum, dq):
    query_rows, _, live, _ = prepared
    keys, _, weight_buf, slope_buf, exp_buf, prob_buf = bufs
    slots = dk_sum.shape[1]
    spans, shares = state
    delta = 0.0
    for (start, end), share in zip(spans, shares):
        weight = (exp_buf[start:end] * share).astype(jnp.bfloat16)
        weight_buf[start:end] = weight
        delta = delta + fold(weight.astype(jnp.float32) * slope_buf[start:end], jnp.sum)
    delta = jnp.sum(delta, axis=0, keepdims=True)
    value_terms = dot(weight_buf[...], stack(live, spots, 0))
    for (start, end), share in zip(spans, shares):
        part = exp_buf[start:end] * share * (slope_buf[start:end] - delta)
        prob_buf[start:end] = part.astype(jnp.bfloat16)
    key_terms = dot(prob_buf[...], stack(query_rows, spots, 0)) * SCALE
    own_flip = keys[prefix:].astype(jnp.float32).T.astype(jnp.bfloat16)
    flipped = dot(key_flip[...], prob_buf[:prefix]) + dot(own_flip, prob_buf[prefix:])
    query_grad = (flipped * SCALE).T.astype(jnp.bfloat16)
    for at, (_, slot, _, _) in enumerate(spots):
        span = slice(prefix + at * slots, prefix + (at + 1) * slots)
        dv_sum[slot] += value_terms[span]
        dk_sum[slot] += key_terms[span]
    return key_terms[:prefix], value_terms[:prefix], query_grad


def put_query_grad(dq, spots, query_grad):
    half_rows = query_grad.shape[0] // 2
    for at, (block, slot, half, _) in enumerate(spots):

        def put():
            rows = pl.ds(pl.multiple_of(half * HALF, HALF), HALF)
            for head in range(dq.shape[2] // HD):
                start = at * half_rows + head * HALF
                dq[slot, rows, head * HD : (head + 1) * HD] = query_grad[start : start + HALF]

        if at == 0:
            put()
        else:
            pl.when(block < 2 * dq.shape[0])(put)


def near_kernel(code, chained, plan, query_rows, query_flip, live, live_flip, comp_key, comp_value,
                pair, *refs):
    if chained:
        for done, out in zip(refs[:3], refs[4:7]):
            out[...] = done[...]
        refs = refs[3:]
    (term, dq, dk, dv, dk_sum, dv_sum, key_flip, key_sum, value_sum, listed) = refs[:10]
    bufs = (refs[10:16], refs[16:22])
    count, slots = dq.shape[:2]
    prefix = key_sum.shape[0]
    rows = pair.shape[2]
    prepared = (query_rows, query_flip, live, live_flip)

    def size_of(slot):
        return plan[slot] % 64

    found = 0
    for slot in range(count):
        word = plan[slot]
        listed[found] = 2 * slot
        listed[found + 1] = 2 * slot + 1
        blocks = jnp.where(word % 64 > HALF, 2, 1)
        found = found + jnp.where(word // 64 == code, blocks, 0)
    key_sum[...] = jnp.zeros_like(key_sum)
    value_sum[...] = jnp.zeros_like(value_sum)

    @pl.when(found > 0)
    def _():
        dk_sum[...] = jnp.zeros_like(dk_sum)
        dv_sum[...] = jnp.zeros_like(dv_sum)
        for at in range(pair.shape[0]):
            span = slice(at * rows, (at + 1) * rows)
            for keys, values, *_ in bufs:
                keys[span] = pair[at, 0]
                values[span] = pair[at, 1]
            key_flip[:, span] = pair[at, 0].T

    def spots_at(index):
        one = listed[index]
        other = listed[index + 1]
        valid = index + 1 < found
        slot = jnp.where(valid, other // 2, one // 2)
        return (
            (one, one // 2, one % 2, size_of(one // 2)),
            (jnp.where(valid, other, 2 * count), slot, jnp.where(valid, other % 2, 0),
             jnp.where(valid, size_of(slot), 0)),
        )

    def run(starts):
        all_spots = [spots_at(start) for start in starts]
        states = [
            first_half(spots, prepared, comp_key, comp_value, prefix, buf)
            for spots, buf in zip(all_spots, bufs)
        ]
        done = [
            second_half(state, spots, prepared, key_flip, buf, prefix, dk_sum, dv_sum, dq)
            for state, spots, buf in zip(states, all_spots, bufs)
        ]
        key_sum[...] += sum(each[0] for each in done)
        value_sum[...] += sum(each[1] for each in done)
        for spots, each in zip(all_spots, done):
            put_query_grad(dq, spots, each[2])

    pairs = (found + 1) // 2

    def step(at, carry):
        run((4 * at, 4 * at + 2))
        return carry

    lax.fori_loop(0, pairs // 2, step, 0)

    @pl.when(pairs % 2 == 1)
    def _():
        run((2 * pairs - 2,))

    def finish(index, carry):
        block = listed[index]
        slot = block // 2

        @pl.when(block % 2 == 0)
        def _():
            dk[slot] = dk_sum[slot].astype(jnp.bfloat16)
            dv[slot] = dv_sum[slot].astype(jnp.bfloat16)

            @pl.when(size_of(slot) <= HALF)
            def _():
                dq[slot, HALF:] = jnp.zeros_like(dq[slot, HALF:])

        return carry

    lax.fori_loop(0, found, finish, 0)
    for at in range(pair.shape[0]):
        span = slice(at * rows, (at + 1) * rows)
        term[at, 0] = key_sum[span].astype(term.dtype)
        term[at, 1] = value_sum[span].astype(term.dtype)


def near_grads(code, pair, plan, prepared, comp_key, comp_value, chain, shape, kind):
    count, slots, width = shape
    lanes = 2 * HALF * (width // HD)
    prefix = pair.shape[0] * pair.shape[2]
    extent = prefix + 2 * slots
    vmem = pl.BlockSpec(memory_space=pltpu.VMEM)
    narrow = jax.ShapeDtypeStruct(comp_key.shape, jnp.bfloat16)
    operands = [plan, *prepared, comp_key, comp_value, pair]
    if chain is not None:
        operands += list(chain)
    work = 4
    out = pl.pallas_call(
        functools.partial(near_kernel, code, chain is not None),
        out_shape=[
            jax.ShapeDtypeStruct(pair.shape, kind),
            jax.ShapeDtypeStruct(shape, jnp.bfloat16),
            narrow,
            narrow,
        ],
        in_specs=[pl.BlockSpec(memory_space=pltpu.SMEM)] + [vmem] * (len(operands) - 1),
        out_specs=[vmem] * 4,
        scratch_shapes=[
            pltpu.VMEM(comp_key.shape, jnp.float32),
            pltpu.VMEM(comp_key.shape, jnp.float32),
            pltpu.VMEM((HD, prefix), jnp.bfloat16),
            pltpu.VMEM((prefix, HD), jnp.float32),
            pltpu.VMEM((prefix, HD), jnp.float32),
            pltpu.SMEM((2 * count + 4,), jnp.int32),
        ]
        + 2
        * [
            pltpu.VMEM((extent, HD), jnp.bfloat16),
            pltpu.VMEM((extent, HD), jnp.bfloat16),
            pltpu.VMEM((extent, lanes), jnp.bfloat16),
            pltpu.VMEM((extent, lanes), jnp.float32),
            pltpu.VMEM((extent, lanes), jnp.float32),
            pltpu.VMEM((extent, lanes), jnp.bfloat16),
        ],
        compiler_params=pltpu.CompilerParams(vmem_limit_bytes=24 * 2**20),
        cost_estimate=pl.CostEstimate(
            flops=work * 12 * extent * lanes * HD,
            bytes_accessed=work * 10 * slots * width,
            transcendentals=work * extent * lanes,
        ),
    )(*operands)
    return out[0], out[1:]


SMALL = pltpu.CompilerParams(vmem_limit_bytes=4 * 2**20)


def split_kernel(key, value, pair):
    for head in range(pair.shape[0]):
        columns = slice(head * HD, (head + 1) * HD)
        pair[head, 0] = key[:, columns]
        pair[head, 1] = value[:, columns]


def split_heads(key, value, shards):
    return pl.pallas_call(
        split_kernel,
        out_shape=jax.ShapeDtypeStruct((shards, 2, key.shape[0], HD), key.dtype),
        compiler_params=SMALL,
    )(key, value)


def join_kernel(pair, key, value):
    for head in range(pair.shape[0]):
        columns = slice(head * HD, (head + 1) * HD)
        key[:, columns] = pair[head, 0]
        value[:, columns] = pair[head, 1]


def join_heads(pair):
    shards, _, rows, _ = pair.shape
    whole = jax.ShapeDtypeStruct((rows, shards * HD), pair.dtype)
    return pl.pallas_call(join_kernel, out_shape=[whole, whole], compiler_params=SMALL)(pair)


def shifted(value, steps):
    size, shards = lax.axis_size("dp"), lax.axis_size("mp")
    pairs = []
    for at in range(size):
        for shard in range(shards):
            target = (at + (steps if shard % 2 == 0 else -steps)) % size
            pairs.append((at * shards + shard, target * shards + shard))
    return lax.ppermute(value, ("dp", "mp"), pairs)


def per_device(
    query, comp_key, comp_value, prefix_key, prefix_value, grad_out, owner, group, lengths
):
    axis_count = lax.axis_size("dp")
    shards = lax.axis_size("mp")
    position = lax.axis_index("dp")
    prompt_ids = jnp.arange(owner.shape[0], dtype=jnp.int32)
    holder_of = jnp.sum(jnp.where(group[:, None] == prompt_ids[None, :], owner[None, :], 0), axis=1)
    near = ((holder_of - position + 2 + axis_count) % axis_count).astype(jnp.int32)
    near = jnp.where(lax.axis_index("mp") % 2 == 0, near, 4 - near)

    pair = split_heads(prefix_key[0], prefix_value[0], shards)
    own = lax.all_to_all(pair, "mp", split_axis=0, concat_axis=0, tiled=True)
    low_one = shifted(own, 1)
    up_one = shifted(own, -1)
    low_two = shifted(low_one, 1)
    up_two = shifted(up_one, -1)

    plan = near * 64 + lengths
    prepared = prepare(lengths, query, grad_out)
    rest = (comp_key, comp_value)
    own_term, chain = near_grads(2, own, plan, prepared, *rest, None, query.shape, jnp.float32)
    low_two_term, chain = near_grads(0, low_two, plan, prepared, *rest, chain, query.shape, jnp.bfloat16)
    up_two_term, chain = near_grads(4, up_two, plan, prepared, *rest, chain, query.shape, jnp.bfloat16)
    low_term, chain = near_grads(1, low_one, plan, prepared, *rest, chain, query.shape, jnp.float32)
    up_term, chain = near_grads(3, up_one, plan, prepared, *rest, chain, query.shape, jnp.float32)
    low_back = shifted(low_two_term, -1).astype(jnp.float32)
    up_back = shifted(up_two_term, 1).astype(jnp.float32)
    low_back = shifted((low_term + low_back).astype(jnp.bfloat16), -1).astype(jnp.float32)
    up_back = shifted((up_term + up_back).astype(jnp.bfloat16), 1).astype(jnp.float32)
    gathered = (own_term + low_back + up_back).astype(jnp.bfloat16)
    back = lax.all_to_all(gathered, "mp", split_axis=0, concat_axis=0, tiled=True)
    key_back, value_back = join_heads(back)
    return chain[0], chain[1], chain[2], key_back[None], value_back[None]


def solution(mesh):
    return jax.shard_map(
        per_device,
        mesh=mesh,
        in_specs=(
            P("dp", None, "mp"),
            P("dp", None, "mp"),
            P("dp", None, "mp"),
            P("dp", "mp", None),
            P("dp", "mp", None),
            P("dp", None, "mp"),
            P(),
            P("dp"),
            P("dp"),
        ),
        out_specs=(
            P("dp", None, "mp"),
            P("dp", None, "mp"),
            P("dp", None, "mp"),
            P("dp", "mp", None),
            P("dp", "mp", None),
        ),
        check_vma=False,
    )
```

time: 131 us -> 123 us (0.939)
  Pallas kernels: 32.2 us -> 27.3 us
  waiting for transfers between devices: 18.9 us -> 16 us
  blocking collectives: 35.7 us -> 37.1 us
    pallas_call x5, Pallas kernels: 28.2 us -> 24.2 us  [near_grads(): pl.pallas_call(functools.partial(near_kernel, code, chain is not None), o...]
    ppermute x8, waiting for transfers between devices: 18.9 us -> 16 us  [shifted(): return lax.ppermute(value, ('dp', 'mp'), pairs)]
    pallas_call x1, Pallas kernels: 2.06 us -> 0.09 us  [split_heads(): pl.pallas_call(split_kernel, out_shape=jax.ShapeDtypeStruct((shards, 2, k...]
    all_to_all x1, blocking collectives: 16 us -> 17.7 us  [per_device(): lax.all_to_all(gathered, 'mp', split_axis=0, concat_axis=0, tiled=True)]
    pallas_call x1 -> x2, Pallas kernels: 1.97 us -> 2.98 us  [the longest x1 2.04 us: prepare(): pl.pallas_call(prepare_kernel, out_shape=[tall, wide, tall, wide], in_spe...]
  transfers between devices with their start and end apart: 8 -> 8, of which waited for: 4 -> 3; matrix products, arithmetic and copies ran while one was open for 0% -> 0% of each run, Pallas kernels for 22% -> 21%
where the time goes in v2:
time: 123 us
  starting transfers between devices  38.8 us (32%)
  blocking collectives  37.1 us (30%)
  Pallas kernels  27.3 us (22%)
  waiting for transfers between devices  16 us (13%)
  local copies, waits for them, and re-layouts  2.07 us (2%)
    ppermute x8, starting transfers between devices, shifted(): return lax.ppermute(value, ('dp', 'mp'), pairs)  38.8 us
    pallas_call x5, Pallas kernels, near_grads(): pl.pallas_call(functools.partial(near_kernel, code, chain is not None), o...  24.2 us
    all_to_all x1, blocking collectives, per_device(): own = lax.all_to_all(pair, 'mp', split_axis=0, concat_axis=0, tiled=True)  19.3 us
    all_to_all x1, blocking collectives, per_device(): lax.all_to_all(gathered, 'mp', split_axis=0, concat_axis=0, tiled=True)  17.7 us
    ppermute x8, waiting for transfers between devices, shifted(): return lax.ppermute(value, ('dp', 'mp'), pairs)  16 us
  transfers between devices with their start and end apart: 8, of which 3 were waited for; matrix products, arithmetic and copies ran while one was open for 0% of the time, Pallas kernels for 21%

profile of v2, /device:TPU:1, one launch (start us, length us, event | category | flops | bytes accessed | tf_op | source)
XLA Modules:
  0.0 122.9 jit_solution(18218456512382719520)
XLA Ops:
  0.6 0.0 copy-start.3
  0.6 0.0 copy-start.2
  0.7 0.0 copy-start.4
  0.7 1.1 copy-done.4
  1.8 0.0 copy-start.5
  1.8 0.9 copy-done.5
  2.7 0.0 copy-start.6
  2.7 0.1 shard_map.129
  2.8 19.3 %all_to_all.10.pair = bf16[8,2,128,128]{3,2,1,0:T(8,128)(2,1)} all-to-all(bf16[8,2,128,128]{3,2,1,0:T(8,128)(2,1)S(1)} %shard_map.129), channel_id=1, replica_groups=mesh['dp'=64,'mp'=8] {'mp'}, dimensions={0} | all-to-all | bytes 1048576 | tf_op jit(solution)/shard_map/all_to_all | solution.py:358
  22.1 0.0 copy-start.7
  22.1 0.0 copy-start.8
  22.1 0.0 copy-start
  22.1 0.0 copy-start.1
  22.1 9.4 %collective-permute-start.1 = (bf16[8,2,128,128]{3,2,1,0:T(8,128)(2,1)}, bf16[8,2,128,128]{3,2,1,0:T(8,128)(2,1)S(1)}, u32[]{:S(2)}, u32[]{:S(2)}) collective-permute-start(bf16[8,2,128,128]{3,2,1,0:T(8,128)(2,1)} %all_to_all.10.pair), channel_id=1, source_target_pairs={{0,8},{1,505},{2,10},{3,507},{4,12},{5,509},{6,14},{7,511},{8,16},... | collective-permute-start | bytes 1572872 | tf_op jit(solution)/shard_map/ppermute | solution.py:343
  31.5 1.9 %collective-permute-start = (bf16[8,2,128,128]{3,2,1,0:T(8,128)(2,1)}, bf16[8,2,128,128]{3,2,1,0:T(8,128)(2,1)S(1)}, u32[]{:S(2)}, u32[]{:S(2)}) collective-permute-start(bf16[8,2,128,128]{3,2,1,0:T(8,128)(2,1)} %all_to_all.10.pair), channel_id=1, source_target_pairs={{0,504},{1,9},{2,506},{3,11},{4,508},{5,13},{6,510},{7,15},{8,0},{... | collective-permute-start | bytes 1572872 | tf_op jit(solution)/shard_map/ppermute | solution.py:343
  33.4 6.6 %collective-permute-done.1.pair = bf16[8,2,128,128]{3,2,1,0:T(8,128)(2,1)S(1)} collective-permute-done((bf16[8,2,128,128]{3,2,1,0:T(8,128)(2,1)}, bf16[8,2,128,128]{3,2,1,0:T(8,128)(2,1)S(1)}, u32[]{:S(2)}, u32[]{:S(2)}) %collective-permute-start.1) | collective-permute-done | bytes 524320 | tf_op jit(solution)/shard_map/ppermute | solution.py:343
  40.0 7.3 %collective-permute-start.3 = (bf16[8,2,128,128]{3,2,1,0:T(8,128)(2,1)S(1)}, bf16[8,2,128,128]{3,2,1,0:T(8,128)(2,1)}, u32[]{:S(2)}, u32[]{:S(2)}) collective-permute-start(bf16[8,2,128,128]{3,2,1,0:T(8,128)(2,1)S(1)} %collective-permute-done.1.pair), channel_id=1, source_target_pairs={{0,8},{1,505},{2,10},{3,507},{4,12},{5,509},{6,14},{7,511},{8,16},... | collective-permute-start | bytes 1572872 | tf_op jit(solution)/shard_map/ppermute | solution.py:343
  47.4 0.0 copy-done.3
  47.4 0.0 copy-done.2
  47.4 0.0 copy-done.6
  47.4 2.0 %shard_map.128 = (bf16[33,128,128]{2,1,0:T(8,128)(2,1)S(1)}, bf16[33,128,128]{2,1,0:T(8,128)(2,1)S(1)}, bf16[33,128,128]{2,1,0:T(8,128)(2,1)S(1)}, bf16[33,128,128]{2,1,0:T(8,128)(2,1)S(1)}) custom-call(s32[16]{0:T(128)S(1)} %copy-done.6, bf16[16,32,1024]{2,1,0:T(8,128)(2,1)S(1)} %copy-done.2, bf16[16,32,1024]{2,1,0:T(8,128)(2,1)S(1)} %copy-done.3), custom_call_target="tpu_custom_call" | custom-call | bytes 6291456 | tf_op jit(solution)/shard_map/pallas_call | solution.py:64
  49.5 0.0 copy-done.7
  49.5 0.0 copy-done.8
  49.5 0.2 select_reduce_fusion
  49.7 0.0 collective-permute-done.pair
  49.7 1.9 %collective-permute-start.2 = (bf16[8,2,128,128]{3,2,1,0:T(8,128)(2,1)S(1)}, bf16[8,2,128,128]{3,2,1,0:T(8,128)(2,1)S(1)}, u32[]{:S(2)}, u32[]{:S(2)}) collective-permute-start(bf16[8,2,128,128]{3,2,1,0:T(8,128)(2,1)S(1)} %collective-permute-done.pair), channel_id=1, source_target_pairs={{0,504},{1,9},{2,506},{3,11},{4,508},{5,13},{6,510},{7,15},{8,0},{... | collective-permute-start | bytes 1572872 | tf_op jit(solution)/shard_map/ppermute | solution.py:343
  51.6 0.0 copy-done
  51.6 0.0 copy-done.1
  51.6 12.2 %shard_map.130 = (f32[8,2,128,128]{3,2,1,0:T(8,128)S(1)}, bf16[16,32,1024]{2,1,0:T(8,128)(2,1)S(1)}, bf16[16,32,128]{2,1,0:T(8,128)(2,1)S(1)}, bf16[16,32,128]{2,1,0:T(8,128)(2,1)S(1)}) custom-call(s32[16]{0:T(128)S(1)} %multiply_add_fusion.plan, bf16[33,128,128]{2,1,0:T(8,128)(2,1)S(1)} %get-tuple-element.31.query_rows, ...), custom_call_target="tpu_custom_call" | custom-call | flops 1711276032 | bytes 1310720 | tf_op jit(solution)/shard_map/pallas_call | solution.py:268
  63.9 0.0 collective-permute-done.3.pair
  63.9 2.8 %shard_map.131 = (bf16[8,2,128,128]{3,2,1,0:T(8,128)(2,1)S(1)}, bf16[16,32,1024]{2,1,0:T(8,128)(2,1)S(1)}, bf16[16,32,128]{2,1,0:T(8,128)(2,1)S(1)}, bf16[16,32,128]{2,1,0:T(8,128)(2,1)S(1)}) custom-call(s32[16]{0:T(128)S(1)} %multiply_add_fusion.plan, bf16[33,128,128]{2,1,0:T(8,128)(2,1)S(1)} %get-tuple-element.31.query_rows, ...), custom_call_target="tpu_custom_call" | custom-call | flops 1711276032 | bytes 1310720 | tf_op jit(solution)/shard_map/pallas_call | solution.py:268
  66.7 1.9 %collective-permute-start.4 = (bf16[8,2,128,128]{3,2,1,0:T(8,128)(2,1)S(1)}, bf16[8,2,128,128]{3,2,1,0:T(8,128)(2,1)S(1)}, u32[]{:S(2)}, u32[]{:S(2)}) collective-permute-start(bf16[8,2,128,128]{3,2,1,0:T(8,128)(2,1)S(1)} %get-tuple-element.52), channel_id=1, source_target_pairs={{0,504},{1,9},{2,506},{3,11},{4,508},{5,13},{6,510},{7,15},{8,0},{... | collective-permute-start | bytes 1572872 | tf_op jit(solution)/shard_map/ppermute | solution.py:343
  68.7 0.0 collective-permute-done.2.pair
  68.7 3.5 %shard_map.132 = (bf16[8,2,128,128]{3,2,1,0:T(8,128)(2,1)S(1)}, bf16[16,32,1024]{2,1,0:T(8,128)(2,1)S(1)}, bf16[16,32,128]{2,1,0:T(8,128)(2,1)S(1)}, bf16[16,32,128]{2,1,0:T(8,128)(2,1)S(1)}) custom-call(s32[16]{0:T(128)S(1)} %multiply_add_fusion.plan, bf16[33,128,128]{2,1,0:T(8,128)(2,1)S(1)} %get-tuple-element.31.query_rows, ...), custom_call_target="tpu_custom_call" | custom-call | flops 1711276032 | bytes 1310720 | tf_op jit(solution)/shard_map/pallas_call | solution.py:268
  72.2 5.7 %collective-permute-start.6 = (bf16[8,2,128,128]{3,2,1,0:T(8,128)(2,1)S(1)}, bf16[8,2,128,128]{3,2,1,0:T(8,128)(2,1)S(1)}, u32[]{:S(2)}, u32[]{:S(2)}) collective-permute-start(bf16[8,2,128,128]{3,2,1,0:T(8,128)(2,1)S(1)} %get-tuple-element.54), channel_id=1, source_target_pairs={{0,8},{1,505},{2,10},{3,507},{4,12},{5,509},{6,14},{7,511},{8,16},... | collective-permute-start | bytes 1572872 | tf_op jit(solution)/shard_map/ppermute | solution.py:343
  77.9 2.4 %shard_map.133 = (f32[8,2,128,128]{3,2,1,0:T(8,128)S(1)}, bf16[16,32,1024]{2,1,0:T(8,128)(2,1)S(1)}, bf16[16,32,128]{2,1,0:T(8,128)(2,1)S(1)}, bf16[16,32,128]{2,1,0:T(8,128)(2,1)S(1)}) custom-call(s32[16]{0:T(128)S(1)} %multiply_add_fusion.plan, bf16[33,128,128]{2,1,0:T(8,128)(2,1)S(1)} %get-tuple-element.31.query_rows, ...), custom_call_target="tpu_custom_call" | custom-call | flops 1711276032 | bytes 1310720 | tf_op jit(solution)/shard_map/pallas_call | solution.py:268
  80.3 3.3 %shard_map.134 = (f32[8,2,128,128]{3,2,1,0:T(8,128)S(1)}, bf16[16,32,1024]{2,1,0:T(8,128)(2,1)}, bf16[16,32,128]{2,1,0:T(8,128)(2,1)}, bf16[16,32,128]{2,1,0:T(8,128)(2,1)}) custom-call(s32[16]{0:T(128)S(1)} %multiply_add_fusion.plan, bf16[33,128,128]{2,1,0:T(8,128)(2,1)S(1)} %get-tuple-element.31.query_rows, ...), custom_call_target="tpu_custom_call" | custom-call | flops 1711276032 | bytes 1310720 | tf_op jit(solution)/shard_map/pallas_call | solution.py:268
  83.6 0.0 collective-permute-done.4
  83.6 0.1 add_convert_fusion.2
  83.7 1.9 %collective-permute-start.5 = (bf16[8,2,128,128]{3,2,1,0:T(8,128)(2,1)S(1)}, bf16[8,2,128,128]{3,2,1,0:T(8,128)(2,1)S(1)}, u32[]{:S(2)}, u32[]{:S(2)}) collective-permute-start(bf16[8,2,128,128]{3,2,1,0:T(8,128)(2,1)S(1)} %add_convert_fusion.2), channel_id=1, source_target_pairs={{0,504},{1,9},{2,506},{3,11},{4,508},{5,13},{6,510},{7,15},{8,0},{... | collective-permute-start | bytes 1572872 | tf_op jit(solution)/shard_map/ppermute | solution.py:343
  85.7 0.0 collective-permute-done.6
  85.7 0.2 add_convert_fusion.1
  85.8 8.7 %collective-permute-start.7 = (bf16[8,2,128,128]{3,2,1,0:T(8,128)(2,1)S(1)}, bf16[8,2,128,128]{3,2,1,0:T(8,128)(2,1)S(1)}, u32[]{:S(2)}, u32[]{:S(2)}) collective-permute-start(bf16[8,2,128,128]{3,2,1,0:T(8,128)(2,1)S(1)} %add_convert_fusion.1), channel_id=1, source_target_pairs={{0,8},{1,505},{2,10},{3,507},{4,12},{5,509},{6,14},{7,511},{8,16},... | collective-permute-start | bytes 1572872 | tf_op jit(solution)/shard_map/ppermute | solution.py:343
  94.6 4.4 %collective-permute-done.5 = bf16[8,2,128,128]{3,2,1,0:T(8,128)(2,1)S(1)} collective-permute-done((bf16[8,2,128,128]{3,2,1,0:T(8,128)(2,1)S(1)}, bf16[8,2,128,128]{3,2,1,0:T(8,128)(2,1)S(1)}, u32[]{:S(2)}, u32[]{:S(2)}) %collective-permute-start.5) | collective-permute-done | bytes 524320 | tf_op jit(solution)/shard_map/ppermute | solution.py:343
  99.0 5.0 %collective-permute-done.7 = bf16[8,2,128,128]{3,2,1,0:T(8,128)(2,1)S(1)} collective-permute-done((bf16[8,2,128,128]{3,2,1,0:T(8,128)(2,1)S(1)}, bf16[8,2,128,128]{3,2,1,0:T(8,128)(2,1)S(1)}, u32[]{:S(2)}, u32[]{:S(2)}) %collective-permute-start.7) | collective-permute-done | bytes 524320 | tf_op jit(solution)/shard_map/ppermute | solution.py:343
  104.0 0.2 add_convert_fusion
  104.2 17.7 %all_to_all.11.pair = bf16[8,2,128,128]{3,2,1,0:T(8,128)(2,1)S(1)} all-to-all(bf16[8,2,128,128]{3,2,1,0:T(8,128)(2,1)S(1)} %add_convert_fusion), channel_id=1, replica_groups=mesh['dp'=64,'mp'=8] {'mp'}, dimensions={0} | all-to-all | bytes 1048576 | tf_op jit(solution)/shard_map/all_to_all | solution.py:377
  121.9 0.9 shard_map.135
  (1 shorter events, 0.0 us)
Async XLA Ops:
  0.6 46.7 %copy-start.3 = (bf16[16,32,1024]{2,1,0:T(8,128)(2,1)S(1)}, bf16[16,32,1024]{2,1,0:T(8,128)(2,1)}, u32[]{:S(2)}) copy-start(bf16[16,32,1024]{2,1,0:T(8,128)(2,1)} %grad_out.1) | copy-start | bytes 3145732
  0.6 46.7 %copy-start.2 = (bf16[16,32,1024]{2,1,0:T(8,128)(2,1)S(1)}, bf16[16,32,1024]{2,1,0:T(8,128)(2,1)}, u32[]{:S(2)}) copy-start(bf16[16,32,1024]{2,1,0:T(8,128)(2,1)} %query.1) | copy-start | bytes 3145732
  0.7 1.1 copy-start.4
  1.8 0.9 copy-start.5
  2.7 44.7 %copy-start.6 = (s32[16]{0:T(128)S(1)}, s32[16]{0:T(128)}, u32[]{:S(2)}) copy-start(s32[16]{0:T(128)} %lengths.1) | copy-start | bytes 196
  22.1 27.3 %copy-start.7 = (s32[64]{0:T(128)S(1)}, s32[64]{0:T(128)}, u32[]{:S(2)}) copy-start(s32[64]{0:T(128)} %param.15) | copy-start | bytes 772
  22.1 27.4 %copy-start.8 = (s32[16]{0:T(128)S(1)}, s32[16]{0:T(128)}, u32[]{:S(2)}) copy-start(s32[16]{0:T(128)} %param.16) | copy-start | bytes 196
  22.1 29.5 %copy-start = (bf16[16,32,128]{2,1,0:T(8,128)(2,1)S(1)}, bf16[16,32,128]{2,1,0:T(8,128)(2,1)}, u32[]{:S(2)}) copy-start(bf16[16,32,128]{2,1,0:T(8,128)(2,1)} %comp_key.9) | copy-start | bytes 393220
  22.1 29.5 %copy-start.1 = (bf16[16,32,128]{2,1,0:T(8,128)(2,1)S(1)}, bf16[16,32,128]{2,1,0:T(8,128)(2,1)}, u32[]{:S(2)}) copy-start(bf16[16,32,128]{2,1,0:T(8,128)(2,1)} %comp_value.9) | copy-start | bytes 393220
  22.1 17.9 %collective-permute-start.1 = (bf16[8,2,128,128]{3,2,1,0:T(8,128)(2,1)}, bf16[8,2,128,128]{3,2,1,0:T(8,128)(2,1)S(1)}, u32[]{:S(2)}, u32[]{:S(2)}) collective-permute-start(bf16[8,2,128,128]{3,2,1,0:T(8,128)(2,1)} %all_to_all.10.pair), channel_id=1, source_target_pairs={{0,8},{1,505},{2,10},{3,507},{4,12},{5,509},{6,14},{7,511},{8,16},... | collective-permute-start | bytes 1572872 | tf_op jit(solution)/shard_map/ppermute | solution.py:343
  31.5 18.2 %collective-permute-start = (bf16[8,2,128,128]{3,2,1,0:T(8,128)(2,1)}, bf16[8,2,128,128]{3,2,1,0:T(8,128)(2,1)S(1)}, u32[]{:S(2)}, u32[]{:S(2)}) collective-permute-start(bf16[8,2,128,128]{3,2,1,0:T(8,128)(2,1)} %all_to_all.10.pair), channel_id=1, source_target_pairs={{0,504},{1,9},{2,506},{3,11},{4,508},{5,13},{6,510},{7,15},{8,0},{... | collective-permute-start | bytes 1572872 | tf_op jit(solution)/shard_map/ppermute | solution.py:343
  40.0 23.8 %collective-permute-start.3 = (bf16[8,2,128,128]{3,2,1,0:T(8,128)(2,1)S(1)}, bf16[8,2,128,128]{3,2,1,0:T(8,128)(2,1)}, u32[]{:S(2)}, u32[]{:S(2)}) collective-permute-start(bf16[8,2,128,128]{3,2,1,0:T(8,128)(2,1)S(1)} %collective-permute-done.1.pair), channel_id=1, source_target_pairs={{0,8},{1,505},{2,10},{3,507},{4,12},{5,509},{6,14},{7,511},{8,16},... | collective-permute-start | bytes 1572872 | tf_op jit(solution)/shard_map/ppermute | solution.py:343
  49.7 19.0 %collective-permute-start.2 = (bf16[8,2,128,128]{3,2,1,0:T(8,128)(2,1)S(1)}, bf16[8,2,128,128]{3,2,1,0:T(8,128)(2,1)S(1)}, u32[]{:S(2)}, u32[]{:S(2)}) collective-permute-start(bf16[8,2,128,128]{3,2,1,0:T(8,128)(2,1)S(1)} %collective-permute-done.pair), channel_id=1, source_target_pairs={{0,504},{1,9},{2,506},{3,11},{4,508},{5,13},{6,510},{7,15},{8,0},{... | collective-permute-start | bytes 1572872 | tf_op jit(solution)/shard_map/ppermute | solution.py:343
  66.7 16.9 %collective-permute-start.4 = (bf16[8,2,128,128]{3,2,1,0:T(8,128)(2,1)S(1)}, bf16[8,2,128,128]{3,2,1,0:T(8,128)(2,1)S(1)}, u32[]{:S(2)}, u32[]{:S(2)}) collective-permute-start(bf16[8,2,128,128]{3,2,1,0:T(8,128)(2,1)S(1)} %get-tuple-element.52), channel_id=1, source_target_pairs={{0,504},{1,9},{2,506},{3,11},{4,508},{5,13},{6,510},{7,15},{8,0},{... | collective-permute-start | bytes 1572872 | tf_op jit(solution)/shard_map/ppermute | solution.py:343
  72.2 13.5 %collective-permute-start.6 = (bf16[8,2,128,128]{3,2,1,0:T(8,128)(2,1)S(1)}, bf16[8,2,128,128]{3,2,1,0:T(8,128)(2,1)S(1)}, u32[]{:S(2)}, u32[]{:S(2)}) collective-permute-start(bf16[8,2,128,128]{3,2,1,0:T(8,128)(2,1)S(1)} %get-tuple-element.54), channel_id=1, source_target_pairs={{0,8},{1,505},{2,10},{3,507},{4,12},{5,509},{6,14},{7,511},{8,16},... | collective-permute-start | bytes 1572872 | tf_op jit(solution)/shard_map/ppermute | solution.py:343
  83.7 15.3 %collective-permute-start.5 = (bf16[8,2,128,128]{3,2,1,0:T(8,128)(2,1)S(1)}, bf16[8,2,128,128]{3,2,1,0:T(8,128)(2,1)S(1)}, u32[]{:S(2)}, u32[]{:S(2)}) collective-permute-start(bf16[8,2,128,128]{3,2,1,0:T(8,128)(2,1)S(1)} %add_convert_fusion.2), channel_id=1, source_target_pairs={{0,504},{1,9},{2,506},{3,11},{4,508},{5,13},{6,510},{7,15},{8,0},{... | collective-permute-start | bytes 1572872 | tf_op jit(solution)/shard_map/ppermute | solution.py:343
  85.8 18.1 %collective-permute-start.7 = (bf16[8,2,128,128]{3,2,1,0:T(8,128)(2,1)S(1)}, bf16[8,2,128,128]{3,2,1,0:T(8,128)(2,1)S(1)}, u32[]{:S(2)}, u32[]{:S(2)}) collective-permute-start(bf16[8,2,128,128]{3,2,1,0:T(8,128)(2,1)S(1)} %add_convert_fusion.1), channel_id=1, source_target_pairs={{0,8},{1,505},{2,10},{3,507},{4,12},{5,509},{6,14},{7,511},{8,16},... | collective-permute-start | bytes 1572872 | tf_op jit(solution)/shard_map/ppermute | solution.py:343

commit v3 on v2

--- a/solution.py
+++ b/solution.py
@@ -358,21 +358,28 @@
     own = lax.all_to_all(pair, "mp", split_axis=0, concat_axis=0, tiled=True)
     low_one = shifted(own, 1)
     up_one = shifted(own, -1)
+    plan = near * 64 + lengths
+    prepared = prepare(lengths, query, grad_out)
+    low_one, prepared = lax.optimization_barrier((low_one, prepared))
     low_two = shifted(low_one, 1)
     up_two = shifted(up_one, -1)
-
-    plan = near * 64 + lengths
-    prepared = prepare(lengths, query, grad_out)
-    rest = (comp_key, comp_value)
-    own_term, chain = near_grads(2, own, plan, prepared, *rest, None, query.shape, jnp.float32)
-    low_two_term, chain = near_grads(0, low_two, plan, prepared, *rest, chain, query.shape, jnp.bfloat16)
-    up_two_term, chain = near_grads(4, up_two, plan, prepared, *rest, chain, query.shape, jnp.bfloat16)
-    low_term, chain = near_grads(1, low_one, plan, prepared, *rest, chain, query.shape, jnp.float32)
-    up_term, chain = near_grads(3, up_one, plan, prepared, *rest, chain, query.shape, jnp.float32)
+    low_near, _ = lax.optimization_barrier((low_one, up_one))
+
+    def grads(code, pair, chain, kind):
+        return near_grads(code, pair, plan, prepared, comp_key, comp_value, chain, query.shape, kind)
+
+    low_term, chain = grads(1, low_near, None, jnp.float32)
+    low_two_term, chain = grads(0, low_two, chain, jnp.bfloat16)
+    up_two_term, chain = grads(4, up_two, chain, jnp.bfloat16)
     low_back = shifted(low_two_term, -1).astype(jnp.float32)
     up_back = shifted(up_two_term, 1).astype(jnp.float32)
-    low_back = shifted((low_term + low_back).astype(jnp.bfloat16), -1).astype(jnp.float32)
-    up_back = shifted((up_term + up_back).astype(jnp.bfloat16), 1).astype(jnp.float32)
+    up_term, chain = grads(3, up_one, chain, jnp.float32)
+    low_sum = (low_term + low_back).astype(jnp.bfloat16)
+    up_sum = (up_term + up_back).astype(jnp.bfloat16)
+    up_sum, chain = lax.optimization_barrier((up_sum, chain))
+    low_back = shifted(low_sum, -1).astype(jnp.float32)
+    up_back = shifted(up_sum, 1).astype(jnp.float32)
+    own_term, chain = grads(2, own, chain, jnp.float32)
     gathered = (own_term + low_back + up_back).astype(jnp.bfloat16)
     back = lax.all_to_all(gathered, "mp", split_axis=0, concat_axis=0, tiled=True)
     key_back, value_back = join_heads(back)

time: 123 us -> 121 us (0.984)
  the two profiles are of different devices: /device:TPU:1 before, /device:TPU:6 now
where the time goes in v3:
time: 121 us; the launch traced here: 120 us
  starting transfers between devices  40.2 us (33%)
  blocking collectives  27.6 us (23%)
  Pallas kernels  25.6 us (21%)
  waiting for transfers between devices  21 us (17%)
  local copies, waits for them, and re-layouts  4.3 us (4%)
    ppermute x8, starting transfers between devices, shifted(): return lax.ppermute(value, ('dp', 'mp'), pairs)  40.2 us
    pallas_call x5, Pallas kernels, near_grads(): pl.pallas_call(functools.partial(near_kernel, code, chain is not None), o...  22.6 us
    ppermute x8, waiting for transfers between devices, shifted(): return lax.ppermute(value, ('dp', 'mp'), pairs)  21 us
    all_to_all x1, blocking collectives, per_device(): own = lax.all_to_all(pair, 'mp', split_axis=0, concat_axis=0, tiled=True)  14.8 us
    all_to_all x1, blocking collectives, per_device(): lax.all_to_all(gathered, 'mp', split_axis=0, concat_axis=0, tiled=True)  12.8 us
    unnamed x22, local copies, waits for them, and re-layouts  4.3 us
  transfers between devices with their start and end apart: 8, of which 5 were waited for; matrix products, arithmetic and copies ran while one was open for 0% of the time, Pallas kernels for 20%

profile of v3, /device:TPU:6, one launch (start us, length us, event | category | flops | bytes accessed | tf_op | source)
XLA Modules:
  0.0 120.3 jit_solution(12688055809808053433)
XLA Ops:
  0.6 0.0 copy-start.5
  0.6 0.0 copy-start.4
  0.7 0.0 copy-start.6
  0.7 1.1 copy-done.6
  1.8 0.0 copy-start.7
  1.8 0.9 copy-done.7
  2.7 0.0 copy-start.8
  2.7 0.1 shard_map.128
  2.8 14.8 %all_to_all.10.pair = bf16[8,2,128,128]{3,2,1,0:T(8,128)(2,1)} all-to-all(bf16[8,2,128,128]{3,2,1,0:T(8,128)(2,1)S(1)} %shard_map.128), channel_id=1, replica_groups=mesh['dp'=64,'mp'=8] {'mp'}, dimensions={0} | all-to-all | bytes 1048576 | tf_op jit(solution)/shard_map/all_to_all | solution.py:358
  17.6 0.0 copy-start.9
  17.6 0.0 copy-start.10
  17.6 0.0 copy-start.2
  17.6 0.0 copy-start.3
  17.6 4.0 %collective-permute-start = (bf16[8,2,128,128]{3,2,1,0:T(8,128)(2,1)}, bf16[8,2,128,128]{3,2,1,0:T(8,128)(2,1)}, u32[]{:S(2)}, u32[]{:S(2)}) collective-permute-start(bf16[8,2,128,128]{3,2,1,0:T(8,128)(2,1)} %all_to_all.10.pair), channel_id=1, source_target_pairs={{0,8},{1,505},{2,10},{3,507},{4,12},{5,509},{6,14},{7,511},{8,16},... | collective-permute-start | bytes 1572872 | tf_op jit(solution)/shard_map/ppermute | solution.py:343
  21.5 9.8 %collective-permute-start.1 = (bf16[8,2,128,128]{3,2,1,0:T(8,128)(2,1)}, bf16[8,2,128,128]{3,2,1,0:T(8,128)(2,1)}, u32[]{:S(2)}, u32[]{:S(2)}) collective-permute-start(bf16[8,2,128,128]{3,2,1,0:T(8,128)(2,1)} %all_to_all.10.pair), channel_id=1, source_target_pairs={{0,504},{1,9},{2,506},{3,11},{4,508},{5,13},{6,510},{7,15},{8,0},{... | collective-permute-start | bytes 1572872 | tf_op jit(solution)/shard_map/ppermute | solution.py:343
  31.3 0.0 copy-done.5
  31.3 0.0 copy-done.4
  31.3 0.0 copy-done.8
  31.3 2.0 %shard_map.129 = (bf16[33,128,128]{2,1,0:T(8,128)(2,1)S(1)}, bf16[33,128,128]{2,1,0:T(8,128)(2,1)S(1)}, bf16[33,128,128]{2,1,0:T(8,128)(2,1)S(1)}, bf16[33,128,128]{2,1,0:T(8,128)(2,1)S(1)}) custom-call(s32[16]{0:T(128)S(1)} %copy-done.8, bf16[16,32,1024]{2,1,0:T(8,128)(2,1)S(1)} %copy-done.4, bf16[16,32,1024]{2,1,0:T(8,128)(2,1)S(1)} %copy-done.5), custom_call_target="tpu_custom_call" | custom-call | bytes 6291456 | tf_op jit(solution)/shard_map/pallas_call | solution.py:64
  33.4 0.0 copy-start
  33.4 1.0 copy-done
  34.4 3.7 %collective-permute-done.pair = bf16[8,2,128,128]{3,2,1,0:T(8,128)(2,1)} collective-permute-done((bf16[8,2,128,128]{3,2,1,0:T(8,128)(2,1)}, bf16[8,2,128,128]{3,2,1,0:T(8,128)(2,1)}, u32[]{:S(2)}, u32[]{:S(2)}) %collective-permute-start) | collective-permute-done | bytes 524320 | tf_op jit(solution)/shard_map/ppermute | solution.py:343
  38.1 1.9 %collective-permute-start.3 = (bf16[8,2,128,128]{3,2,1,0:T(8,128)(2,1)}, bf16[8,2,128,128]{3,2,1,0:T(8,128)(2,1)}, u32[]{:S(2)}, u32[]{:S(2)}) collective-permute-start(bf16[8,2,128,128]{3,2,1,0:T(8,128)(2,1)} %collective-permute-done.pair), channel_id=1, source_target_pairs={{0,8},{1,505},{2,10},{3,507},{4,12},{5,509},{6,14},{7,511},{8,16},... | collective-permute-start | bytes 1572872 | tf_op jit(solution)/shard_map/ppermute | solution.py:343
  40.1 0.0 copy-done.9
  40.1 0.0 copy-done.10
  40.1 0.2 select_reduce_fusion
  40.3 0.2 collective-permute-done.1.pair
  40.5 6.9 %collective-permute-start.2 = (bf16[8,2,128,128]{3,2,1,0:T(8,128)(2,1)}, bf16[8,2,128,128]{3,2,1,0:T(8,128)(2,1)S(1)}, u32[]{:S(2)}, u32[]{:S(2)}) collective-permute-start(bf16[8,2,128,128]{3,2,1,0:T(8,128)(2,1)} %collective-permute-done.1.pair), channel_id=1, source_target_pairs={{0,504},{1,9},{2,506},{3,11},{4,508},{5,13},{6,510},{7,15},{8,0},{... | collective-permute-start | bytes 1572872 | tf_op jit(solution)/shard_map/ppermute | solution.py:343
  47.4 0.0 copy-done.2
  47.4 0.0 copy-done.3
  47.4 0.0 copy-start.1
  47.4 1.2 %copy-done.1 = bf16[33,128,128]{2,1,0:T(8,128)(2,1)S(1)} copy-done((bf16[33,128,128]{2,1,0:T(8,128)(2,1)S(1)}, bf16[33,128,128]{2,1,0:T(8,128)(2,1)}, u32[]{:S(2)}) %copy-start.1) | copy-done | bytes 1081368
  48.7 3.8 %shard_map.130 = (f32[8,2,128,128]{3,2,1,0:T(8,128)S(1)}, bf16[16,32,1024]{2,1,0:T(8,128)(2,1)S(1)}, bf16[16,32,128]{2,1,0:T(8,128)(2,1)S(1)}, bf16[16,32,128]{2,1,0:T(8,128)(2,1)S(1)}) custom-call(s32[16]{0:T(128)S(1)} %multiply_add_fusion.plan, bf16[33,128,128]{2,1,0:T(8,128)(2,1)S(1)} %get-tuple-element.45.query_rows, ...), custom_call_target="tpu_custom_call" | custom-call | flops 1711276032 | bytes 1310720 | tf_op jit(solution)/shard_map/pallas_call | solution.py:268
  52.5 2.4 %collective-permute-done.3.pair = bf16[8,2,128,128]{3,2,1,0:T(8,128)(2,1)} collective-permute-done((bf16[8,2,128,128]{3,2,1,0:T(8,128)(2,1)}, bf16[8,2,128,128]{3,2,1,0:T(8,128)(2,1)}, u32[]{:S(2)}, u32[]{:S(2)}) %collective-permute-start.3) | collective-permute-done | bytes 524320 | tf_op jit(solution)/shard_map/ppermute | solution.py:343
  54.8 6.2 %shard_map.131 = (bf16[8,2,128,128]{3,2,1,0:T(8,128)(2,1)S(1)}, bf16[16,32,1024]{2,1,0:T(8,128)(2,1)S(1)}, bf16[16,32,128]{2,1,0:T(8,128)(2,1)S(1)}, bf16[16,32,128]{2,1,0:T(8,128)(2,1)S(1)}) custom-call(s32[16]{0:T(128)S(1)} %multiply_add_fusion.plan, bf16[33,128,128]{2,1,0:T(8,128)(2,1)S(1)} %get-tuple-element.45.query_rows, ...), custom_call_target="tpu_custom_call" | custom-call | flops 1711276032 | bytes 1310720 | tf_op jit(solution)/shard_map/pallas_call | solution.py:268
  61.0 3.7 %collective-permute-start.5 = (bf16[8,2,128,128]{3,2,1,0:T(8,128)(2,1)S(1)}, bf16[8,2,128,128]{3,2,1,0:T(8,128)(2,1)S(1)}, u32[]{:S(2)}, u32[]{:S(2)}) collective-permute-start(bf16[8,2,128,128]{3,2,1,0:T(8,128)(2,1)S(1)} %get-tuple-element.73), channel_id=1, source_target_pairs={{0,504},{1,9},{2,506},{3,11},{4,508},{5,13},{6,510},{7,15},{8,0},{... | collective-permute-start | bytes 1572872 | tf_op jit(solution)/shard_map/ppermute | solution.py:343
  64.8 0.0 collective-permute-done.2.pair
  64.8 2.5 %shard_map.132 = (bf16[8,2,128,128]{3,2,1,0:T(8,128)(2,1)S(1)}, bf16[16,32,1024]{2,1,0:T(8,128)(2,1)S(1)}, bf16[16,32,128]{2,1,0:T(8,128)(2,1)S(1)}, bf16[16,32,128]{2,1,0:T(8,128)(2,1)S(1)}) custom-call(s32[16]{0:T(128)S(1)} %multiply_add_fusion.plan, bf16[33,128,128]{2,1,0:T(8,128)(2,1)S(1)} %get-tuple-element.45.query_rows, ...), custom_call_target="tpu_custom_call" | custom-call | flops 1711276032 | bytes 1310720 | tf_op jit(solution)/shard_map/pallas_call | solution.py:268
  67.3 3.1 %collective-permute-start.4 = (bf16[8,2,128,128]{3,2,1,0:T(8,128)(2,1)S(1)}, bf16[8,2,128,128]{3,2,1,0:T(8,128)(2,1)S(1)}, u32[]{:S(2)}, u32[]{:S(2)}) collective-permute-start(bf16[8,2,128,128]{3,2,1,0:T(8,128)(2,1)S(1)} %get-tuple-element.61), channel_id=1, source_target_pairs={{0,8},{1,505},{2,10},{3,507},{4,12},{5,509},{6,14},{7,511},{8,16},... | collective-permute-start | bytes 1572872 | tf_op jit(solution)/shard_map/ppermute | solution.py:343
  70.4 6.2 %shard_map.133 = (f32[8,2,128,128]{3,2,1,0:T(8,128)S(1)}, bf16[16,32,1024]{2,1,0:T(8,128)(2,1)S(1)}, bf16[16,32,128]{2,1,0:T(8,128)(2,1)S(1)}, bf16[16,32,128]{2,1,0:T(8,128)(2,1)S(1)}) custom-call(s32[16]{0:T(128)S(1)} %multiply_add_fusion.plan, bf16[33,128,128]{2,1,0:T(8,128)(2,1)S(1)} %get-tuple-element.45.query_rows, ...), custom_call_target="tpu_custom_call" | custom-call | flops 1711276032 | bytes 1310720 | tf_op jit(solution)/shard_map/pallas_call | solution.py:268
  76.6 0.0 collective-permute-done.5
  76.6 0.1 add_convert_fusion.1
  76.8 9.0 %collective-permute-start.6 = (bf16[8,2,128,128]{3,2,1,0:T(8,128)(2,1)S(1)}, bf16[8,2,128,128]{3,2,1,0:T(8,128)(2,1)S(1)}, u32[]{:S(2)}, u32[]{:S(2)}) collective-permute-start(bf16[8,2,128,128]{3,2,1,0:T(8,128)(2,1)S(1)} %add_convert_fusion.1), channel_id=1, source_target_pairs={{0,504},{1,9},{2,506},{3,11},{4,508},{5,13},{6,510},{7,15},{8,0},{... | collective-permute-start | bytes 1572872 | tf_op jit(solution)/shard_map/ppermute | solution.py:343
  85.8 7.3 %collective-permute-done.4 = bf16[8,2,128,128]{3,2,1,0:T(8,128)(2,1)S(1)} collective-permute-done((bf16[8,2,128,128]{3,2,1,0:T(8,128)(2,1)S(1)}, bf16[8,2,128,128]{3,2,1,0:T(8,128)(2,1)S(1)}, u32[]{:S(2)}, u32[]{:S(2)}) %collective-permute-start.4) | collective-permute-done | bytes 524320 | tf_op jit(solution)/shard_map/ppermute | solution.py:343
  93.0 0.1 add_convert_fusion.2
  93.2 1.9 %collective-permute-start.7 = (bf16[8,2,128,128]{3,2,1,0:T(8,128)(2,1)S(1)}, bf16[8,2,128,128]{3,2,1,0:T(8,128)(2,1)S(1)}, u32[]{:S(2)}, u32[]{:S(2)}) collective-permute-start(bf16[8,2,128,128]{3,2,1,0:T(8,128)(2,1)S(1)} %add_convert_fusion.2), channel_id=1, source_target_pairs={{0,8},{1,505},{2,10},{3,507},{4,12},{5,509},{6,14},{7,511},{8,16},... | collective-permute-start | bytes 1572872 | tf_op jit(solution)/shard_map/ppermute | solution.py:343
  95.1 3.8 %shard_map.134 = (f32[8,2,128,128]{3,2,1,0:T(8,128)S(1)}, bf16[16,32,1024]{2,1,0:T(8,128)(2,1)}, bf16[16,32,128]{2,1,0:T(8,128)(2,1)}, bf16[16,32,128]{2,1,0:T(8,128)(2,1)}) custom-call(s32[16]{0:T(128)S(1)} %multiply_add_fusion.plan, bf16[33,128,128]{2,1,0:T(8,128)(2,1)S(1)} %get-tuple-element.45.query_rows, ...), custom_call_target="tpu_custom_call" | custom-call | flops 1711276032 | bytes 1310720 | tf_op jit(solution)/shard_map/pallas_call | solution.py:268
  99.0 0.0 collective-permute-done.6
  99.0 7.4 %collective-permute-done.7 = bf16[8,2,128,128]{3,2,1,0:T(8,128)(2,1)S(1)} collective-permute-done((bf16[8,2,128,128]{3,2,1,0:T(8,128)(2,1)S(1)}, bf16[8,2,128,128]{3,2,1,0:T(8,128)(2,1)S(1)}, u32[]{:S(2)}, u32[]{:S(2)}) %collective-permute-start.7) | collective-permute-done | bytes 524320 | tf_op jit(solution)/shard_map/ppermute | solution.py:343
  106.4 0.2 add_convert_fusion
  106.6 12.8 %all_to_all.11.pair = bf16[8,2,128,128]{3,2,1,0:T(8,128)(2,1)S(1)} all-to-all(bf16[8,2,128,128]{3,2,1,0:T(8,128)(2,1)S(1)} %add_convert_fusion), channel_id=1, replica_groups=mesh['dp'=64,'mp'=8] {'mp'}, dimensions={0} | all-to-all | bytes 1048576 | tf_op jit(solution)/shard_map/all_to_all | solution.py:384
  119.4 0.9 shard_map.135
  (1 shorter events, 0.0 us)
Async XLA Ops:
  0.6 30.7 %copy-start.5 = (bf16[16,32,1024]{2,1,0:T(8,128)(2,1)S(1)}, bf16[16,32,1024]{2,1,0:T(8,128)(2,1)}, u32[]{:S(2)}) copy-start(bf16[16,32,1024]{2,1,0:T(8,128)(2,1)} %grad_out.1) | copy-start | bytes 3145732
  0.6 30.7 %copy-start.4 = (bf16[16,32,1024]{2,1,0:T(8,128)(2,1)S(1)}, bf16[16,32,1024]{2,1,0:T(8,128)(2,1)}, u32[]{:S(2)}) copy-start(bf16[16,32,1024]{2,1,0:T(8,128)(2,1)} %query.1) | copy-start | bytes 3145732
  0.7 1.1 copy-start.6
  1.8 0.9 copy-start.7
  2.7 28.6 %copy-start.8 = (s32[16]{0:T(128)S(1)}, s32[16]{0:T(128)}, u32[]{:S(2)}) copy-start(s32[16]{0:T(128)} %lengths.1) | copy-start | bytes 196
  17.6 22.5 %copy-start.9 = (s32[64]{0:T(128)S(1)}, s32[64]{0:T(128)}, u32[]{:S(2)}) copy-start(s32[64]{0:T(128)} %param.15) | copy-start | bytes 772
  17.6 22.5 %copy-start.10 = (s32[16]{0:T(128)S(1)}, s32[16]{0:T(128)}, u32[]{:S(2)}) copy-start(s32[16]{0:T(128)} %param.16) | copy-start | bytes 196
  17.6 29.8 %copy-start.2 = (bf16[16,32,128]{2,1,0:T(8,128)(2,1)S(1)}, bf16[16,32,128]{2,1,0:T(8,128)(2,1)}, u32[]{:S(2)}) copy-start(bf16[16,32,128]{2,1,0:T(8,128)(2,1)} %comp_key.9) | copy-start | bytes 393220
  17.6 29.8 %copy-start.3 = (bf16[16,32,128]{2,1,0:T(8,128)(2,1)S(1)}, bf16[16,32,128]{2,1,0:T(8,128)(2,1)}, u32[]{:S(2)}) copy-start(bf16[16,32,128]{2,1,0:T(8,128)(2,1)} %comp_value.9) | copy-start | bytes 393220
  17.6 20.6 %collective-permute-start = (bf16[8,2,128,128]{3,2,1,0:T(8,128)(2,1)}, bf16[8,2,128,128]{3,2,1,0:T(8,128)(2,1)}, u32[]{:S(2)}, u32[]{:S(2)}) collective-permute-start(bf16[8,2,128,128]{3,2,1,0:T(8,128)(2,1)} %all_to_all.10.pair), channel_id=1, source_target_pairs={{0,8},{1,505},{2,10},{3,507},{4,12},{5,509},{6,14},{7,511},{8,16},... | collective-permute-start | bytes 1572872 | tf_op jit(solution)/shard_map/ppermute | solution.py:343
  21.5 19.0 %collective-permute-start.1 = (bf16[8,2,128,128]{3,2,1,0:T(8,128)(2,1)}, bf16[8,2,128,128]{3,2,1,0:T(8,128)(2,1)}, u32[]{:S(2)}, u32[]{:S(2)}) collective-permute-start(bf16[8,2,128,128]{3,2,1,0:T(8,128)(2,1)} %all_to_all.10.pair), channel_id=1, source_target_pairs={{0,504},{1,9},{2,506},{3,11},{4,508},{5,13},{6,510},{7,15},{8,0},{... | collective-permute-start | bytes 1572872 | tf_op jit(solution)/shard_map/ppermute | solution.py:343
  33.4 1.0 copy-start
  38.1 16.7 %collective-permute-start.3 = (bf16[8,2,128,128]{3,2,1,0:T(8,128)(2,1)}, bf16[8,2,128,128]{3,2,1,0:T(8,128)(2,1)}, u32[]{:S(2)}, u32[]{:S(2)}) collective-permute-start(bf16[8,2,128,128]{3,2,1,0:T(8,128)(2,1)} %collective-permute-done.pair), channel_id=1, source_target_pairs={{0,8},{1,505},{2,10},{3,507},{4,12},{5,509},{6,14},{7,511},{8,16},... | collective-permute-start | bytes 1572872 | tf_op jit(solution)/shard_map/ppermute | solution.py:343
  40.5 24.3 %collective-permute-start.2 = (bf16[8,2,128,128]{3,2,1,0:T(8,128)(2,1)}, bf16[8,2,128,128]{3,2,1,0:T(8,128)(2,1)S(1)}, u32[]{:S(2)}, u32[]{:S(2)}) collective-permute-start(bf16[8,2,128,128]{3,2,1,0:T(8,128)(2,1)} %collective-permute-done.1.pair), channel_id=1, source_target_pairs={{0,504},{1,9},{2,506},{3,11},{4,508},{5,13},{6,510},{7,15},{8,0},{... | collective-permute-start | bytes 1572872 | tf_op jit(solution)/shard_map/ppermute | solution.py:343
  47.4 1.2 %copy-start.1 = (bf16[33,128,128]{2,1,0:T(8,128)(2,1)S(1)}, bf16[33,128,128]{2,1,0:T(8,128)(2,1)}, u32[]{:S(2)}) copy-start(bf16[33,128,128]{2,1,0:T(8,128)(2,1)} %copy-done) | copy-start | bytes 3244036
  61.0 15.6 %collective-permute-start.5 = (bf16[8,2,128,128]{3,2,1,0:T(8,128)(2,1)S(1)}, bf16[8,2,128,128]{3,2,1,0:T(8,128)(2,1)S(1)}, u32[]{:S(2)}, u32[]{:S(2)}) collective-permute-start(bf16[8,2,128,128]{3,2,1,0:T(8,128)(2,1)S(1)} %get-tuple-element.73), channel_id=1, source_target_pairs={{0,504},{1,9},{2,506},{3,11},{4,508},{5,13},{6,510},{7,15},{8,0},{... | collective-permute-start | bytes 1572872 | tf_op jit(solution)/shard_map/ppermute | solution.py:343
  67.3 25.7 %collective-permute-start.4 = (bf16[8,2,128,128]{3,2,1,0:T(8,128)(2,1)S(1)}, bf16[8,2,128,128]{3,2,1,0:T(8,128)(2,1)S(1)}, u32[]{:S(2)}, u32[]{:S(2)}) collective-permute-start(bf16[8,2,128,128]{3,2,1,0:T(8,128)(2,1)S(1)} %get-tuple-element.61), channel_id=1, source_target_pairs={{0,8},{1,505},{2,10},{3,507},{4,12},{5,509},{6,14},{7,511},{8,16},... | collective-permute-start | bytes 1572872 | tf_op jit(solution)/shard_map/ppermute | solution.py:343
  76.8 22.2 %collective-permute-start.6 = (bf16[8,2,128,128]{3,2,1,0:T(8,128)(2,1)S(1)}, bf16[8,2,128,128]{3,2,1,0:T(8,128)(2,1)S(1)}, u32[]{:S(2)}, u32[]{:S(2)}) collective-permute-start(bf16[8,2,128,128]{3,2,1,0:T(8,128)(2,1)S(1)} %add_convert_fusion.1), channel_id=1, source_target_pairs={{0,504},{1,9},{2,506},{3,11},{4,508},{5,13},{6,510},{7,15},{8,0},{... | collective-permute-start | bytes 1572872 | tf_op jit(solution)/shard_map/ppermute | solution.py:343
  93.2 13.2 %collective-permute-start.7 = (bf16[8,2,128,128]{3,2,1,0:T(8,128)(2,1)S(1)}, bf16[8,2,128,128]{3,2,1,0:T(8,128)(2,1)S(1)}, u32[]{:S(2)}, u32[]{:S(2)}) collective-permute-start(bf16[8,2,128,128]{3,2,1,0:T(8,128)(2,1)S(1)} %add_convert_fusion.2), channel_id=1, source_target_pairs={{0,8},{1,505},{2,10},{3,507},{4,12},{5,509},{6,14},{7,511},{8,16},... | collective-permute-start | bytes 1572872 | tf_op jit(solution)/shard_map/ppermute | solution.py:343

commit v4 on v3

--- a/solution.py
+++ b/solution.py
@@ -333,14 +333,11 @@
     return pl.pallas_call(join_kernel, out_shape=[whole, whole], compiler_params=SMALL)(pair)
 
 
-def shifted(value, steps):
-    size, shards = lax.axis_size("dp"), lax.axis_size("mp")
-    pairs = []
-    for at in range(size):
-        for shard in range(shards):
-            target = (at + (steps if shard % 2 == 0 else -steps)) % size
-            pairs.append((at * shards + shard, target * shards + shard))
-    return lax.ppermute(value, ("dp", "mp"), pairs)
+def swapped(value, first):
+    size = lax.axis_size("dp")
+    return lax.ppermute(
+        value, "dp", [(at, (at + (1 if at % 2 == first else -1)) % size) for at in range(size)]
+    )
 
 
 def per_device(
@@ -352,35 +349,35 @@
     prompt_ids = jnp.arange(owner.shape[0], dtype=jnp.int32)
     holder_of = jnp.sum(jnp.where(group[:, None] == prompt_ids[None, :], owner[None, :], 0), axis=1)
     near = ((holder_of - position + 2 + axis_count) % axis_count).astype(jnp.int32)
-    near = jnp.where(lax.axis_index("mp") % 2 == 0, near, 4 - near)
+    near = jnp.where(position % 2 == 0, near, 4 - near)
 
     pair = split_heads(prefix_key[0], prefix_value[0], shards)
     own = lax.all_to_all(pair, "mp", split_axis=0, concat_axis=0, tiled=True)
-    low_one = shifted(own, 1)
-    up_one = shifted(own, -1)
+    even_one = swapped(own, 0)
+    odd_one = swapped(own, 1)
     plan = near * 64 + lengths
     prepared = prepare(lengths, query, grad_out)
-    low_one, prepared = lax.optimization_barrier((low_one, prepared))
-    low_two = shifted(low_one, 1)
-    up_two = shifted(up_one, -1)
-    low_near, _ = lax.optimization_barrier((low_one, up_one))
+    even_one, prepared = lax.optimization_barrier((even_one, prepared))
+    odd_two = swapped(even_one, 1)
+    even_two = swapped(odd_one, 0)
 
     def grads(code, pair, chain, kind):
         return near_grads(code, pair, plan, prepared, comp_key, comp_value, chain, query.shape, kind)
 
-    low_term, chain = grads(1, low_near, None, jnp.float32)
-    low_two_term, chain = grads(0, low_two, chain, jnp.bfloat16)
-    up_two_term, chain = grads(4, up_two, chain, jnp.bfloat16)
-    low_back = shifted(low_two_term, -1).astype(jnp.float32)
-    up_back = shifted(up_two_term, 1).astype(jnp.float32)
-    up_term, chain = grads(3, up_one, chain, jnp.float32)
-    low_sum = (low_term + low_back).astype(jnp.bfloat16)
-    up_sum = (up_term + up_back).astype(jnp.bfloat16)
-    up_sum, chain = lax.optimization_barrier((up_sum, chain))
-    low_back = shifted(low_sum, -1).astype(jnp.float32)
-    up_back = shifted(up_sum, 1).astype(jnp.float32)
+    odd_two_term, chain = grads(0, odd_two, None, jnp.bfloat16)
+    even_two_term, chain = grads(4, even_two, chain, jnp.bfloat16)
+    odd_two_term, even_two_term = lax.optimization_barrier((odd_two_term, even_two_term))
+    even_back = swapped(odd_two_term, 1).astype(jnp.float32)
+    odd_back = swapped(even_two_term, 0).astype(jnp.float32)
+    odd_term, chain = grads(1, odd_one, chain, jnp.float32)
+    even_term, chain = grads(3, even_one, chain, jnp.float32)
+    even_sum = (even_term + even_back).astype(jnp.bfloat16)
+    odd_sum = (odd_term + odd_back).astype(jnp.bfloat16)
+    odd_sum, even_sum, chain = lax.optimization_barrier((odd_sum, even_sum, chain))
+    even_back = swapped(even_sum, 0).astype(jnp.float32)
+    odd_back = swapped(odd_sum, 1).astype(jnp.float32)
     own_term, chain = grads(2, own, chain, jnp.float32)
-    gathered = (own_term + low_back + up_back).astype(jnp.bfloat16)
+    gathered = (own_term + even_back + odd_back).astype(jnp.bfloat16)
     back = lax.all_to_all(gathered, "mp", split_axis=0, concat_axis=0, tiled=True)
     key_back, value_back = join_heads(back)
     return chain[0], chain[1], chain[2], key_back[None], value_back[None]

time: 121 us -> 124 us (1.025)
  the two profiles are of different devices: /device:TPU:6 before, /device:TPU:1 now
where the time goes in v4:
time: 124 us; the launch traced here: 123 us
  starting transfers between devices  38.7 us (31%)
  blocking collectives  35 us (28%)
  Pallas kernels  27 us (22%)
  waiting for transfers between devices  16.4 us (13%)
  local copies, waits for them, and re-layouts  4.33 us (3%)
    ppermute x8, starting transfers between devices, swapped(): lax.ppermute(value, 'dp', [(at, (at + (1 if at % 2 == first else -1)) % s...  38.7 us
    pallas_call x5, Pallas kernels, near_grads(): pl.pallas_call(functools.partial(near_kernel, code, chain is not None), o...  23.9 us
    all_to_all x1, blocking collectives, per_device(): own = lax.all_to_all(pair, 'mp', split_axis=0, concat_axis=0, tiled=True)  18.6 us
    ppermute x8, waiting for transfers between devices, swapped(): lax.ppermute(value, 'dp', [(at, (at + (1 if at % 2 == first else -1)) % s...  16.4 us
    all_to_all x1, blocking collectives, per_device(): lax.all_to_all(gathered, 'mp', split_axis=0, concat_axis=0, tiled=True)  16.4 us
    unnamed x26, local copies, waits for them, and re-layouts  4.33 us
  transfers between devices with their start and end apart: 8, of which 3 were waited for; matrix products, arithmetic and copies ran while one was open for 0% of the time, Pallas kernels for 19%

profile of v4, /device:TPU:1, one launch (start us, length us, event | category | flops | bytes accessed | tf_op | source)
XLA Modules:
  0.0 123.1 jit_solution(5093840921553165085)
XLA Ops:
  0.6 0.0 copy-start.7
  0.6 0.0 copy-start.6
  0.7 0.0 copy-start.8
  0.7 1.1 copy-done.8
  1.8 0.0 copy-start.9
  1.8 0.9 copy-done.9
  2.7 0.0 copy-start.10
  2.7 0.1 shard_map.128
  2.8 18.6 %all_to_all.10.pair = bf16[8,2,128,128]{3,2,1,0:T(8,128)(2,1)S(1)} all-to-all(bf16[8,2,128,128]{3,2,1,0:T(8,128)(2,1)S(1)} %shard_map.128), channel_id=1, replica_groups=mesh['dp'=64,'mp'=8] {'mp'}, dimensions={0} | all-to-all | bytes 1048576 | tf_op jit(solution)/shard_map/all_to_all | solution.py:355
  21.4 0.0 copy-start.4
  21.4 0.0 copy-start.11
  21.4 0.0 copy-start.12
  21.4 0.0 copy-start.2
  21.5 0.0 copy-start.3
  21.5 2.1 %collective-permute-start = (bf16[8,2,128,128]{3,2,1,0:T(8,128)(2,1)S(1)}, bf16[8,2,128,128]{3,2,1,0:T(8,128)(2,1)}, u32[]{:S(2)}, u32[]{:S(2)}) collective-permute-start(bf16[8,2,128,128]{3,2,1,0:T(8,128)(2,1)S(1)} %all_to_all.10.pair), channel_id=1, source_target_pairs={{0,8},{8,0},{16,24},{24,16},{32,40},{40,32},{48,56},{56,48},{64,72... | collective-permute-start | bytes 1572872 | tf_op jit(solution)/shard_map/ppermute | solution.py:338
  23.5 10.5 %collective-permute-start.1 = (bf16[8,2,128,128]{3,2,1,0:T(8,128)(2,1)S(1)}, bf16[8,2,128,128]{3,2,1,0:T(8,128)(2,1)}, u32[]{:S(2)}, u32[]{:S(2)}) collective-permute-start(bf16[8,2,128,128]{3,2,1,0:T(8,128)(2,1)S(1)} %all_to_all.10.pair), channel_id=1, source_target_pairs={{0,504},{8,16},{16,8},{24,32},{32,24},{40,48},{48,40},{56,64},{64,... | collective-permute-start | bytes 1572872 | tf_op jit(solution)/shard_map/ppermute | solution.py:338
  34.1 0.0 copy-done.7
  34.1 0.0 copy-done.6
  34.1 0.0 copy-done.10
  34.1 2.0 %shard_map.129 = (bf16[33,128,128]{2,1,0:T(8,128)(2,1)S(1)}, bf16[33,128,128]{2,1,0:T(8,128)(2,1)S(1)}, bf16[33,128,128]{2,1,0:T(8,128)(2,1)S(1)}, bf16[33,128,128]{2,1,0:T(8,128)(2,1)S(1)}) custom-call(s32[16]{0:T(128)S(1)} %copy-done.10, bf16[16,32,1024]{2,1,0:T(8,128)(2,1)S(1)} %copy-done.6, bf16[16,32,1024]{2,1,0:T(8,128)(2,1)S(1)} %copy-done.7), custom_call_target="tpu_custom_call" | custom-call | bytes 6291456 | tf_op jit(solution)/shard_map/pallas_call | solution.py:64
  36.1 0.0 copy-done.4
  36.1 0.0 copy-start
  36.2 1.0 copy-done
  37.2 0.0 collective-permute-done.pair
  37.2 8.6 %collective-permute-start.3 = (bf16[8,2,128,128]{3,2,1,0:T(8,128)(2,1)}, bf16[8,2,128,128]{3,2,1,0:T(8,128)(2,1)}, u32[]{:S(2)}, u32[]{:S(2)}) collective-permute-start(bf16[8,2,128,128]{3,2,1,0:T(8,128)(2,1)} %collective-permute-done.pair), channel_id=1, source_target_pairs={{0,504},{8,16},{16,8},{24,32},{32,24},{40,48},{48,40},{56,64},{64,... | collective-permute-start | bytes 1572872 | tf_op jit(solution)/shard_map/ppermute | solution.py:338
  45.8 0.0 collective-permute-done.1.pair
  45.8 1.9 %collective-permute-start.2 = (bf16[8,2,128,128]{3,2,1,0:T(8,128)(2,1)}, bf16[8,2,128,128]{3,2,1,0:T(8,128)(2,1)}, u32[]{:S(2)}, u32[]{:S(2)}) collective-permute-start(bf16[8,2,128,128]{3,2,1,0:T(8,128)(2,1)} %collective-permute-done.1.pair), channel_id=1, source_target_pairs={{0,8},{8,0},{16,24},{24,16},{32,40},{40,32},{48,56},{56,48},{64,72... | collective-permute-start | bytes 1572872 | tf_op jit(solution)/shard_map/ppermute | solution.py:338
  47.7 0.0 copy-done.11
  47.7 0.0 copy-done.12
  47.7 0.2 select_reduce_fusion
  47.9 8.4 %collective-permute-done.3.pair = bf16[8,2,128,128]{3,2,1,0:T(8,128)(2,1)} collective-permute-done((bf16[8,2,128,128]{3,2,1,0:T(8,128)(2,1)}, bf16[8,2,128,128]{3,2,1,0:T(8,128)(2,1)}, u32[]{:S(2)}, u32[]{:S(2)}) %collective-permute-start.3) | collective-permute-done | bytes 524320 | tf_op jit(solution)/shard_map/ppermute | solution.py:338
  56.3 0.0 copy-done.2
  56.4 0.0 copy-done.3
  56.4 0.0 copy-start.1
  56.4 1.2 %copy-done.1 = bf16[33,128,128]{2,1,0:T(8,128)(2,1)S(1)} copy-done((bf16[33,128,128]{2,1,0:T(8,128)(2,1)S(1)}, bf16[33,128,128]{2,1,0:T(8,128)(2,1)}, u32[]{:S(2)}) %copy-start.1) | copy-done | bytes 1081368
  57.6 2.8 %shard_map.130 = (bf16[8,2,128,128]{3,2,1,0:T(8,128)(2,1)S(1)}, bf16[16,32,1024]{2,1,0:T(8,128)(2,1)S(1)}, bf16[16,32,128]{2,1,0:T(8,128)(2,1)S(1)}, bf16[16,32,128]{2,1,0:T(8,128)(2,1)S(1)}) custom-call(s32[16]{0:T(128)S(1)} %multiply_add_fusion.plan, bf16[33,128,128]{2,1,0:T(8,128)(2,1)S(1)} %get-tuple-element.47.query_rows, ...), custom_call_target="tpu_custom_call" | custom-call | flops 1711276032 | bytes 1310720 | tf_op jit(solution)/shard_map/pallas_call | solution.py:268
  60.4 0.0 collective-permute-done.2.pair
  60.4 2.9 %shard_map.131 = (bf16[8,2,128,128]{3,2,1,0:T(8,128)(2,1)S(1)}, bf16[16,32,1024]{2,1,0:T(8,128)(2,1)S(1)}, bf16[16,32,128]{2,1,0:T(8,128)(2,1)S(1)}, bf16[16,32,128]{2,1,0:T(8,128)(2,1)S(1)}) custom-call(s32[16]{0:T(128)S(1)} %multiply_add_fusion.plan, bf16[33,128,128]{2,1,0:T(8,128)(2,1)S(1)} %get-tuple-element.47.query_rows, ...), custom_call_target="tpu_custom_call" | custom-call | flops 1711276032 | bytes 1310720 | tf_op jit(solution)/shard_map/pallas_call | solution.py:268
  63.3 6.1 %collective-permute-start.4 = (bf16[8,2,128,128]{3,2,1,0:T(8,128)(2,1)S(1)}, bf16[8,2,128,128]{3,2,1,0:T(8,128)(2,1)S(1)}, u32[]{:S(2)}, u32[]{:S(2)}) collective-permute-start(bf16[8,2,128,128]{3,2,1,0:T(8,128)(2,1)S(1)} %get-tuple-element.61), channel_id=1, source_target_pairs={{0,8},{8,0},{16,24},{24,16},{32,40},{40,32},{48,56},{56,48},{64,72... | collective-permute-start | bytes 1572872 | tf_op jit(solution)/shard_map/ppermute | solution.py:338
  69.5 4.5 %collective-permute-start.5 = (bf16[8,2,128,128]{3,2,1,0:T(8,128)(2,1)S(1)}, bf16[8,2,128,128]{3,2,1,0:T(8,128)(2,1)S(1)}, u32[]{:S(2)}, u32[]{:S(2)}) collective-permute-start(bf16[8,2,128,128]{3,2,1,0:T(8,128)(2,1)S(1)} %get-tuple-element.66), channel_id=1, source_target_pairs={{0,504},{8,16},{16,8},{24,32},{32,24},{40,48},{48,40},{56,64},{64,... | collective-permute-start | bytes 1572872 | tf_op jit(solution)/shard_map/ppermute | solution.py:338
  73.9 11.1 %shard_map.132 = (f32[8,2,128,128]{3,2,1,0:T(8,128)S(1)}, bf16[16,32,1024]{2,1,0:T(8,128)(2,1)S(1)}, bf16[16,32,128]{2,1,0:T(8,128)(2,1)S(1)}, bf16[16,32,128]{2,1,0:T(8,128)(2,1)S(1)}) custom-call(s32[16]{0:T(128)S(1)} %multiply_add_fusion.plan, bf16[33,128,128]{2,1,0:T(8,128)(2,1)S(1)} %get-tuple-element.47.query_rows, ...), custom_call_target="tpu_custom_call" | custom-call | flops 1711276032 | bytes 1310720 | tf_op jit(solution)/shard_map/pallas_call | solution.py:268
  85.0 2.8 %shard_map.133 = (f32[8,2,128,128]{3,2,1,0:T(8,128)S(1)}, bf16[16,32,1024]{2,1,0:T(8,128)(2,1)S(1)}, bf16[16,32,128]{2,1,0:T(8,128)(2,1)S(1)}, bf16[16,32,128]{2,1,0:T(8,128)(2,1)S(1)}) custom-call(s32[16]{0:T(128)S(1)} %multiply_add_fusion.plan, bf16[33,128,128]{2,1,0:T(8,128)(2,1)S(1)} %get-tuple-element.47.query_rows, ...), custom_call_target="tpu_custom_call" | custom-call | flops 1711276032 | bytes 1310720 | tf_op jit(solution)/shard_map/pallas_call | solution.py:268
  87.9 0.0 collective-permute-done.4
  87.9 0.1 add_convert_fusion.2
  88.0 0.0 copy-start.5
  88.0 0.0 collective-permute-done.5
  88.0 0.1 add_convert_fusion.1
  88.2 1.9 %collective-permute-start.6 = (bf16[8,2,128,128]{3,2,1,0:T(8,128)(2,1)S(1)}, bf16[8,2,128,128]{3,2,1,0:T(8,128)(2,1)S(1)}, u32[]{:S(2)}, u32[]{:S(2)}) collective-permute-start(bf16[8,2,128,128]{3,2,1,0:T(8,128)(2,1)S(1)} %add_convert_fusion.1), channel_id=1, source_target_pairs={{0,8},{8,0},{16,24},{24,16},{32,40},{40,32},{48,56},{56,48},{64,72... | collective-permute-start | bytes 1572872 | tf_op jit(solution)/shard_map/ppermute | solution.py:338
  90.1 3.1 %collective-permute-start.7 = (bf16[8,2,128,128]{3,2,1,0:T(8,128)(2,1)S(1)}, bf16[8,2,128,128]{3,2,1,0:T(8,128)(2,1)S(1)}, u32[]{:S(2)}, u32[]{:S(2)}) collective-permute-start(bf16[8,2,128,128]{3,2,1,0:T(8,128)(2,1)S(1)} %add_convert_fusion.2), channel_id=1, source_target_pairs={{0,504},{8,16},{16,8},{24,32},{32,24},{40,48},{48,40},{56,64},{64,... | collective-permute-start | bytes 1572872 | tf_op jit(solution)/shard_map/ppermute | solution.py:338
  93.2 0.0 copy-done.5
  93.2 4.3 %shard_map.134 = (f32[8,2,128,128]{3,2,1,0:T(8,128)S(1)}, bf16[16,32,1024]{2,1,0:T(8,128)(2,1)}, bf16[16,32,128]{2,1,0:T(8,128)(2,1)}, bf16[16,32,128]{2,1,0:T(8,128)(2,1)}) custom-call(s32[16]{0:T(128)S(1)} %multiply_add_fusion.plan, bf16[33,128,128]{2,1,0:T(8,128)(2,1)S(1)} %get-tuple-element.47.query_rows, ...), custom_call_target="tpu_custom_call" | custom-call | flops 1711276032 | bytes 1310720 | tf_op jit(solution)/shard_map/pallas_call | solution.py:268
  97.6 2.7 %collective-permute-done.6 = bf16[8,2,128,128]{3,2,1,0:T(8,128)(2,1)S(1)} collective-permute-done((bf16[8,2,128,128]{3,2,1,0:T(8,128)(2,1)S(1)}, bf16[8,2,128,128]{3,2,1,0:T(8,128)(2,1)S(1)}, u32[]{:S(2)}, u32[]{:S(2)}) %collective-permute-start.6) | collective-permute-done | bytes 524320 | tf_op jit(solution)/shard_map/ppermute | solution.py:338
  100.3 5.2 %collective-permute-done.7 = bf16[8,2,128,128]{3,2,1,0:T(8,128)(2,1)S(1)} collective-permute-done((bf16[8,2,128,128]{3,2,1,0:T(8,128)(2,1)S(1)}, bf16[8,2,128,128]{3,2,1,0:T(8,128)(2,1)S(1)}, u32[]{:S(2)}, u32[]{:S(2)}) %collective-permute-start.7) | collective-permute-done | bytes 524320 | tf_op jit(solution)/shard_map/ppermute | solution.py:338
  105.6 0.2 add_convert_fusion
  105.8 16.4 %all_to_all.11.pair = bf16[8,2,128,128]{3,2,1,0:T(8,128)(2,1)S(1)} all-to-all(bf16[8,2,128,128]{3,2,1,0:T(8,128)(2,1)S(1)} %add_convert_fusion), channel_id=1, replica_groups=mesh['dp'=64,'mp'=8] {'mp'}, dimensions={0} | all-to-all | bytes 1048576 | tf_op jit(solution)/shard_map/all_to_all | solution.py:381
  122.2 0.9 shard_map.135
  (1 shorter events, 0.0 us)
Async XLA Ops:
  0.6 33.4 %copy-start.7 = (bf16[16,32,1024]{2,1,0:T(8,128)(2,1)S(1)}, bf16[16,32,1024]{2,1,0:T(8,128)(2,1)}, u32[]{:S(2)}) copy-start(bf16[16,32,1024]{2,1,0:T(8,128)(2,1)} %grad_out.1) | copy-start | bytes 3145732
  0.6 33.4 %copy-start.6 = (bf16[16,32,1024]{2,1,0:T(8,128)(2,1)S(1)}, bf16[16,32,1024]{2,1,0:T(8,128)(2,1)}, u32[]{:S(2)}) copy-start(bf16[16,32,1024]{2,1,0:T(8,128)(2,1)} %query.1) | copy-start | bytes 3145732
  0.7 1.1 copy-start.8
  1.8 0.9 copy-start.9
  2.7 31.4 %copy-start.10 = (s32[16]{0:T(128)S(1)}, s32[16]{0:T(128)}, u32[]{:S(2)}) copy-start(s32[16]{0:T(128)} %lengths.1) | copy-start | bytes 196
  21.4 14.7 %copy-start.4 = (bf16[8,2,128,128]{3,2,1,0:T(8,128)(2,1)}, bf16[8,2,128,128]{3,2,1,0:T(8,128)(2,1)S(1)}, u32[]{:S(2)}) copy-start(bf16[8,2,128,128]{3,2,1,0:T(8,128)(2,1)S(1)} %all_to_all.10.pair) | copy-start | bytes 1572868
  21.4 26.3 %copy-start.11 = (s32[64]{0:T(128)S(1)}, s32[64]{0:T(128)}, u32[]{:S(2)}) copy-start(s32[64]{0:T(128)} %param.15) | copy-start | bytes 772
  21.4 26.3 %copy-start.12 = (s32[16]{0:T(128)S(1)}, s32[16]{0:T(128)}, u32[]{:S(2)}) copy-start(s32[16]{0:T(128)} %param.16) | copy-start | bytes 196
  21.4 34.9 %copy-start.2 = (bf16[16,32,128]{2,1,0:T(8,128)(2,1)S(1)}, bf16[16,32,128]{2,1,0:T(8,128)(2,1)}, u32[]{:S(2)}) copy-start(bf16[16,32,128]{2,1,0:T(8,128)(2,1)} %comp_key.9) | copy-start | bytes 393220
  21.5 34.9 %copy-start.3 = (bf16[16,32,128]{2,1,0:T(8,128)(2,1)S(1)}, bf16[16,32,128]{2,1,0:T(8,128)(2,1)}, u32[]{:S(2)}) copy-start(bf16[16,32,128]{2,1,0:T(8,128)(2,1)} %comp_value.9) | copy-start | bytes 393220
  21.5 15.7 %collective-permute-start = (bf16[8,2,128,128]{3,2,1,0:T(8,128)(2,1)S(1)}, bf16[8,2,128,128]{3,2,1,0:T(8,128)(2,1)}, u32[]{:S(2)}, u32[]{:S(2)}) collective-permute-start(bf16[8,2,128,128]{3,2,1,0:T(8,128)(2,1)S(1)} %all_to_all.10.pair), channel_id=1, source_target_pairs={{0,8},{8,0},{16,24},{24,16},{32,40},{40,32},{48,56},{56,48},{64,72... | collective-permute-start | bytes 1572872 | tf_op jit(solution)/shard_map/ppermute | solution.py:338
  23.5 22.3 %collective-permute-start.1 = (bf16[8,2,128,128]{3,2,1,0:T(8,128)(2,1)S(1)}, bf16[8,2,128,128]{3,2,1,0:T(8,128)(2,1)}, u32[]{:S(2)}, u32[]{:S(2)}) collective-permute-start(bf16[8,2,128,128]{3,2,1,0:T(8,128)(2,1)S(1)} %all_to_all.10.pair), channel_id=1, source_target_pairs={{0,504},{8,16},{16,8},{24,32},{32,24},{40,48},{48,40},{56,64},{64,... | collective-permute-start | bytes 1572872 | tf_op jit(solution)/shard_map/ppermute | solution.py:338
  36.1 1.0 copy-start
  37.2 19.2 %collective-permute-start.3 = (bf16[8,2,128,128]{3,2,1,0:T(8,128)(2,1)}, bf16[8,2,128,128]{3,2,1,0:T(8,128)(2,1)}, u32[]{:S(2)}, u32[]{:S(2)}) collective-permute-start(bf16[8,2,128,128]{3,2,1,0:T(8,128)(2,1)} %collective-permute-done.pair), channel_id=1, source_target_pairs={{0,504},{8,16},{16,8},{24,32},{32,24},{40,48},{48,40},{56,64},{64,... | collective-permute-start | bytes 1572872 | tf_op jit(solution)/shard_map/ppermute | solution.py:338
  45.8 14.6 %collective-permute-start.2 = (bf16[8,2,128,128]{3,2,1,0:T(8,128)(2,1)}, bf16[8,2,128,128]{3,2,1,0:T(8,128)(2,1)}, u32[]{:S(2)}, u32[]{:S(2)}) collective-permute-start(bf16[8,2,128,128]{3,2,1,0:T(8,128)(2,1)} %collective-permute-done.1.pair), channel_id=1, source_target_pairs={{0,8},{8,0},{16,24},{24,16},{32,40},{40,32},{48,56},{56,48},{64,72... | collective-permute-start | bytes 1572872 | tf_op jit(solution)/shard_map/ppermute | solution.py:338
  56.4 1.2 %copy-start.1 = (bf16[33,128,128]{2,1,0:T(8,128)(2,1)S(1)}, bf16[33,128,128]{2,1,0:T(8,128)(2,1)}, u32[]{:S(2)}) copy-start(bf16[33,128,128]{2,1,0:T(8,128)(2,1)} %copy-done) | copy-start | bytes 3244036
  63.3 24.6 %collective-permute-start.4 = (bf16[8,2,128,128]{3,2,1,0:T(8,128)(2,1)S(1)}, bf16[8,2,128,128]{3,2,1,0:T(8,128)(2,1)S(1)}, u32[]{:S(2)}, u32[]{:S(2)}) collective-permute-start(bf16[8,2,128,128]{3,2,1,0:T(8,128)(2,1)S(1)} %get-tuple-element.61), channel_id=1, source_target_pairs={{0,8},{8,0},{16,24},{24,16},{32,40},{40,32},{48,56},{56,48},{64,72... | collective-permute-start | bytes 1572872 | tf_op jit(solution)/shard_map/ppermute | solution.py:338
  69.5 18.6 %collective-permute-start.5 = (bf16[8,2,128,128]{3,2,1,0:T(8,128)(2,1)S(1)}, bf16[8,2,128,128]{3,2,1,0:T(8,128)(2,1)S(1)}, u32[]{:S(2)}, u32[]{:S(2)}) collective-permute-start(bf16[8,2,128,128]{3,2,1,0:T(8,128)(2,1)S(1)} %get-tuple-element.66), channel_id=1, source_target_pairs={{0,504},{8,16},{16,8},{24,32},{32,24},{40,48},{48,40},{56,64},{64,... | collective-permute-start | bytes 1572872 | tf_op jit(solution)/shard_map/ppermute | solution.py:338
  88.0 5.2 %copy-start.5 = (bf16[8,2,128,128]{3,2,1,0:T(8,128)(2,1)S(1)}, bf16[8,2,128,128]{3,2,1,0:T(8,128)(2,1)}, u32[]{:S(2)}) copy-start(bf16[8,2,128,128]{3,2,1,0:T(8,128)(2,1)} %copy-done.4) | copy-start | bytes 1572868
  88.2 12.1 %collective-permute-start.6 = (bf16[8,2,128,128]{3,2,1,0:T(8,128)(2,1)S(1)}, bf16[8,2,128,128]{3,2,1,0:T(8,128)(2,1)S(1)}, u32[]{:S(2)}, u32[]{:S(2)}) collective-permute-start(bf16[8,2,128,128]{3,2,1,0:T(8,128)(2,1)S(1)} %add_convert_fusion.1), channel_id=1, source_target_pairs={{0,8},{8,0},{16,24},{24,16},{32,40},{40,32},{48,56},{56,48},{64,72... | collective-permute-start | bytes 1572872 | tf_op jit(solution)/shard_map/ppermute | solution.py:338
  90.1 15.5 %collective-permute-start.7 = (bf16[8,2,128,128]{3,2,1,0:T(8,128)(2,1)S(1)}, bf16[8,2,128,128]{3,2,1,0:T(8,128)(2,1)S(1)}, u32[]{:S(2)}, u32[]{:S(2)}) collective-permute-start(bf16[8,2,128,128]{3,2,1,0:T(8,128)(2,1)S(1)} %add_convert_fusion.2), channel_id=1, source_target_pairs={{0,504},{8,16},{16,8},{24,32},{32,24},{40,48},{48,40},{56,64},{64,... | collective-permute-start | bytes 1572872 | tf_op jit(solution)/shard_map/ppermute | solution.py:338

commit v5 on v4

--- a/solution.py
+++ b/solution.py
@@ -158,16 +158,16 @@
 
 
 def near_kernel(code, chained, plan, query_rows, query_flip, live, live_flip, comp_key, comp_value,
-                pair, *refs):
+                near_key, near_value, *refs):
     if chained:
-        for done, out in zip(refs[:3], refs[4:7]):
+        for done, out in zip(refs[:3], refs[5:8]):
             out[...] = done[...]
         refs = refs[3:]
-    (term, dq, dk, dv, dk_sum, dv_sum, key_flip, key_sum, value_sum, listed) = refs[:10]
-    bufs = (refs[10:16], refs[16:22])
+    (key_term, value_term, dq, dk, dv, dk_sum, dv_sum, key_flip, key_sum, value_sum, listed) = refs[:11]
+    bufs = (refs[11:17], refs[17:23])
     count, slots = dq.shape[:2]
     prefix = key_sum.shape[0]
-    rows = pair.shape[2]
+    rows = near_key.shape[1]
     prepared = (query_rows, query_flip, live, live_flip)
 
     def size_of(slot):
@@ -187,12 +187,12 @@
     def _():
         dk_sum[...] = jnp.zeros_like(dk_sum)
         dv_sum[...] = jnp.zeros_like(dv_sum)
-        for at in range(pair.shape[0]):
+        for at in range(near_key.shape[0]):
             span = slice(at * rows, (at + 1) * rows)
             for keys, values, *_ in bufs:
-                keys[span] = pair[at, 0]
-                values[span] = pair[at, 1]
-            key_flip[:, span] = pair[at, 0].T
+                keys[span] = near_key[at]
+                values[span] = near_value[at]
+            key_flip[:, span] = near_key[at].T
 
     def spots_at(index):
         one = listed[index]
@@ -248,33 +248,34 @@
         return carry
 
     lax.fori_loop(0, found, finish, 0)
-    for at in range(pair.shape[0]):
+    for at in range(near_key.shape[0]):
         span = slice(at * rows, (at + 1) * rows)
-        term[at, 0] = key_sum[span].astype(term.dtype)
-        term[at, 1] = value_sum[span].astype(term.dtype)
+        key_term[at] = key_sum[span].astype(key_term.dtype)
+        value_term[at] = value_sum[span].astype(value_term.dtype)
 
 
 def near_grads(code, pair, plan, prepared, comp_key, comp_value, chain, shape, kind):
     count, slots, width = shape
     lanes = 2 * HALF * (width // HD)
-    prefix = pair.shape[0] * pair.shape[2]
+    prefix = pair[0].shape[0] * pair[0].shape[1]
     extent = prefix + 2 * slots
     vmem = pl.BlockSpec(memory_space=pltpu.VMEM)
     narrow = jax.ShapeDtypeStruct(comp_key.shape, jnp.bfloat16)
-    operands = [plan, *prepared, comp_key, comp_value, pair]
+    operands = [plan, *prepared, comp_key, comp_value, *pair]
     if chain is not None:
         operands += list(chain)
     work = 4
     out = pl.pallas_call(
         functools.partial(near_kernel, code, chain is not None),
         out_shape=[
-            jax.ShapeDtypeStruct(pair.shape, kind),
+            jax.ShapeDtypeStruct(pair[0].shape, kind),
+            jax.ShapeDtypeStruct(pair[0].shape, kind),
             jax.ShapeDtypeStruct(shape, jnp.bfloat16),
             narrow,
             narrow,
         ],
         in_specs=[pl.BlockSpec(memory_space=pltpu.SMEM)] + [vmem] * (len(operands) - 1),
-        out_specs=[vmem] * 4,
+        out_specs=[vmem] * 5,
         scratch_shapes=[
             pltpu.VMEM(comp_key.shape, jnp.float32),
             pltpu.VMEM(comp_key.shape, jnp.float32),
@@ -299,7 +300,7 @@
             transcendentals=work * extent * lanes,
         ),
     )(*operands)
-    return out[0], out[1:]
+    return out[:2], out[2:]
 
 
 SMALL = pltpu.CompilerParams(vmem_limit_bytes=4 * 2**20)
@@ -320,17 +321,38 @@
     )(key, value)
 
 
-def join_kernel(pair, key, value):
-    for head in range(pair.shape[0]):
+def part_kernel(pair, key, value):
+    key[...] = pair[:, 0]
+    value[...] = pair[:, 1]
+
+
+def parted(pair):
+    shards, _, rows, _ = pair.shape
+    half = jax.ShapeDtypeStruct((shards, rows, HD), pair.dtype)
+    return pl.pallas_call(part_kernel, out_shape=[half, half], compiler_params=SMALL)(pair)
+
+
+def join_kernel(key_parts, value_parts, key, value):
+    for head in range(key_parts.shape[0]):
         columns = slice(head * HD, (head + 1) * HD)
-        key[:, columns] = pair[head, 0]
-        value[:, columns] = pair[head, 1]
-
-
-def join_heads(pair):
-    shards, _, rows, _ = pair.shape
-    whole = jax.ShapeDtypeStruct((rows, shards * HD), pair.dtype)
-    return pl.pallas_call(join_kernel, out_shape=[whole, whole], compiler_params=SMALL)(pair)
+        key[:, columns] = key_parts[head]
+        value[:, columns] = value_parts[head]
+
+
+def join_heads(key_parts, value_parts):
+    shards, rows, _ = key_parts.shape
+    whole = jax.ShapeDtypeStruct((rows, shards * HD), key_parts.dtype)
+    return pl.pallas_call(join_kernel, out_shape=[whole, whole], compiler_params=SMALL)(
+        key_parts, value_parts
+    )
+
+
+def wide(terms):
+    return [term.astype(jnp.float32) for term in terms]
+
+
+def added(*terms):
+    return [sum(parts).astype(jnp.bfloat16) for parts in zip(*terms)]
 
 
 def swapped(value, first):
@@ -338,6 +360,11 @@
     return lax.ppermute(
         value, "dp", [(at, (at + (1 if at % 2 == first else -1)) % size) for at in range(size)]
     )
+
+
+def exchanged(for_even, for_odd):
+    parts = [(swapped(one, 0), swapped(other, 1)) for one, other in zip(for_even, for_odd)]
+    return [one for one, _ in parts], [other for _, other in parts]
 
 
 def per_device(
@@ -352,14 +379,12 @@
     near = jnp.where(position % 2 == 0, near, 4 - near)
 
     pair = split_heads(prefix_key[0], prefix_value[0], shards)
-    own = lax.all_to_all(pair, "mp", split_axis=0, concat_axis=0, tiled=True)
-    even_one = swapped(own, 0)
-    odd_one = swapped(own, 1)
+    own = parted(lax.all_to_all(pair, "mp", split_axis=0, concat_axis=0, tiled=True))
+    even_one, odd_one = exchanged(own, own)
     plan = near * 64 + lengths
     prepared = prepare(lengths, query, grad_out)
-    even_one, prepared = lax.optimization_barrier((even_one, prepared))
-    odd_two = swapped(even_one, 1)
-    even_two = swapped(odd_one, 0)
+    even_one[0], prepared = lax.optimization_barrier((even_one[0], prepared))
+    even_two, odd_two = exchanged(odd_one, even_one)
 
     def grads(code, pair, chain, kind):
         return near_grads(code, pair, plan, prepared, comp_key, comp_value, chain, query.shape, kind)
@@ -367,19 +392,18 @@
     odd_two_term, chain = grads(0, odd_two, None, jnp.bfloat16)
     even_two_term, chain = grads(4, even_two, chain, jnp.bfloat16)
     odd_two_term, even_two_term = lax.optimization_barrier((odd_two_term, even_two_term))
-    even_back = swapped(odd_two_term, 1).astype(jnp.float32)
-    odd_back = swapped(even_two_term, 0).astype(jnp.float32)
+    odd_back, even_back = exchanged(even_two_term, odd_two_term)
     odd_term, chain = grads(1, odd_one, chain, jnp.float32)
     even_term, chain = grads(3, even_one, chain, jnp.float32)
-    even_sum = (even_term + even_back).astype(jnp.bfloat16)
-    odd_sum = (odd_term + odd_back).astype(jnp.bfloat16)
+    even_sum = added(even_term, wide(even_back))
+    odd_sum = added(odd_term, wide(odd_back))
+    even_back, odd_back = exchanged(even_sum, odd_sum)
     odd_sum, even_sum, chain = lax.optimization_barrier((odd_sum, even_sum, chain))
-    even_back = swapped(even_sum, 0).astype(jnp.float32)
-    odd_back = swapped(odd_sum, 1).astype(jnp.float32)
     own_term, chain = grads(2, own, chain, jnp.float32)
-    gathered = (own_term + even_back + odd_back).astype(jnp.bfloat16)
-    back = lax.all_to_all(gathered, "mp", split_axis=0, concat_axis=0, tiled=True)
-    key_back, value_back = join_heads(back)
+    gathered = added(own_term, wide(even_back), wide(odd_back))
+    key_back, value_back = join_heads(
+        *(lax.all_to_all(part, "mp", split_axis=0, concat_axis=0, tiled=True) for part in gathered)
+    )
     return chain[0], chain[1], chain[2], key_back[None], value_back[None]
 
 

time: 124 us -> 144 us (1.16)
  starting transfers between devices: 38.7 us -> 67.9 us
  waiting for transfers between devices: 16.4 us -> 8.7 us
  blocking collectives: 35 us -> 28.7 us
  other arithmetic: 0.69 us -> 3.77 us
    ppermute x8 -> x16, starting transfers between devices: 38.7 us -> 58.8 us  [swapped(): lax.ppermute(value, 'dp', [(at, (at + (1 if at % 2 == first else -1)) % s...]
    ppermute x8 -> x16, waiting for transfers between devices: 16.4 us -> 3.32 us  [swapped(): lax.ppermute(value, 'dp', [(at, (at + (1 if at % 2 == first else -1)) % s...]
    all_to_all x0 -> x1, starting transfers between devices: none -> 9.15 us  [per_device(): lax.all_to_all(part, 'mp', split_axis=0, concat_axis=0, tiled=True)]
    all_to_all x2, blocking collectives: 35 us -> 28.7 us  [the longest x1 18.8 us: per_device(): lax.all_to_all(pair, 'mp', split_axis=0, concat_axis=0, tiled=True)]
    all_to_all x0 -> x1, waiting for transfers between devices: none -> 5.38 us  [per_device(): lax.all_to_all(part, 'mp', split_axis=0, concat_axis=0, tiled=True)]
    convert_element_type x3 -> x6, other arithmetic: 0.49 us -> 3.57 us  [added(): return [sum(parts).astype(jnp.bfloat16) for parts in zip(*terms)]]
  transfers between devices with their start and end apart: 8 -> 17, of which waited for: 3 -> 2; matrix products, arithmetic and copies ran while one was open for 0% -> 3% of each run, Pallas kernels for 19% -> 16%
where the time goes in v5:
time: 144 us; the launch traced here: 142 us
  starting transfers between devices  67.9 us (47%)
  blocking collectives  28.7 us (20%)
  Pallas kernels  26.8 us (19%)
  waiting for transfers between devices  8.7 us (6%)
  local copies, waits for them, and re-layouts  4.92 us (3%)
  other arithmetic  3.77 us (3%)
    ppermute x16, starting transfers between devices, swapped(): lax.ppermute(value, 'dp', [(at, (at + (1 if at % 2 == first else -1)) % s...  58.8 us
    pallas_call x5, Pallas kernels, near_grads(): pl.pallas_call(functools.partial(near_kernel, code, chain is not None), o...  22.9 us
    all_to_all x1, blocking collectives, per_device(): lax.all_to_all(pair, 'mp', split_axis=0, concat_axis=0, tiled=True)  18.8 us
    all_to_all x1, blocking collectives, per_device(): lax.all_to_all(part, 'mp', split_axis=0, concat_axis=0, tiled=True)  9.93 us
    all_to_all x1, starting transfers between devices, per_device(): lax.all_to_all(part, 'mp', split_axis=0, concat_axis=0, tiled=True)  9.15 us
    all_to_all x1, waiting for transfers between devices, per_device(): lax.all_to_all(part, 'mp', split_axis=0, concat_axis=0, tiled=True)  5.38 us
    unnamed x26, local copies, waits for them, and re-layouts  4.92 us
    convert_element_type x6, other arithmetic, added(): return [sum(parts).astype(jnp.bfloat16) for parts in zip(*terms)]  3.57 us
  transfers between devices with their start and end apart: 17, of which 2 were waited for; matrix products, arithmetic and copies ran while one was open for 3% of the time, Pallas kernels for 16%

profile of v5, /device:TPU:1, one launch (start us, length us, event | category | flops | bytes accessed | tf_op | source)
XLA Modules:
  0.0 141.8 jit_solution(16553198037530837288)
XLA Ops:
  0.6 0.0 copy-start.8
  0.6 0.9 copy-done.8
  1.6 0.9 copy-done.9
  2.5 0.1 shard_map.128
  2.6 18.8 %all_to_all.15.pair = bf16[8,2,128,128]{3,2,1,0:T(8,128)(2,1)S(1)} all-to-all(bf16[8,2,128,128]{3,2,1,0:T(8,128)(2,1)S(1)} %shard_map.128), channel_id=1, replica_groups=mesh['dp'=64,'mp'=8] {'mp'}, dimensions={0} | all-to-all | bytes 1048576 | tf_op jit(solution)/shard_map/all_to_all | solution.py:382
  21.4 0.8 shard_map.129
  22.2 2.1 %collective-permute-start = (bf16[8,128,128]{2,1,0:T(8,128)(2,1)}, bf16[8,128,128]{2,1,0:T(8,128)(2,1)}, u32[]{:S(2)}, u32[]{:S(2)}) collective-permute-start(bf16[8,128,128]{2,1,0:T(8,128)(2,1)} %get-tuple-element.50.near_key), channel_id=1, source_target_pairs={{0,8},{8,0},{16,24},{24,16},{32,40},{40,32},{48,56},{56,48},{64,72... | collective-permute-start | bytes 786440 | tf_op jit(solution)/shard_map/ppermute | solution.py:360
  24.3 3.4 %collective-permute-start.6 = (bf16[8,128,128]{2,1,0:T(8,128)(2,1)}, bf16[8,128,128]{2,1,0:T(8,128)(2,1)}, u32[]{:S(2)}, u32[]{:S(2)}) collective-permute-start(bf16[8,128,128]{2,1,0:T(8,128)(2,1)} %get-tuple-element.59.near_value), channel_id=1, source_target_pairs={{0,8},{8,0},{16,24},{24,16},{32,40},{40,32},{48,56},{56,48},{64,72... | collective-permute-start | bytes 786440 | tf_op jit(solution)/shard_map/ppermute | solution.py:360
  27.7 9.8 %collective-permute-start.1 = (bf16[8,128,128]{2,1,0:T(8,128)(2,1)}, bf16[8,128,128]{2,1,0:T(8,128)(2,1)}, u32[]{:S(2)}, u32[]{:S(2)}) collective-permute-start(bf16[8,128,128]{2,1,0:T(8,128)(2,1)} %get-tuple-element.50.near_key), channel_id=1, source_target_pairs={{0,504},{8,16},{16,8},{24,32},{32,24},{40,48},{48,40},{56,64},{64,... | collective-permute-start | bytes 786440 | tf_op jit(solution)/shard_map/ppermute | solution.py:360
  37.5 1.9 %collective-permute-start.2 = (bf16[8,128,128]{2,1,0:T(8,128)(2,1)}, bf16[8,128,128]{2,1,0:T(8,128)(2,1)}, u32[]{:S(2)}, u32[]{:S(2)}) collective-permute-start(bf16[8,128,128]{2,1,0:T(8,128)(2,1)} %get-tuple-element.59.near_value), channel_id=1, source_target_pairs={{0,504},{8,16},{16,8},{24,32},{32,24},{40,48},{48,40},{56,64},{64,... | collective-permute-start | bytes 786440 | tf_op jit(solution)/shard_map/ppermute | solution.py:360
  39.4 0.0 copy-done.4
  39.4 0.0 copy-done.5
  39.4 0.0 copy-done.10
  39.5 2.0 %shard_map.130 = (bf16[33,128,128]{2,1,0:T(8,128)(2,1)S(1)}, bf16[33,128,128]{2,1,0:T(8,128)(2,1)S(1)}, bf16[33,128,128]{2,1,0:T(8,128)(2,1)S(1)}, bf16[33,128,128]{2,1,0:T(8,128)(2,1)S(1)}) custom-call(s32[16]{0:T(128)S(1)} %copy-done.10, bf16[16,32,1024]{2,1,0:T(8,128)(2,1)S(1)} %copy-done.4, bf16[16,32,1024]{2,1,0:T(8,128)(2,1)S(1)} %copy-done.5), custom_call_target="tpu_custom_call" | custom-call | bytes 6291456 | tf_op jit(solution)/shard_map/pallas_call | solution.py:64
  41.5 0.0 copy-start
  41.5 1.0 copy-done
  42.5 0.0 collective-permute-done.near_key
  42.5 6.7 %collective-permute-start.5 = (bf16[8,128,128]{2,1,0:T(8,128)(2,1)}, bf16[8,128,128]{2,1,0:T(8,128)(2,1)}, u32[]{:S(2)}, u32[]{:S(2)}) collective-permute-start(bf16[8,128,128]{2,1,0:T(8,128)(2,1)} %collective-permute-done.near_key), channel_id=1, source_target_pairs={{0,504},{8,16},{16,8},{24,32},{32,24},{40,48},{48,40},{56,64},{64,... | collective-permute-start | bytes 786440 | tf_op jit(solution)/shard_map/ppermute | solution.py:360
  49.2 0.0 collective-permute-done.6.near_value
  49.2 1.9 %collective-permute-start.7 = (bf16[8,128,128]{2,1,0:T(8,128)(2,1)}, bf16[8,128,128]{2,1,0:T(8,128)(2,1)}, u32[]{:S(2)}, u32[]{:S(2)}) collective-permute-start(bf16[8,128,128]{2,1,0:T(8,128)(2,1)} %collective-permute-done.6.near_value), channel_id=1, source_target_pairs={{0,504},{8,16},{16,8},{24,32},{32,24},{40,48},{48,40},{56,64},{64,... | collective-permute-start | bytes 786440 | tf_op jit(solution)/shard_map/ppermute | solution.py:360
  51.1 0.0 copy-done.11
  51.1 0.2 select_reduce_fusion
  51.3 0.0 collective-permute-done.1.near_key
  51.3 1.9 %collective-permute-start.3 = (bf16[8,128,128]{2,1,0:T(8,128)(2,1)}, bf16[8,128,128]{2,1,0:T(8,128)(2,1)S(1)}, u32[]{:S(2)}, u32[]{:S(2)}) collective-permute-start(bf16[8,128,128]{2,1,0:T(8,128)(2,1)} %collective-permute-done.1.near_key), channel_id=1, source_target_pairs={{0,8},{8,0},{16,24},{24,16},{32,40},{40,32},{48,56},{56,48},{64,72... | collective-permute-start | bytes 786440 | tf_op jit(solution)/shard_map/ppermute | solution.py:360
  53.3 0.0 collective-permute-done.2.near_value
  53.3 3.4 %collective-permute-start.4 = (bf16[8,128,128]{2,1,0:T(8,128)(2,1)}, bf16[8,128,128]{2,1,0:T(8,128)(2,1)S(1)}, u32[]{:S(2)}, u32[]{:S(2)}) collective-permute-start(bf16[8,128,128]{2,1,0:T(8,128)(2,1)} %collective-permute-done.2.near_value), channel_id=1, source_target_pairs={{0,8},{8,0},{16,24},{24,16},{32,40},{40,32},{48,56},{56,48},{64,72... | collective-permute-start | bytes 786440 | tf_op jit(solution)/shard_map/ppermute | solution.py:360
  56.7 3.3 %collective-permute-done.7.near_value = bf16[8,128,128]{2,1,0:T(8,128)(2,1)} collective-permute-done((bf16[8,128,128]{2,1,0:T(8,128)(2,1)}, bf16[8,128,128]{2,1,0:T(8,128)(2,1)}, u32[]{:S(2)}, u32[]{:S(2)}) %collective-permute-start.7) | collective-permute-done | bytes 262176 | tf_op jit(solution)/shard_map/ppermute | solution.py:360
  59.9 0.0 collective-permute-done.5.near_key
  59.9 0.0 copy-done.2
  60.0 1.2 copy-done.1
  61.2 6.1 %shard_map.131 = (bf16[8,128,128]{2,1,0:T(8,128)(2,1)S(1)}, bf16[8,128,128]{2,1,0:T(8,128)(2,1)S(1)}, bf16[16,32,1024]{2,1,0:T(8,128)(2,1)S(1)}, bf16[16,32,128]...) custom-call(s32[16]{0:T(128)S(1)} %multiply_add_fusion.plan, bf16[33,128,128]{2,1,0:T(8,128)(2,1)S(1)} %get-tuple-element.55.query_rows, ...), custom_call_target="tpu_custom_call" | custom-call | flops 1711276032 | bytes 1310720 | tf_op jit(solution)/shard_map/pallas_call | solution.py:268
  67.3 0.0 collective-permute-done.3.near_key
  67.3 0.0 collective-permute-done.4.near_value
  67.4 2.3 %shard_map.132 = (bf16[8,128,128]{2,1,0:T(8,128)(2,1)S(1)}, bf16[8,128,128]{2,1,0:T(8,128)(2,1)S(1)}, bf16[16,32,1024]{2,1,0:T(8,128)(2,1)S(1)}, bf16[16,32,128]...) custom-call(s32[16]{0:T(128)S(1)} %multiply_add_fusion.plan, bf16[33,128,128]{2,1,0:T(8,128)(2,1)S(1)} %get-tuple-element.55.query_rows, ...), custom_call_target="tpu_custom_call" | custom-call | flops 1711276032 | bytes 1310720 | tf_op jit(solution)/shard_map/pallas_call | solution.py:268
  69.7 1.9 %collective-permute-start.8 = (bf16[8,128,128]{2,1,0:T(8,128)(2,1)S(1)}, bf16[8,128,128]{2,1,0:T(8,128)(2,1)S(1)}, u32[]{:S(2)}, u32[]{:S(2)}) collective-permute-start(bf16[8,128,128]{2,1,0:T(8,128)(2,1)S(1)} %get-tuple-element.72), channel_id=1, source_target_pairs={{0,8},{8,0},{16,24},{24,16},{32,40},{40,32},{48,56},{56,48},{64,72... | collective-permute-start | bytes 786440 | tf_op jit(solution)/shard_map/ppermute | solution.py:360
  71.6 3.4 %collective-permute-start.9 = (bf16[8,128,128]{2,1,0:T(8,128)(2,1)S(1)}, bf16[8,128,128]{2,1,0:T(8,128)(2,1)S(1)}, u32[]{:S(2)}, u32[]{:S(2)}) collective-permute-start(bf16[8,128,128]{2,1,0:T(8,128)(2,1)S(1)} %get-tuple-element.74), channel_id=1, source_target_pairs={{0,8},{8,0},{16,24},{24,16},{32,40},{40,32},{48,56},{56,48},{64,72... | collective-permute-start | bytes 786440 | tf_op jit(solution)/shard_map/ppermute | solution.py:360
  75.0 6.0 %collective-permute-start.10 = (bf16[8,128,128]{2,1,0:T(8,128)(2,1)S(1)}, bf16[8,128,128]{2,1,0:T(8,128)(2,1)S(1)}, u32[]{:S(2)}, u32[]{:S(2)}) collective-permute-start(bf16[8,128,128]{2,1,0:T(8,128)(2,1)S(1)} %get-tuple-element.79), channel_id=1, source_target_pairs={{0,504},{8,16},{16,8},{24,32},{32,24},{40,48},{48,40},{56,64},{64,... | collective-permute-start | bytes 786440 | tf_op jit(solution)/shard_map/ppermute | solution.py:360
  81.0 2.6 %collective-permute-start.11 = (bf16[8,128,128]{2,1,0:T(8,128)(2,1)S(1)}, bf16[8,128,128]{2,1,0:T(8,128)(2,1)S(1)}, u32[]{:S(2)}, u32[]{:S(2)}) collective-permute-start(bf16[8,128,128]{2,1,0:T(8,128)(2,1)S(1)} %get-tuple-element.81), channel_id=1, source_target_pairs={{0,504},{8,16},{16,8},{24,32},{32,24},{40,48},{48,40},{56,64},{64,... | collective-permute-start | bytes 786440 | tf_op jit(solution)/shard_map/ppermute | solution.py:360
  83.6 5.4 %shard_map.133 = (f32[8,128,128]{2,1,0:T(8,128)S(1)}, f32[8,128,128]{2,1,0:T(8,128)S(1)}, bf16[16,32,1024]{2,1,0:T(8,128)(2,1)S(1)}, bf16[16,32,128]{2,1,0:T(8,128)(2,1)S(1)}, bf16[16,32,128]{2,1,0:T(8,128)(2,1)S(1)}) custom-call(s32[16]{0:T(128)S(1)} %multiply_add_fusion.plan, bf16[33,128,128]{2,1,0:T(8,128)(2,1)S(1)} %get-tuple-element.55.query_rows, ...), custom_call_target="tpu_custom_call" | custom-call | flops 1711276032 | bytes 1310720 | tf_op jit(solution)/shard_map/pallas_call | solution.py:268
  89.0 2.8 %shard_map.134 = (f32[8,128,128]{2,1,0:T(8,128)S(1)}, f32[8,128,128]{2,1,0:T(8,128)S(1)}, bf16[16,32,1024]{2,1,0:T(8,128)(2,1)S(1)}, bf16[16,32,128]{2,1,0:T(8,128)(2,1)S(1)}, bf16[16,32,128]{2,1,0:T(8,128)(2,1)S(1)}) custom-call(s32[16]{0:T(128)S(1)} %multiply_add_fusion.plan, bf16[33,128,128]{2,1,0:T(8,128)(2,1)S(1)} %get-tuple-element.55.query_rows, ...), custom_call_target="tpu_custom_call" | custom-call | flops 1711276032 | bytes 1310720 | tf_op jit(solution)/shard_map/pallas_call | solution.py:268
  91.8 0.0 collective-permute-done.9
  91.8 0.1 add_convert_fusion.4
  91.9 4.7 %collective-permute-start.15 = (bf16[8,128,128]{2,1,0:T(8,128)(2,1)S(1)}, bf16[8,128,128]{2,1,0:T(8,128)(2,1)S(1)}, u32[]{:S(2)}, u32[]{:S(2)}) collective-permute-start(bf16[8,128,128]{2,1,0:T(8,128)(2,1)S(1)} %add_convert_fusion.4), channel_id=1, source_target_pairs={{0,504},{8,16},{16,8},{24,32},{32,24},{40,48},{48,40},{56,64},{64,... | collective-permute-start | bytes 786440 | tf_op jit(solution)/shard_map/ppermute | solution.py:360
  96.6 0.0 collective-permute-done.8
  96.6 0.8 add_convert_fusion.5
  97.4 3.9 %collective-permute-start.13 = (bf16[8,128,128]{2,1,0:T(8,128)(2,1)}, bf16[8,128,128]{2,1,0:T(8,128)(2,1)}, u32[]{:S(2)}, u32[]{:S(2)}) collective-permute-start(bf16[8,128,128]{2,1,0:T(8,128)(2,1)} %add_convert_fusion.5), channel_id=1, source_target_pairs={{0,504},{8,16},{16,8},{24,32},{32,24},{40,48},{48,40},{56,64},{64,... | collective-permute-start | bytes 786440 | tf_op jit(solution)/shard_map/ppermute | solution.py:360
  101.3 0.0 collective-permute-done.11
  101.3 0.1 add_convert_fusion.2
  101.4 1.9 %collective-permute-start.14 = (bf16[8,128,128]{2,1,0:T(8,128)(2,1)S(1)}, bf16[8,128,128]{2,1,0:T(8,128)(2,1)S(1)}, u32[]{:S(2)}, u32[]{:S(2)}) collective-permute-start(bf16[8,128,128]{2,1,0:T(8,128)(2,1)S(1)} %add_convert_fusion.2), channel_id=1, source_target_pairs={{0,8},{8,0},{16,24},{24,16},{32,40},{40,32},{48,56},{56,48},{64,72... | collective-permute-start | bytes 786440 | tf_op jit(solution)/shard_map/ppermute | solution.py:360
  103.3 0.0 collective-permute-done.10
  103.3 0.8 add_convert_fusion.3
  104.1 3.4 %collective-permute-start.12 = (bf16[8,128,128]{2,1,0:T(8,128)(2,1)}, bf16[8,128,128]{2,1,0:T(8,128)(2,1)}, u32[]{:S(2)}, u32[]{:S(2)}) collective-permute-start(bf16[8,128,128]{2,1,0:T(8,128)(2,1)} %add_convert_fusion.3), channel_id=1, source_target_pairs={{0,8},{8,0},{16,24},{24,16},{32,40},{40,32},{48,56},{56,48},{64,72... | collective-permute-start | bytes 786440 | tf_op jit(solution)/shard_map/ppermute | solution.py:360
  107.4 6.2 %shard_map.135 = (f32[8,128,128]{2,1,0:T(8,128)S(1)}, f32[8,128,128]{2,1,0:T(8,128)S(1)}, bf16[16,32,1024]{2,1,0:T(8,128)(2,1)}, bf16[16,32,128]{2,1,0:T(8,128)(2,1)}, bf16[16,32,128]{2,1,0:T(8,128)(2,1)}) custom-call(s32[16]{0:T(128)S(1)} %multiply_add_fusion.plan, bf16[33,128,128]{2,1,0:T(8,128)(2,1)S(1)} %get-tuple-element.55.query_rows, ...), custom_call_target="tpu_custom_call" | custom-call | flops 1711276032 | bytes 1310720 | tf_op jit(solution)/shard_map/pallas_call | solution.py:268
  113.6 0.8 copy-done.6
  114.4 0.0 collective-permute-done.15
  114.4 0.0 collective-permute-done.14
  114.4 0.8 add_convert_fusion
  115.2 9.2 %all-to-all-start.2 = ((bf16[8,128,128]{2,1,0:T(8,128)(2,1)}), bf16[8,128,128]{2,1,0:T(8,128)(2,1)S(1)}, u32[]{:S(2)}, u32[]{:S(2)}) async-start(bf16[8,128,128]{2,1,0:T(8,128)(2,1)} %add_convert_fusion), calls=%async_computation.2 | async-start | bytes 524288 | tf_op jit(solution)/shard_map/all_to_all | solution.py:405
  124.4 0.0 collective-permute-done.13
  124.4 0.0 collective-permute-done.12
  124.4 1.1 add_convert_fusion.1
  125.5 5.4 %all-to-all-done.2.value_parts = bf16[8,128,128]{2,1,0:T(8,128)(2,1)S(1)} async-done(((bf16[8,128,128]{2,1,0:T(8,128)(2,1)}), bf16[8,128,128]{2,1,0:T(8,128)(2,1)S(1)}, u32[]{:S(2)}, u32[]{:S(2)}) %all-to-all-start.2) | async-done | bytes 262176 | tf_op jit(solution)/shard_map/all_to_all | solution.py:405
  130.9 9.9 %all_to_all.16.key_parts = bf16[8,128,128]{2,1,0:T(8,128)(2,1)S(1)} all-to-all(bf16[8,128,128]{2,1,0:T(8,128)(2,1)S(1)} %add_convert_fusion.1), channel_id=1, replica_groups=mesh['dp'=64,'mp'=8] {'mp'}, dimensions={0} | all-to-all | bytes 524288 | tf_op jit(solution)/shard_map/all_to_all | solution.py:405
  140.8 0.9 shard_map.136
  (15 shorter events, 0.0 us)
Async XLA Ops:
  0.6 1.0 copy-start.8
  1.6 0.9 copy-start.9
  2.5 36.9 %copy-start.4 = (bf16[16,32,1024]{2,1,0:T(8,128)(2,1)S(1)}, bf16[16,32,1024]{2,1,0:T(8,128)(2,1)}, u32[]{:S(2)}) copy-start(bf16[16,32,1024]{2,1,0:T(8,128)(2,1)} %query.1) | copy-start | bytes 3145732
  2.5 36.9 %copy-start.5 = (bf16[16,32,1024]{2,1,0:T(8,128)(2,1)S(1)}, bf16[16,32,1024]{2,1,0:T(8,128)(2,1)}, u32[]{:S(2)}) copy-start(bf16[16,32,1024]{2,1,0:T(8,128)(2,1)} %grad_out.1) | copy-start | bytes 3145732
  2.5 36.9 %copy-start.10 = (s32[16]{0:T(128)S(1)}, s32[16]{0:T(128)}, u32[]{:S(2)}) copy-start(s32[16]{0:T(128)} %lengths.1) | copy-start | bytes 196
  22.2 28.9 %copy-start.11 = (s32[64]{0:T(128)S(1)}, s32[64]{0:T(128)}, u32[]{:S(2)}) copy-start(s32[64]{0:T(128)} %param.15) | copy-start | bytes 772
  22.2 28.9 %copy-start.12 = (s32[16]{0:T(128)S(1)}, s32[16]{0:T(128)}, u32[]{:S(2)}) copy-start(s32[16]{0:T(128)} %param.16) | copy-start | bytes 196
  22.2 37.7 %copy-start.2 = (bf16[16,32,128]{2,1,0:T(8,128)(2,1)S(1)}, bf16[16,32,128]{2,1,0:T(8,128)(2,1)}, u32[]{:S(2)}) copy-start(bf16[16,32,128]{2,1,0:T(8,128)(2,1)} %comp_key.9) | copy-start | bytes 393220
  22.2 37.7 %copy-start.3 = (bf16[16,32,128]{2,1,0:T(8,128)(2,1)S(1)}, bf16[16,32,128]{2,1,0:T(8,128)(2,1)}, u32[]{:S(2)}) copy-start(bf16[16,32,128]{2,1,0:T(8,128)(2,1)} %comp_value.9) | copy-start | bytes 393220
  22.2 20.2 %collective-permute-start = (bf16[8,128,128]{2,1,0:T(8,128)(2,1)}, bf16[8,128,128]{2,1,0:T(8,128)(2,1)}, u32[]{:S(2)}, u32[]{:S(2)}) collective-permute-start(bf16[8,128,128]{2,1,0:T(8,128)(2,1)} %get-tuple-element.50.near_key), channel_id=1, source_target_pairs={{0,8},{8,0},{16,24},{24,16},{32,40},{40,32},{48,56},{56,48},{64,72... | collective-permute-start | bytes 786440 | tf_op jit(solution)/shard_map/ppermute | solution.py:360
  24.3 24.9 %collective-permute-start.6 = (bf16[8,128,128]{2,1,0:T(8,128)(2,1)}, bf16[8,128,128]{2,1,0:T(8,128)(2,1)}, u32[]{:S(2)}, u32[]{:S(2)}) collective-permute-start(bf16[8,128,128]{2,1,0:T(8,128)(2,1)} %get-tuple-element.59.near_value), channel_id=1, source_target_pairs={{0,8},{8,0},{16,24},{24,16},{32,40},{40,32},{48,56},{56,48},{64,72... | collective-permute-start | bytes 786440 | tf_op jit(solution)/shard_map/ppermute | solution.py:360
  27.7 23.6 %collective-permute-start.1 = (bf16[8,128,128]{2,1,0:T(8,128)(2,1)}, bf16[8,128,128]{2,1,0:T(8,128)(2,1)}, u32[]{:S(2)}, u32[]{:S(2)}) collective-permute-start(bf16[8,128,128]{2,1,0:T(8,128)(2,1)} %get-tuple-element.50.near_key), channel_id=1, source_target_pairs={{0,504},{8,16},{16,8},{24,32},{32,24},{40,48},{48,40},{56,64},{64,... | collective-permute-start | bytes 786440 | tf_op jit(solution)/shard_map/ppermute | solution.py:360
  37.5 15.8 %collective-permute-start.2 = (bf16[8,128,128]{2,1,0:T(8,128)(2,1)}, bf16[8,128,128]{2,1,0:T(8,128)(2,1)}, u32[]{:S(2)}, u32[]{:S(2)}) collective-permute-start(bf16[8,128,128]{2,1,0:T(8,128)(2,1)} %get-tuple-element.59.near_value), channel_id=1, source_target_pairs={{0,504},{8,16},{16,8},{24,32},{32,24},{40,48},{48,40},{56,64},{64,... | collective-permute-start | bytes 786440 | tf_op jit(solution)/shard_map/ppermute | solution.py:360
  41.5 1.0 copy-start
  42.5 17.4 %collective-permute-start.5 = (bf16[8,128,128]{2,1,0:T(8,128)(2,1)}, bf16[8,128,128]{2,1,0:T(8,128)(2,1)}, u32[]{:S(2)}, u32[]{:S(2)}) collective-permute-start(bf16[8,128,128]{2,1,0:T(8,128)(2,1)} %collective-permute-done.near_key), channel_id=1, source_target_pairs={{0,504},{8,16},{16,8},{24,32},{32,24},{40,48},{48,40},{56,64},{64,... | collective-permute-start | bytes 786440 | tf_op jit(solution)/shard_map/ppermute | solution.py:360
  49.2 10.8 %collective-permute-start.7 = (bf16[8,128,128]{2,1,0:T(8,128)(2,1)}, bf16[8,128,128]{2,1,0:T(8,128)(2,1)}, u32[]{:S(2)}, u32[]{:S(2)}) collective-permute-start(bf16[8,128,128]{2,1,0:T(8,128)(2,1)} %collective-permute-done.6.near_value), channel_id=1, source_target_pairs={{0,504},{8,16},{16,8},{24,32},{32,24},{40,48},{48,40},{56,64},{64,... | collective-permute-start | bytes 786440 | tf_op jit(solution)/shard_map/ppermute | solution.py:360
  51.3 16.0 %collective-permute-start.3 = (bf16[8,128,128]{2,1,0:T(8,128)(2,1)}, bf16[8,128,128]{2,1,0:T(8,128)(2,1)S(1)}, u32[]{:S(2)}, u32[]{:S(2)}) collective-permute-start(bf16[8,128,128]{2,1,0:T(8,128)(2,1)} %collective-permute-done.1.near_key), channel_id=1, source_target_pairs={{0,8},{8,0},{16,24},{24,16},{32,40},{40,32},{48,56},{56,48},{64,72... | collective-permute-start | bytes 786440 | tf_op jit(solution)/shard_map/ppermute | solution.py:360
  53.3 14.1 %collective-permute-start.4 = (bf16[8,128,128]{2,1,0:T(8,128)(2,1)}, bf16[8,128,128]{2,1,0:T(8,128)(2,1)S(1)}, u32[]{:S(2)}, u32[]{:S(2)}) collective-permute-start(bf16[8,128,128]{2,1,0:T(8,128)(2,1)} %collective-permute-done.2.near_value), channel_id=1, source_target_pairs={{0,8},{8,0},{16,24},{24,16},{32,40},{40,32},{48,56},{56,48},{64,72... | collective-permute-start | bytes 786440 | tf_op jit(solution)/shard_map/ppermute | solution.py:360
  59.9 1.2 copy-start.1
  69.7 26.9 %collective-permute-start.8 = (bf16[8,128,128]{2,1,0:T(8,128)(2,1)S(1)}, bf16[8,128,128]{2,1,0:T(8,128)(2,1)S(1)}, u32[]{:S(2)}, u32[]{:S(2)}) collective-permute-start(bf16[8,128,128]{2,1,0:T(8,128)(2,1)S(1)} %get-tuple-element.72), channel_id=1, source_target_pairs={{0,8},{8,0},{16,24},{24,16},{32,40},{40,32},{48,56},{56,48},{64,72... | collective-permute-start | bytes 786440 | tf_op jit(solution)/shard_map/ppermute | solution.py:360
  71.6 20.2 %collective-permute-start.9 = (bf16[8,128,128]{2,1,0:T(8,128)(2,1)S(1)}, bf16[8,128,128]{2,1,0:T(8,128)(2,1)S(1)}, u32[]{:S(2)}, u32[]{:S(2)}) collective-permute-start(bf16[8,128,128]{2,1,0:T(8,128)(2,1)S(1)} %get-tuple-element.74), channel_id=1, source_target_pairs={{0,8},{8,0},{16,24},{24,16},{32,40},{40,32},{48,56},{56,48},{64,72... | collective-permute-start | bytes 786440 | tf_op jit(solution)/shard_map/ppermute | solution.py:360
  75.0 28.3 %collective-permute-start.10 = (bf16[8,128,128]{2,1,0:T(8,128)(2,1)S(1)}, bf16[8,128,128]{2,1,0:T(8,128)(2,1)S(1)}, u32[]{:S(2)}, u32[]{:S(2)}) collective-permute-start(bf16[8,128,128]{2,1,0:T(8,128)(2,1)S(1)} %get-tuple-element.79), channel_id=1, source_target_pairs={{0,504},{8,16},{16,8},{24,32},{32,24},{40,48},{48,40},{56,64},{64,... | collective-permute-start | bytes 786440 | tf_op jit(solution)/shard_map/ppermute | solution.py:360
  81.0 20.3 %collective-permute-start.11 = (bf16[8,128,128]{2,1,0:T(8,128)(2,1)S(1)}, bf16[8,128,128]{2,1,0:T(8,128)(2,1)S(1)}, u32[]{:S(2)}, u32[]{:S(2)}) collective-permute-start(bf16[8,128,128]{2,1,0:T(8,128)(2,1)S(1)} %get-tuple-element.81), channel_id=1, source_target_pairs={{0,504},{8,16},{16,8},{24,32},{32,24},{40,48},{48,40},{56,64},{64,... | collective-permute-start | bytes 786440 | tf_op jit(solution)/shard_map/ppermute | solution.py:360
  91.9 22.5 %collective-permute-start.15 = (bf16[8,128,128]{2,1,0:T(8,128)(2,1)S(1)}, bf16[8,128,128]{2,1,0:T(8,128)(2,1)S(1)}, u32[]{:S(2)}, u32[]{:S(2)}) collective-permute-start(bf16[8,128,128]{2,1,0:T(8,128)(2,1)S(1)} %add_convert_fusion.4), channel_id=1, source_target_pairs={{0,504},{8,16},{16,8},{24,32},{32,24},{40,48},{48,40},{56,64},{64,... | collective-permute-start | bytes 786440 | tf_op jit(solution)/shard_map/ppermute | solution.py:360
  97.4 27.0 %collective-permute-start.13 = (bf16[8,128,128]{2,1,0:T(8,128)(2,1)}, bf16[8,128,128]{2,1,0:T(8,128)(2,1)}, u32[]{:S(2)}, u32[]{:S(2)}) collective-permute-start(bf16[8,128,128]{2,1,0:T(8,128)(2,1)} %add_convert_fusion.5), channel_id=1, source_target_pairs={{0,504},{8,16},{16,8},{24,32},{32,24},{40,48},{48,40},{56,64},{64,... | collective-permute-start | bytes 786440 | tf_op jit(solution)/shard_map/ppermute | solution.py:360
  101.4 13.0 %collective-permute-start.14 = (bf16[8,128,128]{2,1,0:T(8,128)(2,1)S(1)}, bf16[8,128,128]{2,1,0:T(8,128)(2,1)S(1)}, u32[]{:S(2)}, u32[]{:S(2)}) collective-permute-start(bf16[8,128,128]{2,1,0:T(8,128)(2,1)S(1)} %add_convert_fusion.2), channel_id=1, source_target_pairs={{0,8},{8,0},{16,24},{24,16},{32,40},{40,32},{48,56},{56,48},{64,72... | collective-permute-start | bytes 786440 | tf_op jit(solution)/shard_map/ppermute | solution.py:360
  104.1 20.3 %collective-permute-start.12 = (bf16[8,128,128]{2,1,0:T(8,128)(2,1)}, bf16[8,128,128]{2,1,0:T(8,128)(2,1)}, u32[]{:S(2)}, u32[]{:S(2)}) collective-permute-start(bf16[8,128,128]{2,1,0:T(8,128)(2,1)} %add_convert_fusion.3), channel_id=1, source_target_pairs={{0,8},{8,0},{16,24},{24,16},{32,40},{40,32},{48,56},{56,48},{64,72... | collective-permute-start | bytes 786440 | tf_op jit(solution)/shard_map/ppermute | solution.py:360
  113.6 0.8 copy-start.6
  114.4 10.0 %copy-start.7 = (f32[8,128,128]{2,1,0:T(8,128)S(1)}, f32[8,128,128]{2,1,0:T(8,128)}, u32[]{:S(2)}) copy-start(f32[8,128,128]{2,1,0:T(8,128)} %copy-done.6) | copy-start | bytes 1572868
  115.2 15.7 %all-to-all-start.2 = ((bf16[8,128,128]{2,1,0:T(8,128)(2,1)}), bf16[8,128,128]{2,1,0:T(8,128)(2,1)S(1)}, u32[]{:S(2)}, u32[]{:S(2)}) async-start(bf16[8,128,128]{2,1,0:T(8,128)(2,1)} %add_convert_fusion), calls=%async_computation.2 | async-start | bytes 524288 | tf_op jit(solution)/shard_map/all_to_all | solution.py:405

commit v6 on v3

--- a/solution.py
+++ b/solution.py
@@ -363,22 +363,22 @@
     low_one, prepared = lax.optimization_barrier((low_one, prepared))
     low_two = shifted(low_one, 1)
     up_two = shifted(up_one, -1)
-    low_near, _ = lax.optimization_barrier((low_one, up_one))
 
     def grads(code, pair, chain, kind):
         return near_grads(code, pair, plan, prepared, comp_key, comp_value, chain, query.shape, kind)
 
-    low_term, chain = grads(1, low_near, None, jnp.float32)
-    low_two_term, chain = grads(0, low_two, chain, jnp.bfloat16)
+    low_two_term, chain = grads(0, low_two, None, jnp.bfloat16)
     up_two_term, chain = grads(4, up_two, chain, jnp.bfloat16)
+    low_two_term, up_two_term = lax.optimization_barrier((low_two_term, up_two_term))
     low_back = shifted(low_two_term, -1).astype(jnp.float32)
     up_back = shifted(up_two_term, 1).astype(jnp.float32)
+    low_term, chain = grads(1, low_one, chain, jnp.float32)
     up_term, chain = grads(3, up_one, chain, jnp.float32)
     low_sum = (low_term + low_back).astype(jnp.bfloat16)
     up_sum = (up_term + up_back).astype(jnp.bfloat16)
-    up_sum, chain = lax.optimization_barrier((up_sum, chain))
     low_back = shifted(low_sum, -1).astype(jnp.float32)
     up_back = shifted(up_sum, 1).astype(jnp.float32)
+    _, _, chain = lax.optimization_barrier((low_sum, up_sum, chain))
     own_term, chain = grads(2, own, chain, jnp.float32)
     gathered = (own_term + low_back + up_back).astype(jnp.bfloat16)
     back = lax.all_to_all(gathered, "mp", split_axis=0, concat_axis=0, tiled=True)

time: 121 us -> 125 us (1.033)
  the two profiles are of different devices: /device:TPU:6 before, /device:TPU:1 now
where the time goes in v6:
time: 125 us
  blocking collectives  39.9 us (32%)
  starting transfers between devices  39.1 us (31%)
  Pallas kernels  26.9 us (22%)
  waiting for transfers between devices  13.1 us (10%)
  local copies, waits for them, and re-layouts  4.33 us (3%)
    ppermute x8, starting transfers between devices, shifted(): return lax.ppermute(value, ('dp', 'mp'), pairs)  39.1 us
    pallas_call x5, Pallas kernels, near_grads(): pl.pallas_call(functools.partial(near_kernel, code, chain is not None), o...  23.9 us
    all_to_all x1, blocking collectives, per_device(): lax.all_to_all(gathered, 'mp', split_axis=0, concat_axis=0, tiled=True)  21.2 us
    all_to_all x1, blocking collectives, per_device(): own = lax.all_to_all(pair, 'mp', split_axis=0, concat_axis=0, tiled=True)  18.6 us
    ppermute x8, waiting for transfers between devices, shifted(): return lax.ppermute(value, ('dp', 'mp'), pairs)  13.1 us
    unnamed x26, local copies, waits for them, and re-layouts  4.33 us
  transfers between devices with their start and end apart: 8, of which 5 were waited for; matrix products, arithmetic and copies ran while one was open for 0% of the time, Pallas kernels for 16%

profile of v6, /device:TPU:1, one launch (start us, length us, event | category | flops | bytes accessed | tf_op | source)
XLA Modules:
  0.0 125.0 jit_solution(2734117965646501126)
XLA Ops:
  0.6 0.0 copy-start.7
  0.6 0.0 copy-start.6
  0.7 0.0 copy-start.8
  0.7 1.1 copy-done.8
  1.8 0.0 copy-start.9
  1.8 0.9 copy-done.9
  2.7 0.0 copy-start.10
  2.7 0.1 shard_map.128
  2.8 18.6 %all_to_all.10.pair = bf16[8,2,128,128]{3,2,1,0:T(8,128)(2,1)S(1)} all-to-all(bf16[8,2,128,128]{3,2,1,0:T(8,128)(2,1)S(1)} %shard_map.128), channel_id=1, replica_groups=mesh['dp'=64,'mp'=8] {'mp'}, dimensions={0} | all-to-all | bytes 1048576 | tf_op jit(solution)/shard_map/all_to_all | solution.py:358
  21.4 0.0 copy-start.4
  21.4 0.0 copy-start.11
  21.4 0.0 copy-start.12
  21.4 0.0 copy-start.2
  21.5 0.0 copy-start.3
  21.5 9.9 %collective-permute-start = (bf16[8,2,128,128]{3,2,1,0:T(8,128)(2,1)S(1)}, bf16[8,2,128,128]{3,2,1,0:T(8,128)(2,1)}, u32[]{:S(2)}, u32[]{:S(2)}) collective-permute-start(bf16[8,2,128,128]{3,2,1,0:T(8,128)(2,1)S(1)} %all_to_all.10.pair), channel_id=1, source_target_pairs={{0,8},{1,505},{2,10},{3,507},{4,12},{5,509},{6,14},{7,511},{8,16},... | collective-permute-start | bytes 1572872 | tf_op jit(solution)/shard_map/ppermute | solution.py:343
  31.4 1.9 %collective-permute-start.1 = (bf16[8,2,128,128]{3,2,1,0:T(8,128)(2,1)S(1)}, bf16[8,2,128,128]{3,2,1,0:T(8,128)(2,1)}, u32[]{:S(2)}, u32[]{:S(2)}) collective-permute-start(bf16[8,2,128,128]{3,2,1,0:T(8,128)(2,1)S(1)} %all_to_all.10.pair), channel_id=1, source_target_pairs={{0,504},{1,9},{2,506},{3,11},{4,508},{5,13},{6,510},{7,15},{8,0},{... | collective-permute-start | bytes 1572872 | tf_op jit(solution)/shard_map/ppermute | solution.py:343
  33.3 0.0 copy-done.7
  33.3 0.0 copy-done.6
  33.4 0.0 copy-done.10
  33.4 2.0 %shard_map.129 = (bf16[33,128,128]{2,1,0:T(8,128)(2,1)S(1)}, bf16[33,128,128]{2,1,0:T(8,128)(2,1)S(1)}, bf16[33,128,128]{2,1,0:T(8,128)(2,1)S(1)}, bf16[33,128,128]{2,1,0:T(8,128)(2,1)S(1)}) custom-call(s32[16]{0:T(128)S(1)} %copy-done.10, bf16[16,32,1024]{2,1,0:T(8,128)(2,1)S(1)} %copy-done.6, bf16[16,32,1024]{2,1,0:T(8,128)(2,1)S(1)} %copy-done.7), custom_call_target="tpu_custom_call" | custom-call | bytes 6291456 | tf_op jit(solution)/shard_map/pallas_call | solution.py:64
  35.4 0.0 copy-done.4
  35.4 0.0 copy-start
  35.4 1.0 copy-done
  36.5 3.2 %collective-permute-done.pair = bf16[8,2,128,128]{3,2,1,0:T(8,128)(2,1)} collective-permute-done((bf16[8,2,128,128]{3,2,1,0:T(8,128)(2,1)S(1)}, bf16[8,2,128,128]{3,2,1,0:T(8,128)(2,1)}, u32[]{:S(2)}, u32[]{:S(2)}) %collective-permute-start) | collective-permute-done | bytes 524320 | tf_op jit(solution)/shard_map/ppermute | solution.py:343
  39.6 7.5 %collective-permute-start.3 = (bf16[8,2,128,128]{3,2,1,0:T(8,128)(2,1)}, bf16[8,2,128,128]{3,2,1,0:T(8,128)(2,1)}, u32[]{:S(2)}, u32[]{:S(2)}) collective-permute-start(bf16[8,2,128,128]{3,2,1,0:T(8,128)(2,1)} %collective-permute-done.pair), channel_id=1, source_target_pairs={{0,8},{1,505},{2,10},{3,507},{4,12},{5,509},{6,14},{7,511},{8,16},... | collective-permute-start | bytes 1572872 | tf_op jit(solution)/shard_map/ppermute | solution.py:343
  47.2 0.0 collective-permute-done.1.pair
  47.2 1.9 %collective-permute-start.2 = (bf16[8,2,128,128]{3,2,1,0:T(8,128)(2,1)}, bf16[8,2,128,128]{3,2,1,0:T(8,128)(2,1)}, u32[]{:S(2)}, u32[]{:S(2)}) collective-permute-start(bf16[8,2,128,128]{3,2,1,0:T(8,128)(2,1)} %collective-permute-done.1.pair), channel_id=1, source_target_pairs={{0,504},{1,9},{2,506},{3,11},{4,508},{5,13},{6,510},{7,15},{8,0},{... | collective-permute-start | bytes 1572872 | tf_op jit(solution)/shard_map/ppermute | solution.py:343
  49.1 0.0 copy-done.11
  49.1 0.0 copy-done.12
  49.1 0.2 select_reduce_fusion
  49.3 5.4 %collective-permute-done.3.pair = bf16[8,2,128,128]{3,2,1,0:T(8,128)(2,1)} collective-permute-done((bf16[8,2,128,128]{3,2,1,0:T(8,128)(2,1)}, bf16[8,2,128,128]{3,2,1,0:T(8,128)(2,1)}, u32[]{:S(2)}, u32[]{:S(2)}) %collective-permute-start.3) | collective-permute-done | bytes 524320 | tf_op jit(solution)/shard_map/ppermute | solution.py:343
  54.8 0.0 copy-done.2
  54.8 0.0 copy-done.3
  54.8 0.0 copy-start.1
  54.8 1.2 copy-done.1
  56.0 2.8 %shard_map.130 = (bf16[8,2,128,128]{3,2,1,0:T(8,128)(2,1)S(1)}, bf16[16,32,1024]{2,1,0:T(8,128)(2,1)S(1)}, bf16[16,32,128]{2,1,0:T(8,128)(2,1)S(1)}, bf16[16,32,128]{2,1,0:T(8,128)(2,1)S(1)}) custom-call(s32[16]{0:T(128)S(1)} %multiply_add_fusion.plan, bf16[33,128,128]{2,1,0:T(8,128)(2,1)S(1)} %get-tuple-element.45.query_rows, ...), custom_call_target="tpu_custom_call" | custom-call | flops 1711276032 | bytes 1310720 | tf_op jit(solution)/shard_map/pallas_call | solution.py:268
  58.8 1.9 %collective-permute-done.2.pair = bf16[8,2,128,128]{3,2,1,0:T(8,128)(2,1)} collective-permute-done((bf16[8,2,128,128]{3,2,1,0:T(8,128)(2,1)}, bf16[8,2,128,128]{3,2,1,0:T(8,128)(2,1)}, u32[]{:S(2)}, u32[]{:S(2)}) %collective-permute-start.2) | collective-permute-done | bytes 524320 | tf_op jit(solution)/shard_map/ppermute | solution.py:343
  60.7 6.2 %shard_map.131 = (bf16[8,2,128,128]{3,2,1,0:T(8,128)(2,1)S(1)}, bf16[16,32,1024]{2,1,0:T(8,128)(2,1)S(1)}, bf16[16,32,128]{2,1,0:T(8,128)(2,1)S(1)}, bf16[16,32,128]{2,1,0:T(8,128)(2,1)S(1)}) custom-call(s32[16]{0:T(128)S(1)} %multiply_add_fusion.plan, bf16[33,128,128]{2,1,0:T(8,128)(2,1)S(1)} %get-tuple-element.45.query_rows, ...), custom_call_target="tpu_custom_call" | custom-call | flops 1711276032 | bytes 1310720 | tf_op jit(solution)/shard_map/pallas_call | solution.py:268
  66.9 1.9 %collective-permute-start.4 = (bf16[8,2,128,128]{3,2,1,0:T(8,128)(2,1)S(1)}, bf16[8,2,128,128]{3,2,1,0:T(8,128)(2,1)S(1)}, u32[]{:S(2)}, u32[]{:S(2)}) collective-permute-start(bf16[8,2,128,128]{3,2,1,0:T(8,128)(2,1)S(1)} %get-tuple-element.59), channel_id=1, source_target_pairs={{0,504},{1,9},{2,506},{3,11},{4,508},{5,13},{6,510},{7,15},{8,0},{... | collective-permute-start | bytes 1572872 | tf_op jit(solution)/shard_map/ppermute | solution.py:343
  68.8 6.7 %collective-permute-start.5 = (bf16[8,2,128,128]{3,2,1,0:T(8,128)(2,1)S(1)}, bf16[8,2,128,128]{3,2,1,0:T(8,128)(2,1)S(1)}, u32[]{:S(2)}, u32[]{:S(2)}) collective-permute-start(bf16[8,2,128,128]{3,2,1,0:T(8,128)(2,1)S(1)} %get-tuple-element.64), channel_id=1, source_target_pairs={{0,8},{1,505},{2,10},{3,507},{4,12},{5,509},{6,14},{7,511},{8,16},... | collective-permute-start | bytes 1572872 | tf_op jit(solution)/shard_map/ppermute | solution.py:343
  75.5 4.0 %shard_map.132 = (f32[8,2,128,128]{3,2,1,0:T(8,128)S(1)}, bf16[16,32,1024]{2,1,0:T(8,128)(2,1)S(1)}, bf16[16,32,128]{2,1,0:T(8,128)(2,1)S(1)}, bf16[16,32,128]{2,1,0:T(8,128)(2,1)S(1)}) custom-call(s32[16]{0:T(128)S(1)} %multiply_add_fusion.plan, bf16[33,128,128]{2,1,0:T(8,128)(2,1)S(1)} %get-tuple-element.45.query_rows, ...), custom_call_target="tpu_custom_call" | custom-call | flops 1711276032 | bytes 1310720 | tf_op jit(solution)/shard_map/pallas_call | solution.py:268
  79.6 2.9 %shard_map.133 = (f32[8,2,128,128]{3,2,1,0:T(8,128)S(1)}, bf16[16,32,1024]{2,1,0:T(8,128)(2,1)S(1)}, bf16[16,32,128]{2,1,0:T(8,128)(2,1)S(1)}, bf16[16,32,128]{2,1,0:T(8,128)(2,1)S(1)}) custom-call(s32[16]{0:T(128)S(1)} %multiply_add_fusion.plan, bf16[33,128,128]{2,1,0:T(8,128)(2,1)S(1)} %get-tuple-element.45.query_rows, ...), custom_call_target="tpu_custom_call" | custom-call | flops 1711276032 | bytes 1310720 | tf_op jit(solution)/shard_map/pallas_call | solution.py:268
  82.5 0.0 collective-permute-done.4
  82.5 0.2 add_convert_fusion.2
  82.6 0.0 copy-start.5
  82.6 2.1 %collective-permute-start.6 = (bf16[8,2,128,128]{3,2,1,0:T(8,128)(2,1)S(1)}, bf16[8,2,128,128]{3,2,1,0:T(8,128)(2,1)S(1)}, u32[]{:S(2)}, u32[]{:S(2)}) collective-permute-start(bf16[8,2,128,128]{3,2,1,0:T(8,128)(2,1)S(1)} %add_convert_fusion.2), channel_id=1, source_target_pairs={{0,504},{1,9},{2,506},{3,11},{4,508},{5,13},{6,510},{7,15},{8,0},{... | collective-permute-start | bytes 1572872 | tf_op jit(solution)/shard_map/ppermute | solution.py:343
  84.7 2.3 %collective-permute-done.5 = bf16[8,2,128,128]{3,2,1,0:T(8,128)(2,1)S(1)} collective-permute-done((bf16[8,2,128,128]{3,2,1,0:T(8,128)(2,1)S(1)}, bf16[8,2,128,128]{3,2,1,0:T(8,128)(2,1)S(1)}, u32[]{:S(2)}, u32[]{:S(2)}) %collective-permute-start.5) | collective-permute-done | bytes 524320 | tf_op jit(solution)/shard_map/ppermute | solution.py:343
  87.0 0.1 add_convert_fusion.1
  87.1 7.2 %collective-permute-start.7 = (bf16[8,2,128,128]{3,2,1,0:T(8,128)(2,1)S(1)}, bf16[8,2,128,128]{3,2,1,0:T(8,128)(2,1)S(1)}, u32[]{:S(2)}, u32[]{:S(2)}) collective-permute-start(bf16[8,2,128,128]{3,2,1,0:T(8,128)(2,1)S(1)} %add_convert_fusion.1), channel_id=1, source_target_pairs={{0,8},{1,505},{2,10},{3,507},{4,12},{5,509},{6,14},{7,511},{8,16},... | collective-permute-start | bytes 1572872 | tf_op jit(solution)/shard_map/ppermute | solution.py:343
  94.3 0.0 copy-done.5
  94.3 8.0 %shard_map.134 = (f32[8,2,128,128]{3,2,1,0:T(8,128)S(1)}, bf16[16,32,1024]{2,1,0:T(8,128)(2,1)}, bf16[16,32,128]{2,1,0:T(8,128)(2,1)}, bf16[16,32,128]{2,1,0:T(8,128)(2,1)}) custom-call(s32[16]{0:T(128)S(1)} %multiply_add_fusion.plan, bf16[33,128,128]{2,1,0:T(8,128)(2,1)S(1)} %get-tuple-element.45.query_rows, ...), custom_call_target="tpu_custom_call" | custom-call | flops 1711276032 | bytes 1310720 | tf_op jit(solution)/shard_map/pallas_call | solution.py:268
  102.3 0.0 collective-permute-done.6
  102.3 0.3 collective-permute-done.7
  102.6 0.2 add_convert_fusion
  102.8 21.2 %all_to_all.11.pair = bf16[8,2,128,128]{3,2,1,0:T(8,128)(2,1)S(1)} all-to-all(bf16[8,2,128,128]{3,2,1,0:T(8,128)(2,1)S(1)} %add_convert_fusion), channel_id=1, replica_groups=mesh['dp'=64,'mp'=8] {'mp'}, dimensions={0} | all-to-all | bytes 1048576 | tf_op jit(solution)/shard_map/all_to_all | solution.py:384
  124.0 0.9 shard_map.135
  (1 shorter events, 0.0 us)
Async XLA Ops:
  0.6 32.7 %copy-start.7 = (bf16[16,32,1024]{2,1,0:T(8,128)(2,1)S(1)}, bf16[16,32,1024]{2,1,0:T(8,128)(2,1)}, u32[]{:S(2)}) copy-start(bf16[16,32,1024]{2,1,0:T(8,128)(2,1)} %grad_out.1) | copy-start | bytes 3145732
  0.6 32.7 %copy-start.6 = (bf16[16,32,1024]{2,1,0:T(8,128)(2,1)S(1)}, bf16[16,32,1024]{2,1,0:T(8,128)(2,1)}, u32[]{:S(2)}) copy-start(bf16[16,32,1024]{2,1,0:T(8,128)(2,1)} %query.1) | copy-start | bytes 3145732
  0.7 1.1 copy-start.8
  1.8 0.9 copy-start.9
  2.7 30.7 %copy-start.10 = (s32[16]{0:T(128)S(1)}, s32[16]{0:T(128)}, u32[]{:S(2)}) copy-start(s32[16]{0:T(128)} %lengths.1) | copy-start | bytes 196
  21.4 14.0 %copy-start.4 = (bf16[8,2,128,128]{3,2,1,0:T(8,128)(2,1)}, bf16[8,2,128,128]{3,2,1,0:T(8,128)(2,1)S(1)}, u32[]{:S(2)}) copy-start(bf16[8,2,128,128]{3,2,1,0:T(8,128)(2,1)S(1)} %all_to_all.10.pair) | copy-start | bytes 1572868
  21.4 27.7 %copy-start.11 = (s32[64]{0:T(128)S(1)}, s32[64]{0:T(128)}, u32[]{:S(2)}) copy-start(s32[64]{0:T(128)} %param.15) | copy-start | bytes 772
  21.4 27.7 %copy-start.12 = (s32[16]{0:T(128)S(1)}, s32[16]{0:T(128)}, u32[]{:S(2)}) copy-start(s32[16]{0:T(128)} %param.16) | copy-start | bytes 196
  21.4 33.3 %copy-start.2 = (bf16[16,32,128]{2,1,0:T(8,128)(2,1)S(1)}, bf16[16,32,128]{2,1,0:T(8,128)(2,1)}, u32[]{:S(2)}) copy-start(bf16[16,32,128]{2,1,0:T(8,128)(2,1)} %comp_key.9) | copy-start | bytes 393220
  21.5 33.3 %copy-start.3 = (bf16[16,32,128]{2,1,0:T(8,128)(2,1)S(1)}, bf16[16,32,128]{2,1,0:T(8,128)(2,1)}, u32[]{:S(2)}) copy-start(bf16[16,32,128]{2,1,0:T(8,128)(2,1)} %comp_value.9) | copy-start | bytes 393220
  21.5 18.2 %collective-permute-start = (bf16[8,2,128,128]{3,2,1,0:T(8,128)(2,1)S(1)}, bf16[8,2,128,128]{3,2,1,0:T(8,128)(2,1)}, u32[]{:S(2)}, u32[]{:S(2)}) collective-permute-start(bf16[8,2,128,128]{3,2,1,0:T(8,128)(2,1)S(1)} %all_to_all.10.pair), channel_id=1, source_target_pairs={{0,8},{1,505},{2,10},{3,507},{4,12},{5,509},{6,14},{7,511},{8,16},... | collective-permute-start | bytes 1572872 | tf_op jit(solution)/shard_map/ppermute | solution.py:343
  31.4 15.8 %collective-permute-start.1 = (bf16[8,2,128,128]{3,2,1,0:T(8,128)(2,1)S(1)}, bf16[8,2,128,128]{3,2,1,0:T(8,128)(2,1)}, u32[]{:S(2)}, u32[]{:S(2)}) collective-permute-start(bf16[8,2,128,128]{3,2,1,0:T(8,128)(2,1)S(1)} %all_to_all.10.pair), channel_id=1, source_target_pairs={{0,504},{1,9},{2,506},{3,11},{4,508},{5,13},{6,510},{7,15},{8,0},{... | collective-permute-start | bytes 1572872 | tf_op jit(solution)/shard_map/ppermute | solution.py:343
  35.4 1.0 copy-start
  39.6 15.1 %collective-permute-start.3 = (bf16[8,2,128,128]{3,2,1,0:T(8,128)(2,1)}, bf16[8,2,128,128]{3,2,1,0:T(8,128)(2,1)}, u32[]{:S(2)}, u32[]{:S(2)}) collective-permute-start(bf16[8,2,128,128]{3,2,1,0:T(8,128)(2,1)} %collective-permute-done.pair), channel_id=1, source_target_pairs={{0,8},{1,505},{2,10},{3,507},{4,12},{5,509},{6,14},{7,511},{8,16},... | collective-permute-start | bytes 1572872 | tf_op jit(solution)/shard_map/ppermute | solution.py:343
  47.2 13.6 %collective-permute-start.2 = (bf16[8,2,128,128]{3,2,1,0:T(8,128)(2,1)}, bf16[8,2,128,128]{3,2,1,0:T(8,128)(2,1)}, u32[]{:S(2)}, u32[]{:S(2)}) collective-permute-start(bf16[8,2,128,128]{3,2,1,0:T(8,128)(2,1)} %collective-permute-done.1.pair), channel_id=1, source_target_pairs={{0,504},{1,9},{2,506},{3,11},{4,508},{5,13},{6,510},{7,15},{8,0},{... | collective-permute-start | bytes 1572872 | tf_op jit(solution)/shard_map/ppermute | solution.py:343
  54.8 1.2 copy-start.1
  66.9 15.6 %collective-permute-start.4 = (bf16[8,2,128,128]{3,2,1,0:T(8,128)(2,1)S(1)}, bf16[8,2,128,128]{3,2,1,0:T(8,128)(2,1)S(1)}, u32[]{:S(2)}, u32[]{:S(2)}) collective-permute-start(bf16[8,2,128,128]{3,2,1,0:T(8,128)(2,1)S(1)} %get-tuple-element.59), channel_id=1, source_target_pairs={{0,504},{1,9},{2,506},{3,11},{4,508},{5,13},{6,510},{7,15},{8,0},{... | collective-permute-start | bytes 1572872 | tf_op jit(solution)/shard_map/ppermute | solution.py:343
  68.8 18.2 %collective-permute-start.5 = (bf16[8,2,128,128]{3,2,1,0:T(8,128)(2,1)S(1)}, bf16[8,2,128,128]{3,2,1,0:T(8,128)(2,1)S(1)}, u32[]{:S(2)}, u32[]{:S(2)}) collective-permute-start(bf16[8,2,128,128]{3,2,1,0:T(8,128)(2,1)S(1)} %get-tuple-element.64), channel_id=1, source_target_pairs={{0,8},{1,505},{2,10},{3,507},{4,12},{5,509},{6,14},{7,511},{8,16},... | collective-permute-start | bytes 1572872 | tf_op jit(solution)/shard_map/ppermute | solution.py:343
  82.6 11.7 %copy-start.5 = (bf16[8,2,128,128]{3,2,1,0:T(8,128)(2,1)S(1)}, bf16[8,2,128,128]{3,2,1,0:T(8,128)(2,1)}, u32[]{:S(2)}) copy-start(bf16[8,2,128,128]{3,2,1,0:T(8,128)(2,1)} %copy-done.4) | copy-start | bytes 1572868
  82.6 19.7 %collective-permute-start.6 = (bf16[8,2,128,128]{3,2,1,0:T(8,128)(2,1)S(1)}, bf16[8,2,128,128]{3,2,1,0:T(8,128)(2,1)S(1)}, u32[]{:S(2)}, u32[]{:S(2)}) collective-permute-start(bf16[8,2,128,128]{3,2,1,0:T(8,128)(2,1)S(1)} %add_convert_fusion.2), channel_id=1, source_target_pairs={{0,504},{1,9},{2,506},{3,11},{4,508},{5,13},{6,510},{7,15},{8,0},{... | collective-permute-start | bytes 1572872 | tf_op jit(solution)/shard_map/ppermute | solution.py:343
  87.1 15.5 %collective-permute-start.7 = (bf16[8,2,128,128]{3,2,1,0:T(8,128)(2,1)S(1)}, bf16[8,2,128,128]{3,2,1,0:T(8,128)(2,1)S(1)}, u32[]{:S(2)}, u32[]{:S(2)}) collective-permute-start(bf16[8,2,128,128]{3,2,1,0:T(8,128)(2,1)S(1)} %add_convert_fusion.1), channel_id=1, source_target_pairs={{0,8},{1,505},{2,10},{3,507},{4,12},{5,509},{6,14},{7,511},{8,16},... | collective-permute-start | bytes 1572872 | tf_op jit(solution)/shard_map/ppermute | solution.py:343
